TPU v7x, 128 devices: a whole 4x4x4 slice. The times are simulated.
128 devices in a mesh: expert: 32 (over z, x, core), group: 4 (over y).
Axes of the slice: x: 4, y: 4, z: 4, core: 2. Of those that a mesh axis runs over, the one named last changes fastest.
Arguments:
- tokens: bfloat16 [4096, 7168], P('expert', 'group'), may hold values from -6 to 6
- routes: int32 [4096, 8], P('expert'), may hold values from 0 to 31, all different within a row; in each aligned block of 128 rows (0 to 127, 128 to 255, ...) at most 36 rows name the same one
- route_weight: float32 [4096, 8], P('expert'), may hold values from 0.1 to 0.6
- gate_weight: bfloat16 [32, 7168, 2048], P('expert', None, 'group'), may hold values from -0.0625 to 0.0625
- up_weight: bfloat16 [32, 7168, 2048], P('expert', None, 'group'), may hold values from -0.0625 to 0.0625
- down_weight: bfloat16 [32, 2048, 7168], P('expert', 'group'), may hold values from -0.125 to 0.125
- delta_values: bfloat16 [8192, 16384], P(('expert', 'group')), may hold values from -6 to 6
- delta_owner: int32 [128, 64], P(('expert', 'group')), may hold values from 0 to 127, as said below
- delta_index: int32 [128, 64], P(('expert', 'group')), may hold values from 0 to 671
- delta_scale: int32 [128, 64], P(('expert', 'group')), may hold values from -1 to 1
- delta_count: int32 [128], P(('expert', 'group')), may hold values from 40 to 64, as said below
Outputs:
- mixed: bfloat16 [4096, 7168], P('expert', 'group')
Inputs may be any that keep to these rules, and one draw needn't show every extreme that they name: `routes`: in the 128 rows of one index of expert no expert is named more than 36 times. `delta_owner`: the entries of one device's list name different owners. One owner is named among the first delta_count entries of every device's list. `delta_count`: some device has all 64 entries live.
All inputs are finite; a program needn't handle non-finite values.
Results may differ from a plain program's by a relative error of at most 0.015.
Values may be sent and summed in bfloat16 or wider, within the bound.
No kernel may reach another device: no remote copies, remote signals or barrier semaphores. Data moves between devices by JAX's collectives and lax.ppermute only.
A program may use at most 320 MiB of HBM per device.

v0:
```python
import math

import jax
import jax.numpy as jnp
from jax import lax
from jax.sharding import PartitionSpec as P


def refresh_share(weight, which, slot_part, blocks, factor, block_side, matrix_id, blocks_mat):
    row_count, col_count = weight.shape
    row_blocks = row_count // block_side
    col_blocks = col_count // block_side
    inside = slot_part - matrix_id * blocks_mat
    valid = which == matrix_id
    block_row = jnp.where(valid, inside // col_blocks, row_blocks).astype(jnp.int32)
    block_col = jnp.where(valid, inside % col_blocks, 0).astype(jnp.int32)
    field = jnp.zeros((row_blocks, block_side, col_blocks, block_side), jnp.float32)
    field = field.at[block_row, :, block_col, :].add(blocks, mode="drop")
    field = field.reshape(row_count, col_count)
    return (weight.astype(jnp.float32) + factor * field).astype(jnp.bfloat16)


def shards(
    tokens,
    routes,
    route_weight,
    gate_weight,
    up_weight,
    down_weight,
    delta_values,
    delta_owner,
    delta_index,
    delta_scale,
    delta_count,
):
    n_expert = lax.axis_size("expert")
    n_group = lax.axis_size("group")
    sources = n_expert * n_group
    model_width = gate_weight.shape[1]
    hidden_loc = gate_weight.shape[2]
    quarter = tokens.shape[1]
    block_side = math.isqrt(delta_values.shape[1])
    blocks_mat = model_width // block_side * (hidden_loc // block_side)
    per_owner = 3 * blocks_mat
    listed = delta_owner.shape[1]
    in_factor = model_width ** (-0.5)
    down_factor = (hidden_loc * n_group) ** (-0.5)
    is_live = jnp.arange(listed, dtype=jnp.int32) < delta_count[0]
    owner_slot = jnp.where(is_live, delta_owner[0], sources)
    outgoing = (
        jnp.zeros((sources, block_side * block_side), jnp.bfloat16)
        .at[owner_slot]
        .set(delta_values, mode="drop")
    )
    slot_index = (
        jnp.full((sources,), per_owner, jnp.int32).at[owner_slot].set(delta_index[0], mode="drop")
    )
    slot_scale = jnp.zeros((sources,), jnp.int32).at[owner_slot].set(delta_scale[0], mode="drop")
    slot_meta = jnp.stack([slot_index, slot_scale], axis=1)
    incoming, meta_in = (
        lax.all_to_all(outgoing, ("expert", "group"), split_axis=0, concat_axis=0, tiled=True),
        lax.all_to_all(slot_meta, ("expert", "group"), split_axis=0, concat_axis=0, tiled=True),
    )
    scaled = incoming.astype(jnp.float32) * jnp.exp2(meta_in[:, 1].astype(jnp.float32))[:, None]
    scaled = scaled.reshape(sources, block_side, block_side)
    slot_part = meta_in[:, 0]
    which = slot_part // blocks_mat
    gate_new = refresh_share(
        gate_weight[0], which, slot_part, scaled, in_factor, block_side, 0, blocks_mat
    )
    up_new = refresh_share(
        up_weight[0], which, slot_part, scaled, in_factor, block_side, 1, blocks_mat
    )
    down_new = refresh_share(
        down_weight[0], which, slot_part, scaled, down_factor, block_side, 2, blocks_mat
    )
    tok_rows = tokens.shape[0]
    top_count = routes.shape[1]
    capacity = tok_rows * top_count * 9 // (8 * n_expert)
    chosen = routes.reshape(-1)
    one_hot = (chosen[:, None] == jnp.arange(n_expert, dtype=jnp.int32)[None, :]).astype(jnp.int32)
    running = jnp.cumsum(one_hot, axis=0)
    slot_number = jnp.take_along_axis(running, chosen[:, None], axis=1)[:, 0] - 1
    position = slot_number * n_expert + chosen
    outgoing_rows = (
        jnp.zeros((capacity * n_expert, quarter), jnp.bfloat16)
        .at[position]
        .set(jnp.repeat(tokens, top_count, axis=0))
    )
    outgoing_rows = outgoing_rows.reshape(capacity, n_expert, quarter)
    spread = jnp.broadcast_to(
        outgoing_rows[:, :, None, :], (capacity, n_expert, n_group, quarter)
    ).reshape(capacity, sources, quarter)
    arrived = lax.all_to_all(spread, ("expert", "group"), split_axis=1, concat_axis=2, tiled=True)
    rows_in = arrived.reshape(capacity * n_expert, model_width)
    gate_act = jnp.dot(rows_in, gate_new, preferred_element_type=jnp.float32)
    up_act = jnp.dot(rows_in, up_new, preferred_element_type=jnp.float32)
    hidden = (jax.nn.silu(gate_act) * up_act).astype(jnp.bfloat16)
    partial_value = jnp.dot(hidden, down_new, preferred_element_type=jnp.float32).astype(
        jnp.bfloat16
    )
    reduced = lax.psum_scatter(
        partial_value.reshape(capacity, n_expert, model_width),
        "group",
        scatter_dimension=2,
        tiled=True,
    ).astype(jnp.float32)
    expert_out = reduced.astype(jnp.bfloat16)
    returned = lax.all_to_all(expert_out, "expert", split_axis=1, concat_axis=1, tiled=True)
    picked = returned.reshape(capacity * n_expert, quarter)[position].reshape(
        tok_rows, top_count, quarter
    )
    result = jnp.sum(route_weight[:, :, None] * picked.astype(jnp.float32), axis=1)
    return result.astype(jnp.bfloat16)


def solution(mesh):
    return jax.shard_map(
        shards,
        mesh=mesh,
        in_specs=(
            P("expert", "group"),
            P("expert", None),
            P("expert", None),
            P("expert", None, "group"),
            P("expert", None, "group"),
            P("expert", "group", None),
            P(("expert", "group"), None),
            P(("expert", "group"), None),
            P(("expert", "group"), None),
            P(("expert", "group"), None),
            P(("expert", "group")),
        ),
        out_specs=P("expert", "group"),
        check_vma=False,
    )
```

profile of v0, /device:TPU:0, one launch (start us, length us, event | category | flops | bytes accessed | tf_op | source)
XLA Modules:
  0.0 784.4 jit_solution(2803180458791813185)
XLA Ops:
  10.5 11.1 %all-to-all-start.1 = ((s32[128,1,2]{2,1,0:T(1,128)}), s32[128,1,2]{2,1,0:T(1,128)S(1)}, u32[]{:S(2)}, u32[]{:S(2)}) async-start(s32[128,1,2]{2,1,0:T(1,128)} %copy.48), calls=%async_computation.1 | async-start | bytes 131072 | tf_op jit(solution)/shard_map/all_to_all | solution.py:62
  35.7 7.9 %reshape.355 = bf16[128,2,8192]{2,1,0:T(2,128)(2,1)} reshape(bf16[128,16384]{1,0:T(8,128)(2,1)} %reduce.8) | data formatting | bytes 8388608
  43.6 10.5 %all-to-all-start.2 = ((bf16[128,2,8192]{2,1,0:T(2,128)(2,1)}), bf16[128,2,8192]{2,1,0:T(2,128)(2,1)}, u32[]{:S(2)}, u32[]{:S(2)}) async-start(bf16[128,2,8192]{2,1,0:T(2,128)(2,1)} %reshape.355), calls=%async_computation.2 | async-start | bytes 8388608 | tf_op jit(solution)/shard_map/all_to_all | solution.py:61
  54.5 9.0 %reduce-window.6 = s32[32,8,128]{2,1,0:T(8,128)S(1)} reduce-window(s32[32,8,128]{2,1,0:T(8,128)S(1)} %fusion.22, s32[]{:T(128)} %constant.95.clone.1), window={size=1x1x128 pad=0_0x0_0x127_0}, to_apply=%region_0.1 | reduce-window | flops 4161536 | bytes 262148 | tf_op jit(solution)/shard_map/reduce-window
  64.1 8.6 %gather_fusion.1 = s32[1024]{0:T(1024)S(1)} fusion(s32[1024,32]{0,1:T(8,128)S(1)} %bitcast.75, s32[1024]{0:T(1024)S(1)} %bitcast.77), kind=kCustom, calls=%fused_computation.1 | custom fusion | bytes 16384 | tf_op jit(solution)/shard_map/jit(take_along_axis)/gather | solution.py:83
  72.8 8.5 %scatter_custom_fusion = bf16[1152,1792]{1,0:T(8,128)(2,1)} fusion(s32[1024]{0:T(1024)S(1)} %bitcast.87, bf16[]{:T(256)} %constant.94.clone.1, bf16[128,1792]{1,0:T(8,128)(2,1)S(1)} %copy-done), kind=kCustom, calls=%fused_computation.25 | custom fusion | bytes 4587522 | tf_op jit(solution)/shard_map/scatter | solution.py:88
  87.7 17.9 %all-to-all-done.2 = bf16[128,2,8192]{2,1,0:T(2,128)(2,1)} async-done(((bf16[128,2,8192]{2,1,0:T(2,128)(2,1)}), bf16[128,2,8192]{2,1,0:T(2,128)(2,1)}, u32[]{:S(2)}, u32[]{:S(2)}) %all-to-all-start.2) | async-done | bytes 4194336 | tf_op jit(solution)/shard_map/all_to_all | solution.py:61
  105.6 7.9 %broadcast_in_dim.57 = bf16[36,32,4,1792]{3,0,2,1:T(8,128)(2,1)} broadcast(bf16[36,32,1792]{2,0,1:T(8,128)(2,1)} %copy.45), dimensions={0,1,3} | broadcast | bytes 20643840 | tf_op jit(solution)/shard_map/broadcast_in_dim | solution.py:91
  120.0 10.1 %copy.47 = bf16[1,7168,512]{1,2,0:T(8,128)(2,1)} copy(bf16[1,7168,512]{2,1,0:T(8,128)(2,1)} %param.14) | data formatting | bytes 14680064 | tf_op args[3]
  130.0 10.0 %copy.51 = bf16[1,7168,512]{1,2,0:T(8,128)(2,1)} copy(bf16[1,7168,512]{2,1,0:T(8,128)(2,1)} %param.15) | data formatting | bytes 14680064 | tf_op args[4]
  140.7 19.7 %reshape.356 = bf16[128,1,16384]{2,1,0:T(2,128)(2,1)} reshape(bf16[128,2,8192]{2,1,0:T(2,128)(2,1)} %all-to-all-done.2) | data formatting | bytes 8388608
  160.4 10.0 %convert_element_type.80 = f32[128,1,16384]{2,1,0:T(1,128)S(1)} convert(bf16[128,1,16384]{2,1,0:T(2,128)(2,1)} %reshape.356) | non-fusion elementwise | flops 2097152 | bytes 12582912 | tf_op jit(solution)/shard_map/convert_element_type | solution.py:64
  181.4 27.7 %scatter_fusion = f32[56,128,4,128]{3,1,2,0:T(8,128)} fusion(f32[56,128,4,128]{3,1,2,0:T(8,128)} %broadcast.326.clone.1, s32[128]{0:T(128)S(1)} %get-tuple-element.7, f32[128,128,128]{2,1,0:T(8,128)} %broadcast_multiply_fusion.3), kind=kCustom, calls=%fused_computation.6 | custom fusion | flops 2097152 | bytes 25166848 | tf_op jit(solution)/shard_map/scatter-add | solution.py:18
  209.1 13.8 %broadcast_multiply_fusion.2 = f32[56,128,4,128]{3,1,2,0:T(8,128)} fusion(f32[56,128,4,128]{3,1,2,0:T(8,128)} %scatter_fusion), kind=kLoop, calls=%fused_computation.23 | loop fusion | flops 3670016 | bytes 29360128 | tf_op jit(solution)/shard_map/mul | solution.py:20
  222.9 14.7 %copy.50 = f32[56,128,4,128]{1,0,3,2:T(8,128)} copy(f32[56,128,4,128]{3,1,2,0:T(8,128)} %broadcast_multiply_fusion.2) | data formatting | bytes 29360128 | tf_op jit(solution)/shard_map/mul | solution.py:20
  237.6 16.0 %mul.78 = f32[1,7168,512]{1,2,0:T(8,128)} reshape(f32[56,128,4,128]{1,0,3,2:T(8,128)} %copy.50) | data formatting | bytes 29360128 | tf_op jit(solution)/shard_map/mul | solution.py:20
  260.7 31.1 %scatter_fusion.1 = f32[56,128,4,128]{3,1,2,0:T(8,128)} fusion(f32[56,128,4,128]{3,1,2,0:T(8,128)} %broadcast.326.clone, s32[128]{0:T(128)S(1)} %get-tuple-element.6, f32[128,128,128]{2,1,0:T(8,128)} %broadcast_multiply_fusion.3), kind=kCustom, calls=%fused_computation.7 | custom fusion | flops 2097152 | bytes 25166848 | tf_op jit(solution)/shard_map/scatter-add | solution.py:18
  291.8 13.8 %broadcast_multiply_fusion.1 = f32[56,128,4,128]{3,1,2,0:T(8,128)} fusion(f32[56,128,4,128]{3,1,2,0:T(8,128)} %scatter_fusion.1), kind=kLoop, calls=%fused_computation.22 | loop fusion | flops 3670016 | bytes 29360128 | tf_op jit(solution)/shard_map/mul | solution.py:20
  305.6 14.7 %copy.52 = f32[56,128,4,128]{1,0,3,2:T(8,128)} copy(f32[56,128,4,128]{3,1,2,0:T(8,128)} %broadcast_multiply_fusion.1) | data formatting | bytes 29360128 | tf_op jit(solution)/shard_map/mul | solution.py:20
  320.3 16.2 %mul.81 = f32[1,7168,512]{1,2,0:T(8,128)} reshape(f32[56,128,4,128]{1,0,3,2:T(8,128)} %copy.52) | data formatting | bytes 29360128 | tf_op jit(solution)/shard_map/mul | solution.py:20
  343.6 30.7 %scatter_fusion.2 = f32[4,128,56,128]{3,1,2,0:T(8,128)} fusion(f32[4,128,56,128]{3,1,2,0:T(8,128)} %broadcast_in_dim.62, s32[128]{0:T(128)S(1)} %get-tuple-element.5, f32[128,128,128]{2,1,0:T(8,128)} %broadcast_multiply_fusion.3), kind=kCustom, calls=%fused_computation.8 | custom fusion | flops 2097152 | bytes 25166848 | tf_op jit(solution)/shard_map/scatter-add | solution.py:18
  374.4 13.8 %broadcast_multiply_fusion = f32[4,128,56,128]{3,1,2,0:T(8,128)} fusion(f32[4,128,56,128]{3,1,2,0:T(8,128)} %scatter_fusion.2), kind=kLoop, calls=%fused_computation.21 | loop fusion | flops 3670016 | bytes 29360128 | tf_op jit(solution)/shard_map/mul | solution.py:20
  388.2 18.9 %copy.53 = f32[4,128,56,128]{3,2,1,0:T(8,128)} copy(f32[4,128,56,128]{3,1,2,0:T(8,128)} %broadcast_multiply_fusion) | data formatting | bytes 29360128 | tf_op jit(solution)/shard_map/mul | solution.py:20
  407.1 16.5 %copy.46 = bf16[36,128,1792]{2,1,0:T(8,128)(2,1)} copy(bf16[36,128,1792]{2,0,1:T(8,128)(2,1)} %all-to-all-done) | data formatting | bytes 33030144 | tf_op jit(solution)/shard_map/all_to_all | solution.py:94
  423.7 26.3 %reshape.271 = bf16[1152,7168]{1,0:T(8,128)(2,1)} reshape(bf16[36,128,1792]{2,1,0:T(8,128)(2,1)} %copy.46) | data formatting | bytes 33030144 | tf_op jit(solution)/shard_map/reshape | solution.py:95
  450.0 18.9 %fusion.2 = f32[1152,512]{1,0:T(8,128)} fusion(bf16[1152,7168]{1,0:T(8,128)(2,1)} %reshape.271, f32[1,7168,512]{1,2,0:T(8,128)} %mul.78, bf16[1,7168,512]{1,2,0:T(8,128)(2,1)} %copy.47), kind=kOutput, calls=%fused_computation.15 | convolution fusion | flops 8466726912 | bytes 40894464 | tf_op jit(solution)/shard_map/dot_general | solution.py:96
  468.9 19.6 %fusion.15 = bf16[1152,512]{1,0:T(8,128)(2,1)S(1)} fusion(bf16[1152,7168]{1,0:T(8,128)(2,1)} %reshape.271, f32[1,7168,512]{1,2,0:T(8,128)} %mul.81, bf16[1,7168,512]{1,2,0:T(8,128)(2,1)} %copy.51, f32[1152,512]{1,0:T(8,128)} %fusion.2), kind=kOutput, calls=%fused_computation.28 | convolution fusion | flops 8470265856 | bytes 42074112 | tf_op jit(solution)/shard_map/dot_general | solution.py:97
  488.5 21.2 %convolution_convert_fusion = bf16[1152,7168]{1,0:T(8,128)(2,1)} fusion(bf16[1152,512]{1,0:T(8,128)(2,1)S(1)} %fusion.15, f32[64,8,56,128]{3,2,1,0:T(8,128)} %bitcast.82, bf16[1,512,7168]{2,1,0:T(8,128)(2,1)} %param.16), kind=kOutput, calls=%fused_computation.9 | convolution fusion | flops 8474984448 | bytes 39714816 | tf_op jit(solution)/shard_map/dot_general | solution.py:99
  509.7 18.0 %copy.54 = bf16[36,32,7168]{2,0,1:T(8,128)(2,1)} copy(bf16[36,32,7168]{2,1,0:T(8,128)(2,1)} %bitcast.81) | data formatting | bytes 33030144 | tf_op jit(solution)/shard_map/reshape | solution.py:103
  527.8 161.8 %reduce-scatter.2.cloned.1.call-done = bf16[36,32,1792]{2,0,1:T(8,128)(2,1)} async-done(((bf16[36,32,7168]{2,0,1:T(8,128)(2,1)}), bf16[36,32,1792]{2,0,1:T(8,128)(2,1)}) %reduce-scatter.2.cloned.1.call-update) | async-done | bytes 4128784 | tf_op jit(solution)/shard_map/reduce_scatter | solution.py:102
  697.1 58.1 %all-to-all-done.3 = bf16[36,32,1792]{2,0,1:T(8,128)(2,1)} async-done(((bf16[36,32,1792]{2,0,1:T(8,128)(2,1)}), bf16[36,32,1792]{2,0,1:T(8,128)(2,1)}, u32[]{:S(2)}, u32[]{:S(2)}) %all-to-all-start.3) | async-done | bytes 4128800 | tf_op jit(solution)/shard_map/all_to_all | solution.py:109
  760.3 10.7 %gather_fusion = bf16[1024,1792]{1,0:T(8,128)(2,1)} fusion(bf16[1152,1792]{1,0:T(8,128)(2,1)} %bitcast.74, s32[1024]{0:T(1024)S(1)} %broadcast_clamp_fusion), kind=kCustom, calls=%fused_computation | custom fusion | bytes 7344128 | tf_op jit(solution)/shard_map/gather | solution.py:110
  (54 shorter events, 75.7 us)
Async XLA Ops:
  6.5 66.2 %copy-start = (bf16[128,1792]{1,0:T(8,128)(2,1)S(1)}, bf16[128,1792]{1,0:T(8,128)(2,1)}, u32[]{:S(2)}) copy-start(bf16[128,1792]{1,0:T(8,128)(2,1)} %param.11) | copy-start | bytes 1376260
  10.5 33.1 %all-to-all-start.1 = ((s32[128,1,2]{2,1,0:T(1,128)}), s32[128,1,2]{2,1,0:T(1,128)S(1)}, u32[]{:S(2)}, u32[]{:S(2)}) async-start(s32[128,1,2]{2,1,0:T(1,128)} %copy.48), calls=%async_computation.1 | async-start | bytes 131072 | tf_op jit(solution)/shard_map/all_to_all | solution.py:62
  35.7 18.4 %copy-start.4 = (s32[128,8]{0,1:T(8,128)S(1)}, s32[128,8]{0,1:T(8,128)}, u32[]{:S(2)}) copy-start(s32[128,8]{0,1:T(8,128)} %param.12) | copy-start | bytes 12292
  43.6 62.0 %all-to-all-start.2 = ((bf16[128,2,8192]{2,1,0:T(2,128)(2,1)}), bf16[128,2,8192]{2,1,0:T(2,128)(2,1)}, u32[]{:S(2)}, u32[]{:S(2)}) async-start(bf16[128,2,8192]{2,1,0:T(2,128)(2,1)} %reshape.355), calls=%async_computation.2 | async-start | bytes 8388608 | tf_op jit(solution)/shard_map/all_to_all | solution.py:61
  72.8 40.8 %copy-start.2 = (s32[1024,1]{0,1:T(1,128)}, s32[1024,1]{0,1:T(1,128)S(1)}, u32[]{:S(2)}) copy-start(s32[1024,1]{0,1:T(1,128)S(1)} %compare_select_fusion.6) | copy-start | bytes 12292
  113.6 293.6 %all-to-all-start = ((bf16[36,128,1792]{2,0,1:T(8,128)(2,1)}), bf16[36,128,1792]{2,0,1:T(8,128)(2,1)}, u32[]{:S(2)}, u32[]{:S(2)}) async-start(bf16[36,128,1792]{2,0,1:T(8,128)(2,1)} %bitcast.76), calls=%async_computation | async-start | bytes 36700160 | tf_op jit(solution)/shard_map/all_to_all | solution.py:94
  119.5 570.0 %reduce-scatter.2.cloned.1.call-start = ((), (), s32[]{:S(2)}) async-start(), calls=%async_computation.5 | async-start | bytes 22937600 | tf_op jit(solution)/shard_map/reduce_scatter | solution.py:102
  527.8 169.2 %copy-start.5 = (f32[128,8]{0,1:T(8,128)S(1)}, f32[128,8]{0,1:T(8,128)}, u32[]{:S(2)}) copy-start(f32[128,8]{0,1:T(8,128)} %param.13) | copy-start | bytes 12292
  527.8 169.3 %copy-start.3 = (s32[1024,1]{0,1:T(1,128)S(1)}, s32[1024,1]{0,1:T(1,128)}, u32[]{:S(2)}) copy-start(s32[1024,1]{0,1:T(1,128)} %copy-done.2) | copy-start | bytes 12292
  689.6 65.6 %all-to-all-start.3 = ((bf16[36,32,1792]{2,0,1:T(8,128)(2,1)}), bf16[36,32,1792]{2,0,1:T(8,128)(2,1)}, u32[]{:S(2)}, u32[]{:S(2)}) async-start(bf16[36,32,1792]{2,0,1:T(8,128)(2,1)} %reduce-scatter.2.cloned.1.call-done), calls=%async_computation.4 | async-start | bytes 9175040 | tf_op jit(solution)/shard_map/all_to_all | solution.py:109
  760.3 16.8 %copy-start.1 = (bf16[128,1792]{1,0:T(8,128)(2,1)S(1)}, bf16[128,1792]{1,0:T(8,128)(2,1)}, u32[]{:S(2)}) copy-start(bf16[128,1792]{1,0:T(8,128)(2,1)} %param.11) | copy-start | bytes 1376260
Sparse Core Ops, SparseCore 0:
  527.9 161.6 reduce-scatter.1
where the time goes:
time: 796 us; the launch traced here: 784 us
  local copies, waits for them, and re-layouts  269 us (34%)
  waiting for transfers between devices  238 us (30%)
  other arithmetic  168 us (21%)
  matrix products  59.7 us (8%)
  starting transfers between devices  35.4 us (4%)
  between operations  14.8 us (2%)
    reduce_scatter x1, waiting for transfers between devices, shards(): lax.psum_scatter(partial_value.reshape(capacity, n_expert, model_width),...  162 us
    scatter-add x3, other arithmetic, refresh_share(): field = field.at[block_row, :, block_col, :].add(blocks, mode='drop')  89.5 us
    mul x5, local copies, waits for them, and re-layouts, refresh_share(): return (weight.astype(jnp.float32) + factor * field).astype(jnp.bfloat16)  80.5 us
    all_to_all x1, waiting for transfers between devices, shards(): lax.all_to_all(expert_out, 'expert', split_axis=1, concat_axis=1, tiled=T...  58.1 us
    unnamed x20, local copies, waits for them, and re-layouts  47.9 us
    mul x3, other arithmetic, refresh_share(): return (weight.astype(jnp.float32) + factor * field).astype(jnp.bfloat16)  41.4 us
    reshape x1, local copies, waits for them, and re-layouts, shards(): rows_in = arrived.reshape(capacity * n_expert, model_width)  26.3 us
    dot_general x1, matrix products, shards(): jnp.dot(hidden, down_new, preferred_element_type=jnp.float32)  21.2 us
  transfers between devices with their start and end apart: 5, of which 3 were waited for; matrix products, arithmetic and copies ran while one was open for 44% of the time, Pallas kernels for 0%

commit v1 on v0

v1 whole, which is shorter than its diff:
```python
import functools

import jax
import jax.numpy as jnp
from jax import lax
from jax.experimental import pallas as pl
from jax.experimental.pallas import tpu as pltpu
from jax.sharding import PartitionSpec as P

BLOCK = 128
META = 16
SLOTS_A = 24
SLOTS_B = 8
SLOTS_C = 4
VMEM_LIMIT = 60 * 2**20
BF16 = jnp.bfloat16
F32 = jnp.float32
LIGHT = pl.CostEstimate(flops=0, bytes_accessed=0, transcendentals=0)
HBM = pl.BlockSpec(memory_space=pltpu.HBM)


def ring(n, shift):
    return [(i, (i + shift) % n) for i in range(n)]


def spread_kernel(owner_ref, count_ref, blocks_ref, meta_ref, out_ref):
    out_ref[:, BLOCK:, :] = meta_ref[...]

    def put(i, carry):
        out_ref[owner_ref[i], :BLOCK, :] = blocks_ref[i]
        return carry

    lax.fori_loop(0, count_ref[0], put, 0)


def spread_blocks(owner, count, blocks, meta):
    sources = meta.shape[0]
    shape = (sources, BLOCK + META, BLOCK)
    return pl.pallas_call(
        spread_kernel,
        out_shape=jax.ShapeDtypeStruct(shape, BF16),
        grid_spec=pltpu.PrefetchScalarGridSpec(
            num_scalar_prefetch=2,
            grid=(1,),
            in_specs=[
                pl.BlockSpec(blocks.shape, lambda i, *_: (0, 0, 0)),
                pl.BlockSpec(meta.shape, lambda i, *_: (0, 0, 0)),
            ],
            out_specs=pl.BlockSpec(shape, lambda i, *_: (0, 0, 0)),
        ),
        compiler_params=pltpu.CompilerParams(vmem_limit_bytes=VMEM_LIMIT),
        cost_estimate=LIGHT,
    )(owner, count, blocks, meta)


def arrange_kernel(order_ref, gate_ref, up_ref, down_ref, gu_ref, dn_ref):
    hid = gate_ref.shape[1]
    gu_ref[:, :hid] = gate_ref[...]
    gu_ref[:, hid:] = up_ref[...]
    dn_ref[...] = down_ref[...]


def arrange(order, gate, up, down):
    width, hid = gate.shape
    n = order.shape[0]
    parts = 2
    step = width // (n * parts)

    def rows(i, order_ref):
        return (order_ref[i // parts] * parts + i % parts, 0)

    def cols(i, order_ref):
        return (0, order_ref[i // parts] * parts + i % parts)

    return pl.pallas_call(
        arrange_kernel,
        out_shape=(
            jax.ShapeDtypeStruct((width, 2 * hid), BF16),
            jax.ShapeDtypeStruct((hid, width), BF16),
        ),
        grid_spec=pltpu.PrefetchScalarGridSpec(
            num_scalar_prefetch=1,
            grid=(n * parts,),
            in_specs=[
                pl.BlockSpec((step, hid), rows),
                pl.BlockSpec((step, hid), rows),
                pl.BlockSpec((hid, step), cols),
            ],
            out_specs=[
                pl.BlockSpec((step, 2 * hid), lambda i, order_ref: (i, 0)),
                pl.BlockSpec((hid, step), lambda i, order_ref: (0, i)),
            ],
        ),
        compiler_params=pltpu.CompilerParams(vmem_limit_bytes=VMEM_LIMIT),
        cost_estimate=LIGHT,
    )(order, gate, up, down)


def patch_kernel(
    factors,
    where_ref,
    scale_ref,
    incoming_ref,
    gate_ref,
    up_ref,
    down_ref,
    gu_in_ref,
    dn_in_ref,
    gu_ref,
    dn_ref,
    blocks,
    held,
    total,
    in_sems,
    out_sems,
    block_sem,
):
    sources = blocks.shape[0]
    load = pltpu.make_async_copy(
        incoming_ref.at[:, pl.ds(0, BLOCK), :], blocks, block_sem.at[0]
    )
    load.start()

    def block_of(ref, row, col):
        return ref.at[
            pl.ds(pl.multiple_of(row * BLOCK, BLOCK), BLOCK),
            pl.ds(pl.multiple_of(col * BLOCK, BLOCK), BLOCK),
        ]

    def fetch(s, ref):
        return pltpu.make_async_copy(
            block_of(ref, where_ref[1, s], where_ref[2, s]), held.at[s], in_sems.at[s]
        )

    def put(s, ref):
        return pltpu.make_async_copy(
            held.at[s], block_of(ref, where_ref[3, s], where_ref[4, s]), out_sems.at[s]
        )

    corner = gate_ref.at[pl.ds(0, BLOCK), pl.ds(0, BLOCK)]

    def arrived(s):
        return pltpu.make_async_copy(corner, held.at[s], in_sems.at[s])

    def written(s):
        return pltpu.make_async_copy(
            held.at[s], gu_ref.at[pl.ds(0, BLOCK), pl.ds(0, BLOCK)], out_sems.at[s]
        )

    def leads(s):
        return where_ref[0, s] == s

    def start(s, carry):
        for m, ref in enumerate((gate_ref, up_ref, down_ref)):

            @pl.when(leads(s) & (where_ref[5, s] == m))
            def _():
                fetch(s, ref).start()

        return carry

    lax.fori_loop(0, sources, start, 0)
    load.wait()

    def add(s, carry):
        first = where_ref[0, s]

        @pl.when(first == s)
        def _():
            total[s] = blocks[s].astype(F32) * scale_ref[s]

        @pl.when((first >= 0) & (first != s))
        def _():
            total[first] = total[first] + blocks[s].astype(F32) * scale_ref[s]

        return carry

    lax.fori_loop(0, sources, add, 0)

    def finish(s, carry):
        @pl.when(leads(s))
        def _():
            arrived(s).wait()
            factor = jnp.where(where_ref[5, s] == 2, F32(factors[1]), F32(factors[0]))
            held[s] = (held[s].astype(F32) + factor * total[s]).astype(BF16)

        @pl.when(leads(s) & (where_ref[5, s] < 2))
        def _():
            put(s, gu_ref).start()

        @pl.when(leads(s) & (where_ref[5, s] == 2))
        def _():
            put(s, dn_ref).start()

        return carry

    lax.fori_loop(0, sources, finish, 0)

    def drain(s, carry):
        @pl.when(leads(s))
        def _():
            written(s).wait()

        return carry

    lax.fori_loop(0, sources, drain, 0)


def patch(factors, where, scale, incoming, gate, up, down, gu, dn):
    sources = incoming.shape[0]
    return pl.pallas_call(
        functools.partial(patch_kernel, factors),
        out_shape=(
            jax.ShapeDtypeStruct(gu.shape, BF16),
            jax.ShapeDtypeStruct(dn.shape, BF16),
        ),
        grid_spec=pltpu.PrefetchScalarGridSpec(
            num_scalar_prefetch=2,
            grid=(1,),
            in_specs=[HBM] * 6,
            out_specs=[HBM, HBM],
            scratch_shapes=[
                pltpu.VMEM((sources, BLOCK, BLOCK), BF16),
                pltpu.VMEM((sources, BLOCK, BLOCK), BF16),
                pltpu.VMEM((sources, BLOCK, BLOCK), F32),
                pltpu.SemaphoreType.DMA((sources,)),
                pltpu.SemaphoreType.DMA((sources,)),
                pltpu.SemaphoreType.DMA((1,)),
            ],
        ),
        input_output_aliases={6: 0, 7: 1},
        compiler_params=pltpu.CompilerParams(vmem_limit_bytes=VMEM_LIMIT),
        cost_estimate=LIGHT,
    )(where, scale, incoming, gate, up, down, gu, dn)


def dot(a, b):
    return jnp.dot(a, b, preferred_element_type=F32)


def weighted(table, rows):
    both = dot(table, rows)
    n = both.shape[0] // 2
    return both[:n] + both[n:]


def two_parts(table):
    high = table.astype(BF16)
    low = (table - high.astype(F32)).astype(BF16)
    return jnp.concatenate([high, low], axis=0)


def silu_product(acc):
    hid = acc.shape[1] // 2
    return (jax.nn.silu(acc[:, :hid]) * acc[:, hid:]).astype(BF16)


def up_kernel(slots, rows_ref, folded_ref, gu_ref, hidden_b_ref, hidden_c_ref, acc_b, acc_c):
    step, steps = pl.program_id(0), pl.num_programs(0)

    @pl.when(step == 0)
    def _():
        acc_b[...] = jnp.zeros_like(acc_b)
        acc_c[...] = jnp.zeros_like(acc_c)

    n = rows_ref.shape[0]
    row = lax.broadcasted_iota(jnp.int32, (n, n), 0)
    col = lax.broadcasted_iota(jnp.int32, (n, n), 1)
    same = (row // slots == col // slots) & (row % (slots // 2) == col % (slots // 2))
    second = (step >= steps // 2).astype(jnp.int32)
    pick = (same & ((col % slots) // (slots // 2) == second)).astype(BF16)
    acc_b[...] += dot(rows_ref[...], gu_ref[...])
    acc_c[...] += dot(dot(pick, folded_ref[...]).astype(BF16), gu_ref[...])

    @pl.when(step == steps - 1)
    def _():
        hidden_b_ref[...] = silu_product(acc_b[...])
        hidden_c_ref[...] = silu_product(acc_c[...])


def up_projection(slots, rows, gu):
    n = rows.shape[0]
    width, wide = gu.shape
    steps = 8
    step = width // steps
    out = jax.ShapeDtypeStruct((n, wide // 2), BF16)
    return pl.pallas_call(
        functools.partial(up_kernel, slots),
        out_shape=(out, out),
        grid=(steps,),
        in_specs=[
            pl.BlockSpec((n, step), lambda k: (0, k)),
            pl.BlockSpec((n, step), lambda k: (0, steps + k % (steps // 2))),
            pl.BlockSpec((step, wide), lambda k: (k, 0)),
        ],
        out_specs=[pl.BlockSpec((n, wide // 2), lambda k: (0, 0))] * 2,
        scratch_shapes=[pltpu.VMEM((n, wide), F32), pltpu.VMEM((n, wide), F32)],
        compiler_params=pltpu.CompilerParams(vmem_limit_bytes=VMEM_LIMIT),
        cost_estimate=LIGHT,
    )(rows, rows, gu)


def down_kernel(slots, hidden_b_ref, hidden_c_ref, dn_ref, dn_second_ref, out_ref):
    step = pl.program_id(0)

    @pl.when(step < 8)
    def _():
        out_ref[...] = dot(hidden_b_ref[...], dn_ref[...]).astype(BF16)

    @pl.when(step >= 8)
    def _():
        first = dot(hidden_c_ref[...], dn_ref[...])
        second = dot(hidden_c_ref[...], dn_second_ref[...])
        row = lax.broadcasted_iota(jnp.int32, first.shape, 0)
        out_ref[...] = jnp.where(row % slots < slots // 2, first, second).astype(BF16)


def down_projection(slots, hidden_b, hidden_c, dn):
    n, hid = hidden_b.shape
    width = dn.shape[1]
    step = width // 8
    return pl.pallas_call(
        functools.partial(down_kernel, slots),
        out_shape=jax.ShapeDtypeStruct((n, width + width // 2), BF16),
        grid=(12,),
        in_specs=[
            pl.BlockSpec((n, hid), lambda k: (0, 0)),
            pl.BlockSpec((n, hid), lambda k: (0, 0)),
            pl.BlockSpec((hid, step), lambda k: (0, k % 8)),
            pl.BlockSpec((hid, step), lambda k: (0, 4 + jnp.maximum(k - 8, 0))),
        ],
        out_specs=pl.BlockSpec((n, step), lambda k: (0, k)),
        compiler_params=pltpu.CompilerParams(vmem_limit_bytes=VMEM_LIMIT),
        cost_estimate=LIGHT,
    )(hidden_b, hidden_c, dn, dn)


def mix_kernel(share_b_ref, share_c_ref, rows_ref, folded_ref, out_ref):
    n = out_ref.shape[1]
    both = dot(share_b_ref[...], rows_ref[...]) + dot(share_c_ref[...], folded_ref[...])
    out_ref[0] = (both[:n] + both[n:]).astype(BF16)


def mix_whole(share_b, share_c, rows):
    n = rows.shape[0]
    width = rows.shape[1] * 2 // 3
    two = share_b.shape[0]
    step = width // 8
    return pl.pallas_call(
        mix_kernel,
        out_shape=jax.ShapeDtypeStruct((4, two // 2, width // 4), BF16),
        grid=(8,),
        in_specs=[
            pl.BlockSpec((two, n), lambda k: (0, 0)),
            pl.BlockSpec((two, n), lambda k: (k // 4, 0)),
            pl.BlockSpec((n, step), lambda k: (0, k)),
            pl.BlockSpec((n, step), lambda k: (0, 8 + k % 4)),
        ],
        out_specs=pl.BlockSpec((1, two // 2, step), lambda k: (k // 2, 0, k % 2)),
        compiler_params=pltpu.CompilerParams(vmem_limit_bytes=VMEM_LIMIT),
        cost_estimate=LIGHT,
    )(share_b, share_c, rows, rows)


def shards(
    tokens,
    routes,
    route_weight,
    gate_weight,
    up_weight,
    down_weight,
    delta_values,
    delta_owner,
    delta_index,
    delta_scale,
    delta_count,
):
    n_expert = lax.axis_size("expert")
    n_group = lax.axis_size("group")
    sources = n_expert * n_group
    me = lax.axis_index("group")
    tok_rows, quarter = tokens.shape
    width, hid = gate_weight.shape[1:]
    listed = delta_owner.shape[1]
    top_count = routes.shape[1]
    capacity = tok_rows * top_count * 9 // (8 * n_expert)
    slots_a = SLOTS_A
    slots_b, slots_c = SLOTS_B, SLOTS_C
    assert slots_a + slots_b + slots_c == capacity and slots_b == 2 * slots_c
    half = width // 2
    gate, up, down = gate_weight[0], up_weight[0], down_weight[0]

    def shift(x, by):
        return lax.ppermute(x, "group", ring(n_group, by))

    def exchange(x, axes):
        return lax.all_to_all(x, axes, split_axis=0, concat_axis=0, tiled=True)

    order = jnp.stack([me, (me + 3) % 4, (me + 1) % 4, (me + 2) % 4]).astype(jnp.int32)
    place = jnp.zeros((4,), jnp.int32).at[order].set(jnp.arange(4, dtype=jnp.int32))

    named = routes[:, :, None] == jnp.arange(n_expert, dtype=jnp.int32)
    member = jnp.any(named, axis=1)
    share = jnp.sum(jnp.where(named, route_weight[:, :, None], 0.0), axis=1)
    before = jnp.tri(tok_rows, k=-1, dtype=BF16)
    rank = dot(before, member.astype(BF16)).astype(jnp.int32)
    rank = jnp.where(member, rank, -1).T
    slot_a = jnp.arange(slots_a, dtype=jnp.int32)
    slot_b = jnp.arange(slots_a, slots_a + slots_b, dtype=jnp.int32)
    slot_c = slots_a + slots_b + slot_b % slots_c
    front = (slot_b - slots_a) < slots_c
    slot_c0, slot_c1 = jnp.where(front, slot_c, -2), jnp.where(front, -2, slot_c)

    def pick(slots):
        hit = rank[:, None, :] == slots[None, :, None]
        return hit.astype(BF16).reshape(n_expert * slots.shape[0], tok_rows)

    def shares(slots):
        hit = rank.T[:, :, None] == slots[None, None, :]
        table = jnp.where(hit, share[:, :, None], 0.0)
        return two_parts(table.reshape(tok_rows, n_expert * slots.shape[0]))

    pick_a = lax.optimization_barrier(pick(slot_a))

    send_a = dot(pick_a, tokens).astype(BF16)
    send_a, tokens = lax.optimization_barrier((send_a, tokens))
    tokens_all = jnp.concatenate(
        [tokens, shift(tokens, 1), shift(tokens, -1), shift(tokens, 2)], axis=1
    )
    recv_a = exchange(send_a.reshape(n_expert, slots_a, quarter), "expert")
    rows_a = recv_a.reshape(n_expert * slots_a, quarter)

    live = jnp.arange(listed, dtype=jnp.int32) < delta_count[0]
    to = (delta_owner[0][None, :] == jnp.arange(sources, dtype=jnp.int32)[:, None]) & live[None, :]
    slot_out = jnp.sum(jnp.where(to, delta_index[0][None, :] + 1, 0), axis=1)
    scale_out = jnp.sum(jnp.where(to, delta_scale[0][None, :], 0), axis=1)
    meta = jnp.stack([slot_out // 8, slot_out % 8, scale_out], axis=1)
    meta = jnp.pad(meta, ((0, 0), (0, META - 3))).astype(BF16)
    meta = jnp.broadcast_to(meta[:, :, None], (sources, META, BLOCK))
    blocks = delta_values.reshape(listed, BLOCK, BLOCK)
    blocks, meta, tokens_all = lax.optimization_barrier((blocks, meta, tokens_all))
    outgoing = spread_blocks(delta_owner[0], delta_count, blocks, meta)
    incoming = exchange(outgoing, ("expert", "group"))

    gu, dn = arrange(order, gate, up, down)

    pick_c = jnp.concatenate([pick(slot_c0), pick(slot_c1)], axis=1)
    share_c = jnp.concatenate([shares(slot_c0), shares(slot_c1)], axis=0)
    tables = (pick(slot_b), pick_c, shares(slot_a), shares(slot_b), share_c)
    pick_b, pick_c, share_a, share_b, share_c = lax.optimization_barrier(tables)
    tokens_all, gu, dn = lax.optimization_barrier((tokens_all, gu, dn))
    send_b = dot(pick_b, tokens_all).astype(BF16)
    halves = jnp.concatenate([tokens_all[:, :half], tokens_all[:, half:]], axis=0)
    send_c = dot(pick_c, halves).astype(BF16)
    send_b = jnp.concatenate([send_b, send_c], axis=1)

    rows = n_expert * slots_a // 2
    after, ahead = shift(rows_a, 1), shift(rows_a, -1)
    far_top, far_bottom = shift(after[:rows], 1), shift(ahead[rows:], -1)

    send_b, incoming = lax.optimization_barrier((send_b, incoming))
    recv_b = exchange(send_b.reshape(n_expert, slots_b, width + half), "expert")
    rows_b = recv_b.reshape(n_expert * slots_b, width + half)

    meta_in = incoming[:, BLOCK : BLOCK + META, 0].astype(jnp.int32)
    slot = meta_in[:, 0] * 8 + meta_in[:, 1] - 1
    scale = jnp.exp2(meta_in[:, 2].astype(F32))
    same = slot[:, None] == slot[None, :]
    entry = jnp.arange(sources, dtype=jnp.int32)
    first = jnp.min(jnp.where(same, entry[None, :], sources), axis=1)
    first = jnp.where(slot >= 0, first, -1)
    row_blocks, col_blocks = width // BLOCK, hid // BLOCK
    per_matrix = row_blocks * col_blocks
    near = row_blocks // n_group
    slot = jnp.maximum(slot, 0)
    matrix = slot // per_matrix
    inside = slot % per_matrix
    is_down = matrix == 2
    wide = jnp.where(is_down, inside % row_blocks, inside // col_blocks)
    narrow = jnp.where(is_down, inside // row_blocks, inside % col_blocks)
    moved = place[wide // near] * near + wide % near
    where = jnp.stack(
        [
            first,
            jnp.where(is_down, narrow, wide),
            jnp.where(is_down, wide, narrow),
            jnp.where(is_down, narrow, moved),
            jnp.where(is_down, moved, narrow + col_blocks * (matrix == 1)),
            matrix,
        ]
    ).astype(jnp.int32)
    factors = (width**-0.5, (hid * n_group) ** -0.5)
    gu, dn = patch(factors, where, scale, incoming, gate, up, down, gu, dn)

    acc = dot(rows_a, gu[:quarter])
    acc = acc + dot(after, gu[quarter : 2 * quarter])
    acc = acc + dot(ahead, gu[2 * quarter : 3 * quarter])
    acc, far_top, far_bottom = lax.optimization_barrier((acc, far_top, far_bottom))
    last = gu[3 * quarter :]
    hidden_top = silu_product(acc[:rows] + dot(far_top, last))
    hidden_bottom = silu_product(acc[rows:] + dot(far_bottom, last))

    def part(hidden, index):
        return dot(hidden, dn[:, index * quarter : (index + 1) * quarter])

    top_3, bottom_3 = part(hidden_top, 3).astype(BF16), part(hidden_bottom, 3).astype(BF16)
    top_3, bottom_3, rows_b = lax.optimization_barrier((top_3, bottom_3, rows_b))
    top_3, bottom_3 = shift(top_3, -1), shift(bottom_3, 1)

    hidden_b, hidden_c = up_projection(slots_b, rows_b, gu)
    part_b = down_projection(slots_b, hidden_b, hidden_c, dn)
    back_b = exchange(part_b.reshape(n_expert, slots_b, width + half), "expert")

    hidden_a = jnp.concatenate([hidden_top, hidden_bottom], axis=0)
    part_1, part_2 = part(hidden_a, 1), part(hidden_a, 2)
    none = jnp.zeros_like(top_3)
    part_1 = (part_1 + jnp.concatenate([top_3, none], axis=0).astype(F32)).astype(BF16)
    part_2 = (part_2 + jnp.concatenate([none, bottom_3], axis=0).astype(F32)).astype(BF16)
    part_1, part_2 = shift(part_1, -1), shift(part_2, 1)
    out_a = part(hidden_a, 0) + part_1.astype(F32) + part_2.astype(F32)
    out_a, back_b = lax.optimization_barrier((out_a.astype(BF16), back_b))
    back_a = exchange(out_a.reshape(n_expert, slots_a, quarter), "expert")

    mix_b = mix_whole(share_b, share_c, back_b.reshape(n_expert * slots_b, width + half))
    result = mix_b[0].astype(F32)
    for i, by in ((1, -1), (2, 1), (3, 2)):
        result = result + shift(mix_b[i], by).astype(F32)
    mix_a = weighted(share_a, back_a.reshape(n_expert * slots_a, quarter))
    return (result + mix_a).astype(BF16)


def solution(mesh):
    return jax.shard_map(
        shards,
        mesh=mesh,
        in_specs=(
            P("expert", "group"),
            P("expert", None),
            P("expert", None),
            P("expert", None, "group"),
            P("expert", None, "group"),
            P("expert", "group", None),
            P(("expert", "group"), None),
            P(("expert", "group"), None),
            P(("expert", "group"), None),
            P(("expert", "group"), None),
            P(("expert", "group")),
        ),
        out_specs=P("expert", "group"),
        check_vma=False,
    )
```

time: 796 us -> 375 us (0.47); the launches traced: 784 us -> 373 us
  local copies, waits for them, and re-layouts: 269 us -> 11.6 us
  other arithmetic: 168 us -> 18.6 us
  Pallas kernels: 0 us -> 75.6 us
  waiting for transfers between devices: 238 us -> 168 us
  starting transfers between devices: 35.4 us -> 59.9 us
  matrix products: 59.7 us -> 37.6 us
  between operations: 14.8 us -> 1.34 us
    reduce_scatter x1 -> x0, waiting for transfers between devices: 162 us -> none  [shards(): lax.psum_scatter(partial_value.reshape(capacity, n_expert, model_width),...]
    ppermute x0 -> x14, waiting for transfers between devices: none -> 115 us  [shift(): return lax.ppermute(x, 'group', ring(n_group, by))]
    scatter-add x3 -> x0, other arithmetic: 89.5 us -> none  [refresh_share(): field = field.at[block_row, :, block_col, :].add(blocks, mode='drop')]
    mul x5 -> x0, local copies, waits for them, and re-layouts: 80.5 us -> none  [refresh_share(): return (weight.astype(jnp.float32) + factor * field).astype(jnp.bfloat16)]
    pallas_call x0 -> x6, Pallas kernels: none -> 75.6 us  [the longest x1 17.3 us: arrange(): pl.pallas_call(arrange_kernel, out_shape=(jax.ShapeDtypeStruct((width, 2...]
    unnamed x20 -> x36, local copies, waits for them, and re-layouts: 47.9 us -> 2.24 us
    mul x4 -> x0, other arithmetic: 45.3 us -> none  [the longest x3 41.4 us: refresh_share(): return (weight.astype(jnp.float32) + factor * field).astype(jnp.bfloat16)]
    reshape x2 -> x0, local copies, waits for them, and re-layouts: 44.3 us -> none  [the longest x1 26.3 us: shards(): rows_in = arrived.reshape(capacity * n_expert, model_width)]
  transfers between devices with their start and end apart: 5 -> 19, of which waited for: 3 -> 10; matrix products, arithmetic and copies ran while one was open for 44% -> 16% of each run, Pallas kernels for 0% -> 20%
where the time goes in v1:
time: 375 us; the launch traced here: 373 us
  waiting for transfers between devices  168 us (45%)
  Pallas kernels  75.6 us (20%)
  starting transfers between devices  59.9 us (16%)
  matrix products  37.6 us (10%)
  other arithmetic  18.6 us (5%)
  local copies, waits for them, and re-layouts  11.6 us (3%)
    ppermute x14, waiting for transfers between devices, shift(): return lax.ppermute(x, 'group', ring(n_group, by))  115 us
    all_to_all x5, waiting for transfers between devices, exchange(): return lax.all_to_all(x, axes, split_axis=0, concat_axis=0, tiled=True)  53.4 us
    dot_general x15, matrix products, dot(): return jnp.dot(a, b, preferred_element_type=F32)  37.6 us
    all_to_all x5, starting transfers between devices, exchange(): return lax.all_to_all(x, axes, split_axis=0, concat_axis=0, tiled=True)  34.9 us
    ppermute x14, starting transfers between devices, shift(): return lax.ppermute(x, 'group', ring(n_group, by))  25 us
    pallas_call x1, Pallas kernels, arrange(): pl.pallas_call(arrange_kernel, out_shape=(jax.ShapeDtypeStruct((width, 2...  17.3 us
    pallas_call x1, Pallas kernels, up_projection(): pl.pallas_call(functools.partial(up_kernel, slots), out_shape=(out, out),...  15.5 us
    pallas_call x1, Pallas kernels, patch(): pl.pallas_call(functools.partial(patch_kernel, factors), out_shape=(jax.S...  15.4 us
  transfers between devices with their start and end apart: 19, of which 10 were waited for; matrix products, arithmetic and copies ran while one was open for 16% of the time, Pallas kernels for 20%

profile of v1, /device:TPU:0, one launch (start us, length us, event | category | flops | bytes accessed | tf_op | source)
XLA Modules:
  0.0 372.8 jit_solution(5366253588594075054)
XLA Ops:
  1.2 3.5 convolution_convert_fusion.2
  4.7 8.6 %all-to-all-start = ((bf16[32,24,1792]{2,1,0:T(8,128)(2,1)}), bf16[32,24,1792]{2,1,0:T(8,128)(2,1)}, u32[]{:S(2)}, u32[]{:S(2)}) async-start(bf16[32,24,1792]{2,1,0:T(8,128)(2,1)} %bitcast.7), calls=%async_computation | async-start | bytes 5505024 | tf_op jit(solution)/shard_map/all_to_all | solution.py:397
  13.4 3.3 collective-permute-start.2
  22.5 6.0 %collective-permute-done.2 = bf16[128,1792]{1,0:T(8,128)(2,1)} collective-permute-done((bf16[128,1792]{1,0:T(8,128)(2,1)S(1)}, bf16[128,1792]{1,0:T(8,128)(2,1)}, u32[]{:S(2)}, u32[]{:S(2)}) %collective-permute-start.2) | collective-permute-done | bytes 458784 | tf_op jit(solution)/shard_map/ppermute | solution.py:394
  28.5 9.4 %collective-permute-done.1 = bf16[128,1792]{1,0:T(8,128)(2,1)} collective-permute-done((bf16[128,1792]{1,0:T(8,128)(2,1)S(1)}, bf16[128,1792]{1,0:T(8,128)(2,1)}, u32[]{:S(2)}, u32[]{:S(2)}) %collective-permute-start.1) | collective-permute-done | bytes 458784 | tf_op jit(solution)/shard_map/ppermute | solution.py:394
  40.6 4.9 %shard_map.110 = bf16[128,144,128]{2,1,0:T(8,128)(2,1)} custom-call(s32[64]{0:T(128)} %bitcast.161, s32[1]{0:T(128)} %copy.53.count_ref, bf16[64,128,128]{2,1,0:T(8,128)(2,1)} %bitcast.155, bf16[128,16,128]{2,1,0:T(8,128)(2,1)} %broadcast_in_dim.146.meta_ref), custom_call_target="tpu_custom_call" | custom-call | tf_op jit(solution)/shard_map/pallas_call | solution.py:39
  45.5 5.4 %all-to-all-done = bf16[32,24,1792]{2,1,0:T(8,128)(2,1)} async-done(((bf16[32,24,1792]{2,1,0:T(8,128)(2,1)}), bf16[32,24,1792]{2,1,0:T(8,128)(2,1)}, u32[]{:S(2)}, u32[]{:S(2)}) %all-to-all-start) | async-done | bytes 2752544 | tf_op jit(solution)/shard_map/all_to_all | solution.py:397
  50.9 5.9 %all-to-all-start.1 = ((bf16[128,144,128]{2,1,0:T(8,128)(2,1)}), bf16[128,144,128]{2,1,0:T(8,128)(2,1)}, u32[]{:S(2)}, u32[]{:S(2)}) async-start(bf16[128,144,128]{2,1,0:T(8,128)(2,1)} %shard_map.110), calls=%async_computation.1 | async-start | bytes 9437184 | tf_op jit(solution)/shard_map/all_to_all | solution.py:397
  60.6 17.3 %shard_map.109 = (bf16[7168,1024]{1,0:T(8,128)(2,1)}, bf16[512,7168]{1,0:T(8,128)(2,1)}) custom-call(s32[4]{0:T(128)} %pad_add_fusion.order_ref, bf16[7168,512]{1,0:T(8,128)(2,1)} %bitcast.146, bf16[7168,512]{1,0:T(8,128)(2,1)} %bitcast.148, bf16[512,7168]{1,0:T(8,128)(2,1)} %bitcast.150), custom_call_target="tpu_custom_call" | custom-call | tf_op jit(solution)/shard_map/pallas_call | solution.py:75
  83.9 2.7 pad_maximum_fusion
  86.6 27.5 %all-to-all-done.1.incoming_ref = bf16[128,144,128]{2,1,0:T(8,128)(2,1)} async-done(((bf16[128,144,128]{2,1,0:T(8,128)(2,1)}), bf16[128,144,128]{2,1,0:T(8,128)(2,1)}, u32[]{:S(2)}, u32[]{:S(2)}) %all-to-all-start.1) | async-done | bytes 4718624 | tf_op jit(solution)/shard_map/all_to_all | solution.py:397
  115.7 5.1 %all-to-all-start.2 = ((bf16[32,8,10752]{2,1,0:T(8,128)(2,1)}), bf16[32,8,10752]{2,1,0:T(8,128)(2,1)}, u32[]{:S(2)}, u32[]{:S(2)}) async-start(bf16[32,8,10752]{2,1,0:T(8,128)(2,1)} %bitcast.153), calls=%async_computation.2 | async-start | bytes 11010048 | tf_op jit(solution)/shard_map/all_to_all | solution.py:397
  120.7 2.6 fusion.52
  124.6 15.4 %shard_map.111 = (bf16[7168,1024]{1,0:T(8,128)(2,1)}, bf16[512,7168]{1,0:T(8,128)(2,1)}) custom-call(s32[6,128]{1,0:T(8,128)} %stack.56.where_ref, f32[128]{0:T(128)} %fusion.59.scale_ref, bf16[128,144,128]{2,1,0:T(8,128)(2,1)} %all-to-all-done.1.incoming_ref, bf16[7168,512]{1,0:T(8,128)(2,1)} %bitcast.147, ...), custom_call_target="tpu_custom_call", output_to_operand_aliasing={{0}: (6, {}), {1}: (7, {})} | custom-call | tf_op jit(solution)/shard_map/pallas_call | solution.py:211
  140.0 6.0 %fusion.4 = f32[768,1024]{1,0:T(8,128)S(1)} fusion(bf16[768,1792]{1,0:T(8,128)(2,1)} %bitcast.8, bf16[7168,1024]{1,0:T(8,128)(2,1)} %get-tuple-element.49.gu_ref), kind=kOutput, calls=%fused_computation.11 | convolution fusion | flops 2818572288 | bytes 9568256 | tf_op jit(solution)/shard_map/dot_general | solution.py:238
  146.0 22.5 %collective-permute-done.3 = bf16[768,1792]{1,0:T(8,128)(2,1)} collective-permute-done((bf16[768,1792]{1,0:T(8,128)(2,1)}, bf16[768,1792]{1,0:T(8,128)(2,1)}, u32[]{:S(2)}, u32[]{:S(2)}) %collective-permute-start.3) | collective-permute-done | bytes 2752544 | tf_op jit(solution)/shard_map/ppermute | solution.py:394
  171.5 3.3 collective-permute-start.6
  174.8 4.8 %fusion.2 = f32[768,1024]{1,0:T(8,128)S(1)} fusion(bf16[768,1792]{1,0:T(8,128)(2,1)} %collective-permute-done.3, bf16[7168,1024]{1,0:T(8,128)(2,1)S(1)} %copy-done), kind=kOutput, calls=%fused_computation.9 | convolution fusion | flops 2818572288 | bytes 9568256 | tf_op jit(solution)/shard_map/dot_general | solution.py:238
  179.6 4.8 %add_add_fusion = f32[768,1024]{1,0:T(8,128)S(1)} fusion(f32[768,1024]{1,0:T(8,128)S(1)} %fusion.4, f32[768,1024]{1,0:T(8,128)S(1)} %fusion.2, bf16[768,1792]{1,0:T(8,128)(2,1)} %collective-permute-done.4, bf16[7168,1024]{1,0:T(8,128)(2,1)S(1)} %copy-done), kind=kOutput, calls=%fused_computation.18 | convolution fusion | flops 2820145152 | bytes 15859712 | tf_op jit(solution)/shard_map/dot_general | solution.py:238
  184.4 18.6 %collective-permute-done.5 = bf16[384,1792]{1,0:T(8,128)(2,1)S(1)} collective-permute-done((bf16[384,1792]{1,0:T(8,128)(2,1)S(1)}, bf16[384,1792]{1,0:T(8,128)(2,1)S(1)}, u32[]{:S(2)}, u32[]{:S(2)}) %collective-permute-start.5) | collective-permute-done | bytes 1376288 | tf_op jit(solution)/shard_map/ppermute | solution.py:394
  211.6 3.5 collective-permute-start.7
  215.1 15.5 %shard_map.112 = (bf16[256,512]{1,0:T(8,128)(2,1)}, bf16[256,512]{1,0:T(8,128)(2,1)}) custom-call(bf16[256,10752]{1,0:T(8,128)(2,1)} %bitcast.41.rows_ref.folded_ref, bf16[256,10752]{1,0:T(8,128)(2,1)} %bitcast.41.rows_ref.folded_ref, bf16[7168,1024]{1,0:T(8,128)(2,1)} %get-tuple-element.49.gu_ref), custom_call_target="tpu_custom_call" | custom-call | tf_op jit(solution)/shard_map/pallas_call | solution.py:287
  230.6 14.0 %shard_map.113 = bf16[256,10752]{1,0:T(8,128)(2,1)} custom-call(bf16[256,512]{1,0:T(8,128)(2,1)} %get-tuple-element.58.hidden_b_ref, bf16[256,512]{1,0:T(8,128)(2,1)} %get-tuple-element.59.hidden_c_ref, bf16[512,7168]{1,0:T(8,128)(2,1)} %get-tuple-element.53.dn_ref.dn_second_ref, bf16[512,7168]{1,0:T(8,128)(2,1)} %get-tuple-element.53.dn_ref.dn_second_ref), custom_call_target="tpu_custom_call" | custom-call | tf_op jit(solution)/shard_map/pallas_call | solution.py:322
  244.6 8.0 %all-to-all-start.3 = ((bf16[32,8,10752]{2,1,0:T(8,128)(2,1)}), bf16[32,8,10752]{2,1,0:T(8,128)(2,1)}, u32[]{:S(2)}, u32[]{:S(2)}) async-start(bf16[32,8,10752]{2,1,0:T(8,128)(2,1)} %bitcast.152), calls=%async_computation.3 | async-start | bytes 11010048 | tf_op jit(solution)/shard_map/all_to_all | solution.py:397
  252.7 3.9 %add_convert_fusion.1 = bf16[768,1792]{1,0:T(8,128)(2,1)S(1)} fusion(bf16[384,1792]{1,0:T(8,128)(2,1)} %collective-permute-done.9, bf16[512,7168]{1,0:T(8,128)(2,1)} %get-tuple-element.53.dn_ref.dn_second_ref, bf16[384,512]{1,0:T(8,128)(2,1)} %copy-done.5, bf16[384,512]{1,0:T(8,128)(2,1)} %copy-done.3), kind=kOutput, calls=%fused_computation.4 | convolution fusion | flops 1414987776 | bytes 6750208 | tf_op jit(solution)/shard_map/dot_general | solution.py:238
  256.7 3.0 add_convert_fusion.2
  259.7 3.3 collective-permute-start.8
  264.6 55.0 %collective-permute-done.10 = bf16[768,1792]{1,0:T(8,128)(2,1)S(1)} collective-permute-done((bf16[768,1792]{1,0:T(8,128)(2,1)S(1)}, bf16[768,1792]{1,0:T(8,128)(2,1)S(1)}, u32[]{:S(2)}, u32[]{:S(2)}) %collective-permute-start.10) | collective-permute-done | bytes 2752544 | tf_op jit(solution)/shard_map/ppermute | solution.py:394
  324.6 7.3 %all-to-all-start.4 = ((bf16[32,24,1792]{2,1,0:T(8,128)(2,1)}), bf16[32,24,1792]{2,1,0:T(8,128)(2,1)S(1)}, u32[]{:S(2)}, u32[]{:S(2)}) async-start(bf16[32,24,1792]{2,1,0:T(8,128)(2,1)} %bitcast.48), calls=%async_computation.4 | async-start | bytes 5505024 | tf_op jit(solution)/shard_map/all_to_all | solution.py:397
  331.8 8.5 %shard_map.114 = bf16[4,128,1792]{2,1,0:T(8,128)(2,1)} custom-call(bf16[256,256]{1,0:T(8,128)(2,1)} %pad_maximum_fusion.8.share_b_ref, bf16[512,256]{1,0:T(8,128)(2,1)} %pad_maximum_fusion.4.share_c_ref, bf16[256,10752]{1,0:T(8,128)(2,1)} %bitcast.43.rows_ref.folded_ref, bf16[256,10752]{1,0:T(8,128)(2,1)} %bitcast.43.rows_ref.folded_ref), custom_call_target="tpu_custom_call" | custom-call | tf_op jit(solution)/shard_map/pallas_call | solution.py:349
  342.7 2.7 collective-permute-start.13
  348.7 20.6 %all-to-all-done.4 = bf16[32,24,1792]{2,1,0:T(8,128)(2,1)S(1)} async-done(((bf16[32,24,1792]{2,1,0:T(8,128)(2,1)}), bf16[32,24,1792]{2,1,0:T(8,128)(2,1)S(1)}, u32[]{:S(2)}, u32[]{:S(2)}) %all-to-all-start.4) | async-done | bytes 2752544 | tf_op jit(solution)/shard_map/all_to_all | solution.py:397
  (123 shorter events, 48.6 us)
Async XLA Ops:
  4.7 8.7 %copy-start.2 = (bf16[128,1792]{1,0:T(8,128)(2,1)S(1)}, bf16[128,1792]{1,0:T(8,128)(2,1)}, u32[]{:S(2)}) copy-start(bf16[128,1792]{1,0:T(8,128)(2,1)} %param.11) | copy-start | bytes 1376260
  4.7 14.0 %copy-start.8 = (s32[128,8]{0,1:T(8,128)S(1)}, s32[128,8]{0,1:T(8,128)}, u32[]{:S(2)}) copy-start(s32[128,8]{0,1:T(8,128)} %param.12) | copy-start | bytes 12292
  4.7 14.0 %copy-start.9 = (f32[128,8]{0,1:T(8,128)S(1)}, f32[128,8]{0,1:T(8,128)}, u32[]{:S(2)}) copy-start(f32[128,8]{0,1:T(8,128)} %param.13) | copy-start | bytes 12292
  4.7 14.8 %copy-start.1 = (bf16[64,16384]{1,0:T(8,128)(2,1)S(1)}, bf16[64,16384]{1,0:T(8,128)(2,1)}, u32[]{:S(2)}) copy-start(bf16[64,16384]{1,0:T(8,128)(2,1)} %param.17) | copy-start | bytes 6291460
  4.7 46.1 %all-to-all-start = ((bf16[32,24,1792]{2,1,0:T(8,128)(2,1)}), bf16[32,24,1792]{2,1,0:T(8,128)(2,1)}, u32[]{:S(2)}, u32[]{:S(2)}) async-start(bf16[32,24,1792]{2,1,0:T(8,128)(2,1)} %bitcast.7), calls=%async_computation | async-start | bytes 5505024 | tf_op jit(solution)/shard_map/all_to_all | solution.py:397
  13.4 8.7 %copy-start.12 = (s32[1,64]{1,0:T(1,128)S(1)}, s32[1,64]{1,0:T(1,128)}, u32[]{:S(2)}) copy-start(s32[1,64]{1,0:T(1,128)} %param.19) | copy-start | bytes 772
  13.4 8.8 %copy-start.10 = (s32[1,64]{1,0:T(1,128)S(1)}, s32[1,64]{1,0:T(1,128)}, u32[]{:S(2)}) copy-start(s32[1,64]{1,0:T(1,128)} %param.18) | copy-start | bytes 772
  13.4 8.7 %copy-start.11 = (s32[1,64]{1,0:T(1,128)S(1)}, s32[1,64]{1,0:T(1,128)}, u32[]{:S(2)}) copy-start(s32[1,64]{1,0:T(1,128)} %param.20) | copy-start | bytes 772
  13.4 15.1 %collective-permute-start.2 = (bf16[128,1792]{1,0:T(8,128)(2,1)S(1)}, bf16[128,1792]{1,0:T(8,128)(2,1)}, u32[]{:S(2)}, u32[]{:S(2)}) collective-permute-start(bf16[128,1792]{1,0:T(8,128)(2,1)S(1)} %copy-done.2), channel_id=1, source_target_pairs={{0,2},{1,3},{2,0},{3,1},{4,6},{5,7},{6,4},{7,5},{8,10},{9,11},{10,... | collective-permute-start | bytes 1376264 | tf_op jit(solution)/shard_map/ppermute | solution.py:394
  16.7 21.3 %collective-permute-start.1 = (bf16[128,1792]{1,0:T(8,128)(2,1)S(1)}, bf16[128,1792]{1,0:T(8,128)(2,1)}, u32[]{:S(2)}, u32[]{:S(2)}) collective-permute-start(bf16[128,1792]{1,0:T(8,128)(2,1)S(1)} %copy-done.2), channel_id=1, source_target_pairs={{0,3},{1,0},{2,1},{3,2},{4,7},{5,4},{6,5},{7,6},{8,11},{9,8},{10,9... | collective-permute-start | bytes 1376264 | tf_op jit(solution)/shard_map/ppermute | solution.py:394
  17.8 20.2 %collective-permute-start = (bf16[128,1792]{1,0:T(8,128)(2,1)S(1)}, bf16[128,1792]{1,0:T(8,128)(2,1)}, u32[]{:S(2)}, u32[]{:S(2)}) collective-permute-start(bf16[128,1792]{1,0:T(8,128)(2,1)S(1)} %copy-done.2), channel_id=1, source_target_pairs={{0,1},{1,2},{2,3},{3,0},{4,5},{5,6},{6,7},{7,4},{8,9},{9,10},{10,1... | collective-permute-start | bytes 1376264 | tf_op jit(solution)/shard_map/ppermute | solution.py:394
  50.9 63.2 %all-to-all-start.1 = ((bf16[128,144,128]{2,1,0:T(8,128)(2,1)}), bf16[128,144,128]{2,1,0:T(8,128)(2,1)}, u32[]{:S(2)}, u32[]{:S(2)}) async-start(bf16[128,144,128]{2,1,0:T(8,128)(2,1)} %shard_map.110), calls=%async_computation.1 | async-start | bytes 9437184 | tf_op jit(solution)/shard_map/all_to_all | solution.py:397
  80.5 88.0 %collective-permute-start.3 = (bf16[768,1792]{1,0:T(8,128)(2,1)}, bf16[768,1792]{1,0:T(8,128)(2,1)}, u32[]{:S(2)}, u32[]{:S(2)}) collective-permute-start(bf16[768,1792]{1,0:T(8,128)(2,1)} %bitcast.8), channel_id=1, source_target_pairs={{0,1},{1,2},{2,3},{3,0},{4,5},{5,6},{6,7},{7,4},{8,9},{9,10},{10,1... | collective-permute-start | bytes 8257544 | tf_op jit(solution)/shard_map/ppermute | solution.py:394
  81.5 88.6 %collective-permute-start.4 = (bf16[768,1792]{1,0:T(8,128)(2,1)}, bf16[768,1792]{1,0:T(8,128)(2,1)}, u32[]{:S(2)}, u32[]{:S(2)}) collective-permute-start(bf16[768,1792]{1,0:T(8,128)(2,1)} %bitcast.8), channel_id=1, source_target_pairs={{0,3},{1,0},{2,1},{3,2},{4,7},{5,4},{6,5},{7,6},{8,11},{9,8},{10,9... | collective-permute-start | bytes 8257544 | tf_op jit(solution)/shard_map/ppermute | solution.py:394
  115.7 95.7 %all-to-all-start.2 = ((bf16[32,8,10752]{2,1,0:T(8,128)(2,1)}), bf16[32,8,10752]{2,1,0:T(8,128)(2,1)}, u32[]{:S(2)}, u32[]{:S(2)}) async-start(bf16[32,8,10752]{2,1,0:T(8,128)(2,1)} %bitcast.153), calls=%async_computation.2 | async-start | bytes 11010048 | tf_op jit(solution)/shard_map/all_to_all | solution.py:397
  140.0 34.8 %copy-start = (bf16[7168,1024]{1,0:T(8,128)(2,1)S(1)}, bf16[7168,1024]{1,0:T(8,128)(2,1)}, u32[]{:S(2)}) copy-start(bf16[7168,1024]{1,0:T(8,128)(2,1)} %get-tuple-element.49.gu_ref) | copy-start | bytes 44040196
  170.0 33.0 %collective-permute-start.5 = (bf16[384,1792]{1,0:T(8,128)(2,1)S(1)}, bf16[384,1792]{1,0:T(8,128)(2,1)S(1)}, u32[]{:S(2)}, u32[]{:S(2)}) collective-permute-start(bf16[384,1792]{1,0:T(8,128)(2,1)S(1)} %slice.121), channel_id=1, source_target_pairs={{0,1},{1,2},{2,3},{3,0},{4,5},{5,6},{6,7},{7,4},{8,9},{9,10},{10,1... | collective-permute-start | bytes 4128776 | tf_op jit(solution)/shard_map/ppermute | solution.py:394
  171.5 32.2 %collective-permute-start.6 = (bf16[384,1792]{1,0:T(8,128)(2,1)S(1)}, bf16[384,1792]{1,0:T(8,128)(2,1)S(1)}, u32[]{:S(2)}, u32[]{:S(2)}) collective-permute-start(bf16[384,1792]{1,0:T(8,128)(2,1)S(1)} %slice.122), channel_id=1, source_target_pairs={{0,3},{1,0},{2,1},{3,2},{4,7},{5,4},{6,5},{7,6},{8,11},{9,8},{10,9... | collective-permute-start | bytes 4128776 | tf_op jit(solution)/shard_map/ppermute | solution.py:394
  203.8 3.7 slice-start
  211.4 41.3 %collective-permute-start.9 = (bf16[384,1792]{1,0:T(8,128)(2,1)}, bf16[384,1792]{1,0:T(8,128)(2,1)}, u32[]{:S(2)}, u32[]{:S(2)}) collective-permute-start(bf16[384,1792]{1,0:T(8,128)(2,1)} %convolution_convert_fusion.3), channel_id=1, source_target_pairs={{0,1},{1,2},{2,3},{3,0},{4,5},{5,6},{6,7},{7,4},{8,9},{9,10},{10,1... | collective-permute-start | bytes 4128776 | tf_op jit(solution)/shard_map/ppermute | solution.py:394
  211.6 45.1 %collective-permute-start.7 = (bf16[384,1792]{1,0:T(8,128)(2,1)}, bf16[384,1792]{1,0:T(8,128)(2,1)}, u32[]{:S(2)}, u32[]{:S(2)}) collective-permute-start(bf16[384,1792]{1,0:T(8,128)(2,1)} %convolution_convert_fusion.4), channel_id=1, source_target_pairs={{0,3},{1,0},{2,1},{3,2},{4,7},{5,4},{6,5},{7,6},{8,11},{9,8},{10,9... | collective-permute-start | bytes 4128776 | tf_op jit(solution)/shard_map/ppermute | solution.py:394
  244.6 12.0 %slice-start.2 = ((s8[7340032]{0:T(1024)(128)(4,1)}), s8[3145728]{0:T(1024)(128)(4,1)S(1)}, s32[]{:S(2)}) async-start(s8[7340032]{0:T(1024)(128)(4,1)} %bitcast.144), calls=%async_computation.7 | async-start | bytes 6291456
  244.6 79.9 %all-to-all-start.3 = ((bf16[32,8,10752]{2,1,0:T(8,128)(2,1)}), bf16[32,8,10752]{2,1,0:T(8,128)(2,1)}, u32[]{:S(2)}, u32[]{:S(2)}) async-start(bf16[32,8,10752]{2,1,0:T(8,128)(2,1)} %bitcast.152), calls=%async_computation.3 | async-start | bytes 11010048 | tf_op jit(solution)/shard_map/all_to_all | solution.py:397
  252.7 4.0 %slice-start.3 = ((s8[7340032]{0:T(1024)(128)(4,1)}), s8[4194304]{0:T(1024)(128)(4,1)S(1)}, s32[]{:S(2)}) async-start(s8[7340032]{0:T(1024)(128)(4,1)} %bitcast.144), calls=%async_computation.8 | async-start | bytes 8388608
  252.7 4.0 %copy-start.4 = (bf16[384,512]{1,0:T(8,128)(2,1)S(1)}, bf16[384,512]{1,0:T(8,128)(2,1)}, u32[]{:S(2)}) copy-start(bf16[384,512]{1,0:T(8,128)(2,1)} %copy-done.3) | copy-start | bytes 1179652
  252.7 4.0 %copy-start.6 = (bf16[384,512]{1,0:T(8,128)(2,1)S(1)}, bf16[384,512]{1,0:T(8,128)(2,1)}, u32[]{:S(2)}) copy-start(bf16[384,512]{1,0:T(8,128)(2,1)} %copy-done.5) | copy-start | bytes 1179652
  256.6 63.1 %collective-permute-start.10 = (bf16[768,1792]{1,0:T(8,128)(2,1)S(1)}, bf16[768,1792]{1,0:T(8,128)(2,1)S(1)}, u32[]{:S(2)}, u32[]{:S(2)}) collective-permute-start(bf16[768,1792]{1,0:T(8,128)(2,1)S(1)} %add_convert_fusion.1), channel_id=1, source_target_pairs={{0,1},{1,2},{2,3},{3,0},{4,5},{5,6},{6,7},{7,4},{8,9},{9,10},{10,1... | collective-permute-start | bytes 8257544 | tf_op jit(solution)/shard_map/ppermute | solution.py:394
  259.7 62.3 %collective-permute-start.8 = (bf16[768,1792]{1,0:T(8,128)(2,1)S(1)}, bf16[768,1792]{1,0:T(8,128)(2,1)S(1)}, u32[]{:S(2)}, u32[]{:S(2)}) collective-permute-start(bf16[768,1792]{1,0:T(8,128)(2,1)S(1)} %add_convert_fusion.2), channel_id=1, source_target_pairs={{0,3},{1,0},{2,1},{3,2},{4,7},{5,4},{6,5},{7,6},{8,11},{9,8},{10,9... | collective-permute-start | bytes 8257544 | tf_op jit(solution)/shard_map/ppermute | solution.py:394
  324.6 44.7 %all-to-all-start.4 = ((bf16[32,24,1792]{2,1,0:T(8,128)(2,1)}), bf16[32,24,1792]{2,1,0:T(8,128)(2,1)S(1)}, u32[]{:S(2)}, u32[]{:S(2)}) async-start(bf16[32,24,1792]{2,1,0:T(8,128)(2,1)} %bitcast.48), calls=%async_computation.4 | async-start | bytes 5505024 | tf_op jit(solution)/shard_map/all_to_all | solution.py:397
  342.7 27.5 %collective-permute-start.13 = (bf16[128,1792]{1,0:T(8,128)(2,1)}, bf16[128,1792]{1,0:T(8,128)(2,1)}, u32[]{:S(2)}, u32[]{:S(2)}) collective-permute-start(bf16[128,1792]{1,0:T(8,128)(2,1)} %get-tuple-element.74), channel_id=1, source_target_pairs={{0,2},{1,3},{2,0},{3,1},{4,6},{5,7},{6,4},{7,5},{8,10},{9,11},{10,... | collective-permute-start | bytes 1376264 | tf_op jit(solution)/shard_map/ppermute | solution.py:394
  345.5 24.8 %collective-permute-start.12 = (bf16[128,1792]{1,0:T(8,128)(2,1)}, bf16[128,1792]{1,0:T(8,128)(2,1)}, u32[]{:S(2)}, u32[]{:S(2)}) collective-permute-start(bf16[128,1792]{1,0:T(8,128)(2,1)} %get-tuple-element.75), channel_id=1, source_target_pairs={{0,1},{1,2},{2,3},{3,0},{4,5},{5,6},{6,7},{7,4},{8,9},{9,10},{10,1... | collective-permute-start | bytes 1376264 | tf_op jit(solution)/shard_map/ppermute | solution.py:394
  347.3 23.0 %collective-permute-start.11 = (bf16[128,1792]{1,0:T(8,128)(2,1)}, bf16[128,1792]{1,0:T(8,128)(2,1)}, u32[]{:S(2)}, u32[]{:S(2)}) collective-permute-start(bf16[128,1792]{1,0:T(8,128)(2,1)} %get-tuple-element.73), channel_id=1, source_target_pairs={{0,3},{1,0},{2,1},{3,2},{4,7},{5,4},{6,5},{7,6},{8,11},{9,8},{10,9... | collective-permute-start | bytes 1376264 | tf_op jit(solution)/shard_map/ppermute | solution.py:394
  (4 other events, 7.3 us)

commit v2 on v1

--- a/solution.py
+++ b/solution.py
@@ -255,33 +255,37 @@
     return (jax.nn.silu(acc[:, :hid]) * acc[:, hid:]).astype(BF16)
 
 
-def up_kernel(slots, rows_ref, folded_ref, gu_ref, hidden_b_ref, hidden_c_ref, acc_b, acc_c):
+def up_kernel(slots, rows_ref, folded_ref, gu_ref, hidden_b_ref, hidden_c_ref, acc, rows, pick):
     step, steps = pl.program_id(0), pl.num_programs(0)
+    n = rows_ref.shape[0]
 
     @pl.when(step == 0)
     def _():
-        acc_b[...] = jnp.zeros_like(acc_b)
-        acc_c[...] = jnp.zeros_like(acc_c)
-
-    n = rows_ref.shape[0]
-    row = lax.broadcasted_iota(jnp.int32, (n, n), 0)
-    col = lax.broadcasted_iota(jnp.int32, (n, n), 1)
-    same = (row // slots == col // slots) & (row % (slots // 2) == col % (slots // 2))
-    second = (step >= steps // 2).astype(jnp.int32)
-    pick = (same & ((col % slots) // (slots // 2) == second)).astype(BF16)
-    acc_b[...] += dot(rows_ref[...], gu_ref[...])
-    acc_c[...] += dot(dot(pick, folded_ref[...]).astype(BF16), gu_ref[...])
+        acc[...] = jnp.zeros_like(acc)
+
+    @pl.when((step == 0) | (step == steps // 2))
+    def _():
+        row = lax.broadcasted_iota(jnp.int32, (n, n), 0)
+        col = lax.broadcasted_iota(jnp.int32, (n, n), 1)
+        same = (row // slots == col // slots) & (row % (slots // 2) == col % (slots // 2))
+        second = (step >= steps // 2).astype(jnp.int32)
+        here = same & ((col % slots) // (slots // 2) == second)
+        pick[...] = jnp.where(here, 1.0, 0.0).astype(BF16)
+
+    rows[:n] = rows_ref[...]
+    rows[n:] = dot(pick[...], folded_ref[...]).astype(BF16)
+    acc[...] += dot(rows[...], gu_ref[...])
 
     @pl.when(step == steps - 1)
     def _():
-        hidden_b_ref[...] = silu_product(acc_b[...])
-        hidden_c_ref[...] = silu_product(acc_c[...])
+        hidden_b_ref[...] = silu_product(acc[:n])
+        hidden_c_ref[...] = silu_product(acc[n:])
 
 
 def up_projection(slots, rows, gu):
     n = rows.shape[0]
     width, wide = gu.shape
-    steps = 8
+    steps = 4
     step = width // steps
     out = jax.ShapeDtypeStruct((n, wide // 2), BF16)
     return pl.pallas_call(
@@ -294,25 +298,25 @@
             pl.BlockSpec((step, wide), lambda k: (k, 0)),
         ],
         out_specs=[pl.BlockSpec((n, wide // 2), lambda k: (0, 0))] * 2,
-        scratch_shapes=[pltpu.VMEM((n, wide), F32), pltpu.VMEM((n, wide), F32)],
+        scratch_shapes=[
+            pltpu.VMEM((2 * n, wide), F32),
+            pltpu.VMEM((2 * n, step), BF16),
+            pltpu.VMEM((n, n), BF16),
+        ],
         compiler_params=pltpu.CompilerParams(vmem_limit_bytes=VMEM_LIMIT),
         cost_estimate=LIGHT,
     )(rows, rows, gu)
 
 
 def down_kernel(slots, hidden_b_ref, hidden_c_ref, dn_ref, dn_second_ref, out_ref):
-    step = pl.program_id(0)
-
-    @pl.when(step < 8)
-    def _():
-        out_ref[...] = dot(hidden_b_ref[...], dn_ref[...]).astype(BF16)
-
-    @pl.when(step >= 8)
-    def _():
-        first = dot(hidden_c_ref[...], dn_ref[...])
-        second = dot(hidden_c_ref[...], dn_second_ref[...])
-        row = lax.broadcasted_iota(jnp.int32, first.shape, 0)
-        out_ref[...] = jnp.where(row % slots < slots // 2, first, second).astype(BF16)
+    step = dn_ref.shape[1]
+    hidden_c = hidden_c_ref[...]
+    row = lax.broadcasted_iota(jnp.int32, (hidden_c.shape[0], step), 0)
+    out_ref[:, :step] = dot(hidden_b_ref[...], dn_ref[...]).astype(BF16)
+    out_ref[:, step : 2 * step] = dot(hidden_b_ref[...], dn_second_ref[...]).astype(BF16)
+    first, second = dot(hidden_c, dn_ref[...]), dot(hidden_c, dn_second_ref[...])
+    folded = jnp.where(row % slots < slots // 2, first, second)
+    out_ref[:, 2 * step :] = folded.astype(BF16)
 
 
 def down_projection(slots, hidden_b, hidden_c, dn):
@@ -321,15 +325,15 @@
     step = width // 8
     return pl.pallas_call(
         functools.partial(down_kernel, slots),
-        out_shape=jax.ShapeDtypeStruct((n, width + width // 2), BF16),
-        grid=(12,),
+        out_shape=jax.ShapeDtypeStruct((n, 12 * step), BF16),
+        grid=(4,),
         in_specs=[
             pl.BlockSpec((n, hid), lambda k: (0, 0)),
             pl.BlockSpec((n, hid), lambda k: (0, 0)),
-            pl.BlockSpec((hid, step), lambda k: (0, k % 8)),
-            pl.BlockSpec((hid, step), lambda k: (0, 4 + jnp.maximum(k - 8, 0))),
+            pl.BlockSpec((hid, step), lambda k: (0, k)),
+            pl.BlockSpec((hid, step), lambda k: (0, 4 + k)),
         ],
-        out_specs=pl.BlockSpec((n, step), lambda k: (0, k)),
+        out_specs=pl.BlockSpec((n, 3 * step), lambda k: (0, k)),
         compiler_params=pltpu.CompilerParams(vmem_limit_bytes=VMEM_LIMIT),
         cost_estimate=LIGHT,
     )(hidden_b, hidden_c, dn, dn)
@@ -353,8 +357,8 @@
         in_specs=[
             pl.BlockSpec((two, n), lambda k: (0, 0)),
             pl.BlockSpec((two, n), lambda k: (k // 4, 0)),
-            pl.BlockSpec((n, step), lambda k: (0, k)),
-            pl.BlockSpec((n, step), lambda k: (0, 8 + k % 4)),
+            pl.BlockSpec((n, step), lambda k: (0, 3 * (k % 4) + k // 4)),
+            pl.BlockSpec((n, step), lambda k: (0, 3 * (k % 4) + 2)),
         ],
         out_specs=pl.BlockSpec((1, two // 2, step), lambda k: (k // 2, 0, k % 2)),
         compiler_params=pltpu.CompilerParams(vmem_limit_bytes=VMEM_LIMIT),
@@ -397,7 +401,6 @@
         return lax.all_to_all(x, axes, split_axis=0, concat_axis=0, tiled=True)
 
     order = jnp.stack([me, (me + 3) % 4, (me + 1) % 4, (me + 2) % 4]).astype(jnp.int32)
-    place = jnp.zeros((4,), jnp.int32).at[order].set(jnp.arange(4, dtype=jnp.int32))
 
     named = routes[:, :, None] == jnp.arange(n_expert, dtype=jnp.int32)
     member = jnp.any(named, axis=1)
@@ -478,7 +481,9 @@
     is_down = matrix == 2
     wide = jnp.where(is_down, inside % row_blocks, inside // col_blocks)
     narrow = jnp.where(is_down, inside // row_blocks, inside % col_blocks)
-    moved = place[wide // near] * near + wide % near
+    distance = (wide // near - me + n_group) % n_group
+    place = jnp.where(distance == 0, 0, jnp.where(distance == 3, 1, distance + 1))
+    moved = place * near + wide % near
     where = jnp.stack(
         [
             first,

time: 375 us -> 367 us (0.979)
  Pallas kernels: 75.6 us -> 68.2 us
  waiting for transfers between devices: 168 us -> 173 us
    pallas_call x1, Pallas kernels: 14 us -> 8.67 us  [down_projection(): pl.pallas_call(functools.partial(down_kernel, slots), out_shape=jax.Shape...]
  transfers between devices with their start and end apart: 19 -> 19, of which waited for: 10 -> 10; matrix products, arithmetic and copies ran while one was open for 16% -> 15% of each run, Pallas kernels for 20% -> 19%
where the time goes in v2:
time: 367 us; the launch traced here: 365 us
  waiting for transfers between devices  173 us (47%)
  Pallas kernels  68.2 us (19%)
  starting transfers between devices  59.9 us (16%)
  matrix products  37.6 us (10%)
  other arithmetic  15.3 us (4%)
  local copies, waits for them, and re-layouts  10.3 us (3%)
    ppermute x14, waiting for transfers between devices, shift(): return lax.ppermute(x, 'group', ring(n_group, by))  117 us
    all_to_all x5, waiting for transfers between devices, exchange(): return lax.all_to_all(x, axes, split_axis=0, concat_axis=0, tiled=True)  55.5 us
    dot_general x15, matrix products, dot(): return jnp.dot(a, b, preferred_element_type=F32)  37.6 us
    all_to_all x5, starting transfers between devices, exchange(): return lax.all_to_all(x, axes, split_axis=0, concat_axis=0, tiled=True)  34.9 us
    ppermute x14, starting transfers between devices, shift(): return lax.ppermute(x, 'group', ring(n_group, by))  25 us
    pallas_call x1, Pallas kernels, arrange(): pl.pallas_call(arrange_kernel, out_shape=(jax.ShapeDtypeStruct((width, 2...  17.3 us
    pallas_call x1, Pallas kernels, patch(): pl.pallas_call(functools.partial(patch_kernel, factors), out_shape=(jax.S...  15.4 us
    pallas_call x1, Pallas kernels, up_projection(): pl.pallas_call(functools.partial(up_kernel, slots), out_shape=(out, out),...  13.4 us
  transfers between devices with their start and end apart: 19, of which 10 were waited for; matrix products, arithmetic and copies ran while one was open for 15% of the time, Pallas kernels for 19%

profile of v2, /device:TPU:0, one launch (start us, length us, event | category | flops | bytes accessed | tf_op | source)
XLA Modules:
  0.0 365.3 jit_solution(2080763137171030241)
XLA Ops:
  1.2 3.5 convolution_convert_fusion.2
  4.7 8.6 %all-to-all-start = ((bf16[32,24,1792]{2,1,0:T(8,128)(2,1)}), bf16[32,24,1792]{2,1,0:T(8,128)(2,1)}, u32[]{:S(2)}, u32[]{:S(2)}) async-start(bf16[32,24,1792]{2,1,0:T(8,128)(2,1)} %bitcast.7), calls=%async_computation | async-start | bytes 5505024 | tf_op jit(solution)/shard_map/all_to_all | solution.py:401
  13.4 3.3 collective-permute-start.2
  22.4 6.0 %collective-permute-done.2 = bf16[128,1792]{1,0:T(8,128)(2,1)S(1)} collective-permute-done((bf16[128,1792]{1,0:T(8,128)(2,1)S(1)}, bf16[128,1792]{1,0:T(8,128)(2,1)S(1)}, u32[]{:S(2)}, u32[]{:S(2)}) %collective-permute-start.2) | collective-permute-done | bytes 458784 | tf_op jit(solution)/shard_map/ppermute | solution.py:398
  28.4 9.6 %collective-permute-done.1 = bf16[128,1792]{1,0:T(8,128)(2,1)} collective-permute-done((bf16[128,1792]{1,0:T(8,128)(2,1)S(1)}, bf16[128,1792]{1,0:T(8,128)(2,1)}, u32[]{:S(2)}, u32[]{:S(2)}) %collective-permute-start.1) | collective-permute-done | bytes 458784 | tf_op jit(solution)/shard_map/ppermute | solution.py:398
  40.5 4.9 %shard_map.110 = bf16[128,144,128]{2,1,0:T(8,128)(2,1)} custom-call(s32[64]{0:T(128)} %bitcast.146, s32[1]{0:T(128)} %copy.53.count_ref, bf16[64,128,128]{2,1,0:T(8,128)(2,1)} %bitcast.140, bf16[128,16,128]{2,1,0:T(8,128)(2,1)} %broadcast_in_dim.147.meta_ref), custom_call_target="tpu_custom_call" | custom-call | tf_op jit(solution)/shard_map/pallas_call | solution.py:39
  45.4 5.5 %all-to-all-done = bf16[32,24,1792]{2,1,0:T(8,128)(2,1)} async-done(((bf16[32,24,1792]{2,1,0:T(8,128)(2,1)}), bf16[32,24,1792]{2,1,0:T(8,128)(2,1)}, u32[]{:S(2)}, u32[]{:S(2)}) %all-to-all-start) | async-done | bytes 2752544 | tf_op jit(solution)/shard_map/all_to_all | solution.py:401
  50.9 5.9 %all-to-all-start.1 = ((bf16[128,144,128]{2,1,0:T(8,128)(2,1)}), bf16[128,144,128]{2,1,0:T(8,128)(2,1)}, u32[]{:S(2)}, u32[]{:S(2)}) async-start(bf16[128,144,128]{2,1,0:T(8,128)(2,1)} %shard_map.110), calls=%async_computation.1 | async-start | bytes 9437184 | tf_op jit(solution)/shard_map/all_to_all | solution.py:401
  59.4 17.3 %shard_map.109 = (bf16[7168,1024]{1,0:T(8,128)(2,1)}, bf16[512,7168]{1,0:T(8,128)(2,1)}) custom-call(s32[4]{0:T(128)} %pad_add_fusion.order_ref, bf16[7168,512]{1,0:T(8,128)(2,1)} %bitcast.131, bf16[7168,512]{1,0:T(8,128)(2,1)} %bitcast.133, bf16[512,7168]{1,0:T(8,128)(2,1)} %bitcast.135), custom_call_target="tpu_custom_call" | custom-call | tf_op jit(solution)/shard_map/pallas_call | solution.py:75
  81.9 2.7 pad_maximum_fusion
  84.6 29.4 %all-to-all-done.1.incoming_ref = bf16[128,144,128]{2,1,0:T(8,128)(2,1)} async-done(((bf16[128,144,128]{2,1,0:T(8,128)(2,1)}), bf16[128,144,128]{2,1,0:T(8,128)(2,1)}, u32[]{:S(2)}, u32[]{:S(2)}) %all-to-all-start.1) | async-done | bytes 4718624 | tf_op jit(solution)/shard_map/all_to_all | solution.py:401
  115.7 5.0 %all-to-all-start.2 = ((bf16[32,8,10752]{2,1,0:T(8,128)(2,1)}), bf16[32,8,10752]{2,1,0:T(8,128)(2,1)}, u32[]{:S(2)}, u32[]{:S(2)}) async-start(bf16[32,8,10752]{2,1,0:T(8,128)(2,1)} %bitcast.138), calls=%async_computation.2 | async-start | bytes 11010048 | tf_op jit(solution)/shard_map/all_to_all | solution.py:401
  122.1 15.4 %shard_map.111 = (bf16[7168,1024]{1,0:T(8,128)(2,1)}, bf16[512,7168]{1,0:T(8,128)(2,1)}) custom-call(s32[6,128]{1,0:T(8,128)} %stack.41.where_ref, f32[128]{0:T(128)} %fusion.58.scale_ref, bf16[128,144,128]{2,1,0:T(8,128)(2,1)} %all-to-all-done.1.incoming_ref, bf16[7168,512]{1,0:T(8,128)(2,1)} %bitcast.132, ...), custom_call_target="tpu_custom_call", output_to_operand_aliasing={{0}: (6, {}), {1}: (7, {})} | custom-call | tf_op jit(solution)/shard_map/pallas_call | solution.py:211
  137.6 6.0 %fusion.4 = f32[768,1024]{1,0:T(8,128)S(1)} fusion(bf16[768,1792]{1,0:T(8,128)(2,1)} %bitcast.8, bf16[7168,1024]{1,0:T(8,128)(2,1)} %get-tuple-element.49.gu_ref), kind=kOutput, calls=%fused_computation.10 | convolution fusion | flops 2818572288 | bytes 9568256 | tf_op jit(solution)/shard_map/dot_general | solution.py:238
  143.6 25.0 %collective-permute-done.3 = bf16[768,1792]{1,0:T(8,128)(2,1)} collective-permute-done((bf16[768,1792]{1,0:T(8,128)(2,1)}, bf16[768,1792]{1,0:T(8,128)(2,1)}, u32[]{:S(2)}, u32[]{:S(2)}) %collective-permute-start.3) | collective-permute-done | bytes 2752544 | tf_op jit(solution)/shard_map/ppermute | solution.py:398
  171.5 3.3 collective-permute-start.6
  174.8 4.8 %fusion.2 = f32[768,1024]{1,0:T(8,128)S(1)} fusion(bf16[768,1792]{1,0:T(8,128)(2,1)} %collective-permute-done.3, bf16[7168,1024]{1,0:T(8,128)(2,1)S(1)} %copy-done), kind=kOutput, calls=%fused_computation.8 | convolution fusion | flops 2818572288 | bytes 9568256 | tf_op jit(solution)/shard_map/dot_general | solution.py:238
  179.6 4.8 %add_add_fusion = f32[768,1024]{1,0:T(8,128)S(1)} fusion(f32[768,1024]{1,0:T(8,128)S(1)} %fusion.4, f32[768,1024]{1,0:T(8,128)S(1)} %fusion.2, bf16[768,1792]{1,0:T(8,128)(2,1)} %collective-permute-done.4, bf16[7168,1024]{1,0:T(8,128)(2,1)S(1)} %copy-done), kind=kOutput, calls=%fused_computation.17 | convolution fusion | flops 2820145152 | bytes 15859712 | tf_op jit(solution)/shard_map/dot_general | solution.py:238
  184.4 18.6 %collective-permute-done.5 = bf16[384,1792]{1,0:T(8,128)(2,1)S(1)} collective-permute-done((bf16[384,1792]{1,0:T(8,128)(2,1)S(1)}, bf16[384,1792]{1,0:T(8,128)(2,1)S(1)}, u32[]{:S(2)}, u32[]{:S(2)}) %collective-permute-start.5) | collective-permute-done | bytes 1376288 | tf_op jit(solution)/shard_map/ppermute | solution.py:398
  211.6 3.5 collective-permute-start.7
  215.1 13.4 %shard_map.112 = (bf16[256,512]{1,0:T(8,128)(2,1)}, bf16[256,512]{1,0:T(8,128)(2,1)}) custom-call(bf16[256,10752]{1,0:T(8,128)(2,1)} %bitcast.31.rows_ref.folded_ref, bf16[256,10752]{1,0:T(8,128)(2,1)} %bitcast.31.rows_ref.folded_ref, bf16[7168,1024]{1,0:T(8,128)(2,1)} %get-tuple-element.49.gu_ref), custom_call_target="tpu_custom_call" | custom-call | tf_op jit(solution)/shard_map/pallas_call | solution.py:291
  228.5 8.7 %shard_map.113 = bf16[256,10752]{1,0:T(8,128)(2,1)} custom-call(bf16[256,512]{1,0:T(8,128)(2,1)} %get-tuple-element.58.hidden_b_ref, bf16[256,512]{1,0:T(8,128)(2,1)} %get-tuple-element.59.hidden_c_ref, bf16[512,7168]{1,0:T(8,128)(2,1)} %get-tuple-element.53.dn_ref.dn_second_ref, bf16[512,7168]{1,0:T(8,128)(2,1)} %get-tuple-element.53.dn_ref.dn_second_ref), custom_call_target="tpu_custom_call" | custom-call | tf_op jit(solution)/shard_map/pallas_call | solution.py:326
  237.2 8.0 %all-to-all-start.3 = ((bf16[32,8,10752]{2,1,0:T(8,128)(2,1)}), bf16[32,8,10752]{2,1,0:T(8,128)(2,1)}, u32[]{:S(2)}, u32[]{:S(2)}) async-start(bf16[32,8,10752]{2,1,0:T(8,128)(2,1)} %bitcast.137), calls=%async_computation.3 | async-start | bytes 11010048 | tf_op jit(solution)/shard_map/all_to_all | solution.py:401
  245.2 3.9 %add_convert_fusion.1 = bf16[768,1792]{1,0:T(8,128)(2,1)S(1)} fusion(bf16[384,1792]{1,0:T(8,128)(2,1)} %collective-permute-done.9, bf16[512,7168]{1,0:T(8,128)(2,1)} %get-tuple-element.53.dn_ref.dn_second_ref, bf16[384,512]{1,0:T(8,128)(2,1)} %copy-done.5, bf16[384,512]{1,0:T(8,128)(2,1)} %copy-done.3), kind=kOutput, calls=%fused_computation.3 | convolution fusion | flops 1414987776 | bytes 6750208 | tf_op jit(solution)/shard_map/dot_general | solution.py:238
  249.3 3.0 add_convert_fusion.2
  252.3 3.3 collective-permute-start.8
  257.2 55.0 %collective-permute-done.10 = bf16[768,1792]{1,0:T(8,128)(2,1)S(1)} collective-permute-done((bf16[768,1792]{1,0:T(8,128)(2,1)S(1)}, bf16[768,1792]{1,0:T(8,128)(2,1)S(1)}, u32[]{:S(2)}, u32[]{:S(2)}) %collective-permute-start.10) | collective-permute-done | bytes 2752544 | tf_op jit(solution)/shard_map/ppermute | solution.py:398
  317.1 7.3 %all-to-all-start.4 = ((bf16[32,24,1792]{2,1,0:T(8,128)(2,1)}), bf16[32,24,1792]{2,1,0:T(8,128)(2,1)S(1)}, u32[]{:S(2)}, u32[]{:S(2)}) async-start(bf16[32,24,1792]{2,1,0:T(8,128)(2,1)} %bitcast.38), calls=%async_computation.4 | async-start | bytes 5505024 | tf_op jit(solution)/shard_map/all_to_all | solution.py:401
  324.4 8.5 %shard_map.114 = bf16[4,128,1792]{2,1,0:T(8,128)(2,1)} custom-call(bf16[256,256]{1,0:T(8,128)(2,1)} %pad_maximum_fusion.8.share_b_ref, bf16[512,256]{1,0:T(8,128)(2,1)} %pad_maximum_fusion.4.share_c_ref, bf16[256,10752]{1,0:T(8,128)(2,1)} %bitcast.33.rows_ref.folded_ref, bf16[256,10752]{1,0:T(8,128)(2,1)} %bitcast.33.rows_ref.folded_ref), custom_call_target="tpu_custom_call" | custom-call | tf_op jit(solution)/shard_map/pallas_call | solution.py:353
  335.3 2.7 collective-permute-start.13
  341.3 20.6 %all-to-all-done.4 = bf16[32,24,1792]{2,1,0:T(8,128)(2,1)S(1)} async-done(((bf16[32,24,1792]{2,1,0:T(8,128)(2,1)}), bf16[32,24,1792]{2,1,0:T(8,128)(2,1)S(1)}, u32[]{:S(2)}, u32[]{:S(2)}) %all-to-all-start.4) | async-done | bytes 2752544 | tf_op jit(solution)/shard_map/all_to_all | solution.py:401
  362.8 2.5 fusion.29
  (117 shorter events, 44.0 us)
Async XLA Ops:
  4.7 8.7 %copy-start.2 = (bf16[128,1792]{1,0:T(8,128)(2,1)S(1)}, bf16[128,1792]{1,0:T(8,128)(2,1)}, u32[]{:S(2)}) copy-start(bf16[128,1792]{1,0:T(8,128)(2,1)} %param.11) | copy-start | bytes 1376260
  4.7 14.0 %copy-start.7 = (s32[128,8]{0,1:T(8,128)S(1)}, s32[128,8]{0,1:T(8,128)}, u32[]{:S(2)}) copy-start(s32[128,8]{0,1:T(8,128)} %param.12) | copy-start | bytes 12292
  4.7 14.0 %copy-start.8 = (f32[128,8]{0,1:T(8,128)S(1)}, f32[128,8]{0,1:T(8,128)}, u32[]{:S(2)}) copy-start(f32[128,8]{0,1:T(8,128)} %param.13) | copy-start | bytes 12292
  4.7 14.7 %copy-start.1 = (bf16[64,16384]{1,0:T(8,128)(2,1)S(1)}, bf16[64,16384]{1,0:T(8,128)(2,1)}, u32[]{:S(2)}) copy-start(bf16[64,16384]{1,0:T(8,128)(2,1)} %param.17) | copy-start | bytes 6291460
  4.7 46.1 %all-to-all-start = ((bf16[32,24,1792]{2,1,0:T(8,128)(2,1)}), bf16[32,24,1792]{2,1,0:T(8,128)(2,1)}, u32[]{:S(2)}, u32[]{:S(2)}) async-start(bf16[32,24,1792]{2,1,0:T(8,128)(2,1)} %bitcast.7), calls=%async_computation | async-start | bytes 5505024 | tf_op jit(solution)/shard_map/all_to_all | solution.py:401
  13.4 8.6 %copy-start.11 = (s32[1,64]{1,0:T(1,128)S(1)}, s32[1,64]{1,0:T(1,128)}, u32[]{:S(2)}) copy-start(s32[1,64]{1,0:T(1,128)} %param.19) | copy-start | bytes 772
  13.4 8.6 %copy-start.9 = (s32[1,64]{1,0:T(1,128)S(1)}, s32[1,64]{1,0:T(1,128)}, u32[]{:S(2)}) copy-start(s32[1,64]{1,0:T(1,128)} %param.18) | copy-start | bytes 772
  13.4 8.6 %copy-start.10 = (s32[1,64]{1,0:T(1,128)S(1)}, s32[1,64]{1,0:T(1,128)}, u32[]{:S(2)}) copy-start(s32[1,64]{1,0:T(1,128)} %param.20) | copy-start | bytes 772
  13.4 15.0 %collective-permute-start.2 = (bf16[128,1792]{1,0:T(8,128)(2,1)S(1)}, bf16[128,1792]{1,0:T(8,128)(2,1)S(1)}, u32[]{:S(2)}, u32[]{:S(2)}) collective-permute-start(bf16[128,1792]{1,0:T(8,128)(2,1)S(1)} %copy-done.2), channel_id=1, source_target_pairs={{0,2},{1,3},{2,0},{3,1},{4,6},{5,7},{6,4},{7,5},{8,10},{9,11},{10,... | collective-permute-start | bytes 1376264 | tf_op jit(solution)/shard_map/ppermute | solution.py:398
  16.7 21.3 %collective-permute-start.1 = (bf16[128,1792]{1,0:T(8,128)(2,1)S(1)}, bf16[128,1792]{1,0:T(8,128)(2,1)}, u32[]{:S(2)}, u32[]{:S(2)}) collective-permute-start(bf16[128,1792]{1,0:T(8,128)(2,1)S(1)} %copy-done.2), channel_id=1, source_target_pairs={{0,3},{1,0},{2,1},{3,2},{4,7},{5,4},{6,5},{7,6},{8,11},{9,8},{10,9... | collective-permute-start | bytes 1376264 | tf_op jit(solution)/shard_map/ppermute | solution.py:398
  17.8 20.2 %collective-permute-start = (bf16[128,1792]{1,0:T(8,128)(2,1)S(1)}, bf16[128,1792]{1,0:T(8,128)(2,1)}, u32[]{:S(2)}, u32[]{:S(2)}) collective-permute-start(bf16[128,1792]{1,0:T(8,128)(2,1)S(1)} %copy-done.2), channel_id=1, source_target_pairs={{0,1},{1,2},{2,3},{3,0},{4,5},{5,6},{6,7},{7,4},{8,9},{9,10},{10,1... | collective-permute-start | bytes 1376264 | tf_op jit(solution)/shard_map/ppermute | solution.py:398
  50.9 63.2 %all-to-all-start.1 = ((bf16[128,144,128]{2,1,0:T(8,128)(2,1)}), bf16[128,144,128]{2,1,0:T(8,128)(2,1)}, u32[]{:S(2)}, u32[]{:S(2)}) async-start(bf16[128,144,128]{2,1,0:T(8,128)(2,1)} %shard_map.110), calls=%async_computation.1 | async-start | bytes 9437184 | tf_op jit(solution)/shard_map/all_to_all | solution.py:401
  78.6 89.9 %collective-permute-start.3 = (bf16[768,1792]{1,0:T(8,128)(2,1)}, bf16[768,1792]{1,0:T(8,128)(2,1)}, u32[]{:S(2)}, u32[]{:S(2)}) collective-permute-start(bf16[768,1792]{1,0:T(8,128)(2,1)} %bitcast.8), channel_id=1, source_target_pairs={{0,1},{1,2},{2,3},{3,0},{4,5},{5,6},{6,7},{7,4},{8,9},{9,10},{10,1... | collective-permute-start | bytes 8257544 | tf_op jit(solution)/shard_map/ppermute | solution.py:398
  79.6 90.5 %collective-permute-start.4 = (bf16[768,1792]{1,0:T(8,128)(2,1)}, bf16[768,1792]{1,0:T(8,128)(2,1)}, u32[]{:S(2)}, u32[]{:S(2)}) collective-permute-start(bf16[768,1792]{1,0:T(8,128)(2,1)} %bitcast.8), channel_id=1, source_target_pairs={{0,3},{1,0},{2,1},{3,2},{4,7},{5,4},{6,5},{7,6},{8,11},{9,8},{10,9... | collective-permute-start | bytes 8257544 | tf_op jit(solution)/shard_map/ppermute | solution.py:398
  115.7 95.7 %all-to-all-start.2 = ((bf16[32,8,10752]{2,1,0:T(8,128)(2,1)}), bf16[32,8,10752]{2,1,0:T(8,128)(2,1)}, u32[]{:S(2)}, u32[]{:S(2)}) async-start(bf16[32,8,10752]{2,1,0:T(8,128)(2,1)} %bitcast.138), calls=%async_computation.2 | async-start | bytes 11010048 | tf_op jit(solution)/shard_map/all_to_all | solution.py:401
  137.6 37.2 %copy-start = (bf16[7168,1024]{1,0:T(8,128)(2,1)S(1)}, bf16[7168,1024]{1,0:T(8,128)(2,1)}, u32[]{:S(2)}) copy-start(bf16[7168,1024]{1,0:T(8,128)(2,1)} %get-tuple-element.49.gu_ref) | copy-start | bytes 44040196
  170.0 33.0 %collective-permute-start.5 = (bf16[384,1792]{1,0:T(8,128)(2,1)S(1)}, bf16[384,1792]{1,0:T(8,128)(2,1)S(1)}, u32[]{:S(2)}, u32[]{:S(2)}) collective-permute-start(bf16[384,1792]{1,0:T(8,128)(2,1)S(1)} %slice.116), channel_id=1, source_target_pairs={{0,1},{1,2},{2,3},{3,0},{4,5},{5,6},{6,7},{7,4},{8,9},{9,10},{10,1... | collective-permute-start | bytes 4128776 | tf_op jit(solution)/shard_map/ppermute | solution.py:398
  171.5 32.2 %collective-permute-start.6 = (bf16[384,1792]{1,0:T(8,128)(2,1)S(1)}, bf16[384,1792]{1,0:T(8,128)(2,1)S(1)}, u32[]{:S(2)}, u32[]{:S(2)}) collective-permute-start(bf16[384,1792]{1,0:T(8,128)(2,1)S(1)} %slice.117), channel_id=1, source_target_pairs={{0,3},{1,0},{2,1},{3,2},{4,7},{5,4},{6,5},{7,6},{8,11},{9,8},{10,9... | collective-permute-start | bytes 4128776 | tf_op jit(solution)/shard_map/ppermute | solution.py:398
  203.8 3.7 %slice-start = ((s8[7340032]{0:T(1024)(128)(4,1)}), s8[4194304]{0:T(1024)(128)(4,1)S(1)}, s32[]{:S(2)}) async-start(s8[7340032]{0:T(1024)(128)(4,1)} %bitcast.127), calls=%async_computation.5 | async-start | bytes 8388608
  211.4 33.8 %collective-permute-start.9 = (bf16[384,1792]{1,0:T(8,128)(2,1)}, bf16[384,1792]{1,0:T(8,128)(2,1)}, u32[]{:S(2)}, u32[]{:S(2)}) collective-permute-start(bf16[384,1792]{1,0:T(8,128)(2,1)} %convolution_convert_fusion.3), channel_id=1, source_target_pairs={{0,1},{1,2},{2,3},{3,0},{4,5},{5,6},{6,7},{7,4},{8,9},{9,10},{10,1... | collective-permute-start | bytes 4128776 | tf_op jit(solution)/shard_map/ppermute | solution.py:398
  211.6 37.6 %collective-permute-start.7 = (bf16[384,1792]{1,0:T(8,128)(2,1)}, bf16[384,1792]{1,0:T(8,128)(2,1)}, u32[]{:S(2)}, u32[]{:S(2)}) collective-permute-start(bf16[384,1792]{1,0:T(8,128)(2,1)} %convolution_convert_fusion.4), channel_id=1, source_target_pairs={{0,3},{1,0},{2,1},{3,2},{4,7},{5,4},{6,5},{7,6},{8,11},{9,8},{10,9... | collective-permute-start | bytes 4128776 | tf_op jit(solution)/shard_map/ppermute | solution.py:398
  237.2 12.0 %slice-start.2 = ((s8[7340032]{0:T(1024)(128)(4,1)}), s8[3145728]{0:T(1024)(128)(4,1)S(1)}, s32[]{:S(2)}) async-start(s8[7340032]{0:T(1024)(128)(4,1)} %bitcast.129), calls=%async_computation.7 | async-start | bytes 6291456
  237.2 79.9 %all-to-all-start.3 = ((bf16[32,8,10752]{2,1,0:T(8,128)(2,1)}), bf16[32,8,10752]{2,1,0:T(8,128)(2,1)}, u32[]{:S(2)}, u32[]{:S(2)}) async-start(bf16[32,8,10752]{2,1,0:T(8,128)(2,1)} %bitcast.137), calls=%async_computation.3 | async-start | bytes 11010048 | tf_op jit(solution)/shard_map/all_to_all | solution.py:401
  245.2 4.0 %slice-start.3 = ((s8[7340032]{0:T(1024)(128)(4,1)}), s8[4194304]{0:T(1024)(128)(4,1)S(1)}, s32[]{:S(2)}) async-start(s8[7340032]{0:T(1024)(128)(4,1)} %bitcast.129), calls=%async_computation.8 | async-start | bytes 8388608
  245.2 4.0 %copy-start.4 = (bf16[384,512]{1,0:T(8,128)(2,1)S(1)}, bf16[384,512]{1,0:T(8,128)(2,1)}, u32[]{:S(2)}) copy-start(bf16[384,512]{1,0:T(8,128)(2,1)} %copy-done.3) | copy-start | bytes 1179652
  245.2 4.0 %copy-start.6 = (bf16[384,512]{1,0:T(8,128)(2,1)S(1)}, bf16[384,512]{1,0:T(8,128)(2,1)}, u32[]{:S(2)}) copy-start(bf16[384,512]{1,0:T(8,128)(2,1)} %copy-done.5) | copy-start | bytes 1179652
  249.1 63.1 %collective-permute-start.10 = (bf16[768,1792]{1,0:T(8,128)(2,1)S(1)}, bf16[768,1792]{1,0:T(8,128)(2,1)S(1)}, u32[]{:S(2)}, u32[]{:S(2)}) collective-permute-start(bf16[768,1792]{1,0:T(8,128)(2,1)S(1)} %add_convert_fusion.1), channel_id=1, source_target_pairs={{0,1},{1,2},{2,3},{3,0},{4,5},{5,6},{6,7},{7,4},{8,9},{9,10},{10,1... | collective-permute-start | bytes 8257544 | tf_op jit(solution)/shard_map/ppermute | solution.py:398
  252.3 62.3 %collective-permute-start.8 = (bf16[768,1792]{1,0:T(8,128)(2,1)S(1)}, bf16[768,1792]{1,0:T(8,128)(2,1)S(1)}, u32[]{:S(2)}, u32[]{:S(2)}) collective-permute-start(bf16[768,1792]{1,0:T(8,128)(2,1)S(1)} %add_convert_fusion.2), channel_id=1, source_target_pairs={{0,3},{1,0},{2,1},{3,2},{4,7},{5,4},{6,5},{7,6},{8,11},{9,8},{10,9... | collective-permute-start | bytes 8257544 | tf_op jit(solution)/shard_map/ppermute | solution.py:398
  317.1 44.7 %all-to-all-start.4 = ((bf16[32,24,1792]{2,1,0:T(8,128)(2,1)}), bf16[32,24,1792]{2,1,0:T(8,128)(2,1)S(1)}, u32[]{:S(2)}, u32[]{:S(2)}) async-start(bf16[32,24,1792]{2,1,0:T(8,128)(2,1)} %bitcast.38), calls=%async_computation.4 | async-start | bytes 5505024 | tf_op jit(solution)/shard_map/all_to_all | solution.py:401
  335.3 27.5 %collective-permute-start.13 = (bf16[128,1792]{1,0:T(8,128)(2,1)}, bf16[128,1792]{1,0:T(8,128)(2,1)}, u32[]{:S(2)}, u32[]{:S(2)}) collective-permute-start(bf16[128,1792]{1,0:T(8,128)(2,1)} %get-tuple-element.74), channel_id=1, source_target_pairs={{0,2},{1,3},{2,0},{3,1},{4,6},{5,7},{6,4},{7,5},{8,10},{9,11},{10,... | collective-permute-start | bytes 1376264 | tf_op jit(solution)/shard_map/ppermute | solution.py:398
  338.0 24.7 %collective-permute-start.12 = (bf16[128,1792]{1,0:T(8,128)(2,1)}, bf16[128,1792]{1,0:T(8,128)(2,1)}, u32[]{:S(2)}, u32[]{:S(2)}) collective-permute-start(bf16[128,1792]{1,0:T(8,128)(2,1)} %get-tuple-element.75), channel_id=1, source_target_pairs={{0,1},{1,2},{2,3},{3,0},{4,5},{5,6},{6,7},{7,4},{8,9},{9,10},{10,1... | collective-permute-start | bytes 1376264 | tf_op jit(solution)/shard_map/ppermute | solution.py:398
  339.8 22.9 %collective-permute-start.11 = (bf16[128,1792]{1,0:T(8,128)(2,1)}, bf16[128,1792]{1,0:T(8,128)(2,1)}, u32[]{:S(2)}, u32[]{:S(2)}) collective-permute-start(bf16[128,1792]{1,0:T(8,128)(2,1)} %get-tuple-element.73), channel_id=1, source_target_pairs={{0,3},{1,0},{2,1},{3,2},{4,7},{5,4},{6,5},{7,6},{8,11},{9,8},{10,9... | collective-permute-start | bytes 1376264 | tf_op jit(solution)/shard_map/ppermute | solution.py:398
  (3 other events, 6.4 us)

commit v3 on v2

--- a/solution.py
+++ b/solution.py
@@ -8,7 +8,7 @@
 from jax.sharding import PartitionSpec as P
 
 BLOCK = 128
-META = 16
+META = 8
 SLOTS_A = 24
 SLOTS_B = 8
 SLOTS_C = 4

time: 367 us -> 365 us (level)
  waiting for transfers between devices: 173 us -> 169 us
    all_to_all x5, waiting for transfers between devices: 55.5 us -> 51.6 us  [exchange(): return lax.all_to_all(x, axes, split_axis=0, concat_axis=0, tiled=True)]
where the time goes in v3:
time: 365 us; the launch traced here: 363 us
  waiting for transfers between devices  169 us (46%)
  Pallas kernels  68.2 us (19%)
  starting transfers between devices  59.9 us (16%)
  matrix products  37.6 us (10%)
  other arithmetic  15.9 us (4%)
  local copies, waits for them, and re-layouts  10.6 us (3%)
    ppermute x14, waiting for transfers between devices, shift(): return lax.ppermute(x, 'group', ring(n_group, by))  118 us
    all_to_all x5, waiting for transfers between devices, exchange(): return lax.all_to_all(x, axes, split_axis=0, concat_axis=0, tiled=True)  51.6 us
    dot_general x15, matrix products, dot(): return jnp.dot(a, b, preferred_element_type=F32)  37.6 us
    all_to_all x5, starting transfers between devices, exchange(): return lax.all_to_all(x, axes, split_axis=0, concat_axis=0, tiled=True)  34.8 us
    ppermute x14, starting transfers between devices, shift(): return lax.ppermute(x, 'group', ring(n_group, by))  25.1 us
    pallas_call x1, Pallas kernels, arrange(): pl.pallas_call(arrange_kernel, out_shape=(jax.ShapeDtypeStruct((width, 2...  17.3 us
    pallas_call x1, Pallas kernels, patch(): pl.pallas_call(functools.partial(patch_kernel, factors), out_shape=(jax.S...  15.5 us
    pallas_call x1, Pallas kernels, up_projection(): pl.pallas_call(functools.partial(up_kernel, slots), out_shape=(out, out),...  13.4 us
  transfers between devices with their start and end apart: 19, of which 10 were waited for; matrix products, arithmetic and copies ran while one was open for 15% of the time, Pallas kernels for 19%

profile of v3, /device:TPU:0, one launch (start us, length us, event | category | flops | bytes accessed | tf_op | source)
XLA Modules:
  0.0 362.6 jit_solution(937662794157578548)
XLA Ops:
  1.2 3.5 convolution_convert_fusion.2
  4.7 8.6 %all-to-all-start = ((bf16[32,24,1792]{2,1,0:T(8,128)(2,1)}), bf16[32,24,1792]{2,1,0:T(8,128)(2,1)}, u32[]{:S(2)}, u32[]{:S(2)}) async-start(bf16[32,24,1792]{2,1,0:T(8,128)(2,1)} %bitcast.7), calls=%async_computation | async-start | bytes 5505024 | tf_op jit(solution)/shard_map/all_to_all | solution.py:401
  13.4 3.3 collective-permute-start.2
  22.4 6.0 %collective-permute-done.2 = bf16[128,1792]{1,0:T(8,128)(2,1)} collective-permute-done((bf16[128,1792]{1,0:T(8,128)(2,1)S(1)}, bf16[128,1792]{1,0:T(8,128)(2,1)}, u32[]{:S(2)}, u32[]{:S(2)}) %collective-permute-start.2) | collective-permute-done | bytes 458784 | tf_op jit(solution)/shard_map/ppermute | solution.py:398
  28.5 9.4 %collective-permute-done.1 = bf16[128,1792]{1,0:T(8,128)(2,1)} collective-permute-done((bf16[128,1792]{1,0:T(8,128)(2,1)S(1)}, bf16[128,1792]{1,0:T(8,128)(2,1)}, u32[]{:S(2)}, u32[]{:S(2)}) %collective-permute-start.1) | collective-permute-done | bytes 458784 | tf_op jit(solution)/shard_map/ppermute | solution.py:398
  40.3 4.8 %shard_map.110 = bf16[128,136,128]{2,1,0:T(8,128)(2,1)} custom-call(s32[64]{0:T(128)} %bitcast.146, s32[1]{0:T(128)} %copy.53.count_ref, bf16[64,128,128]{2,1,0:T(8,128)(2,1)} %bitcast.140, bf16[128,8,128]{2,1,0:T(8,128)(2,1)} %broadcast_in_dim.147.meta_ref), custom_call_target="tpu_custom_call" | custom-call | tf_op jit(solution)/shard_map/pallas_call | solution.py:39
  45.1 5.7 %all-to-all-done = bf16[32,24,1792]{2,1,0:T(8,128)(2,1)} async-done(((bf16[32,24,1792]{2,1,0:T(8,128)(2,1)}), bf16[32,24,1792]{2,1,0:T(8,128)(2,1)}, u32[]{:S(2)}, u32[]{:S(2)}) %all-to-all-start) | async-done | bytes 2752544 | tf_op jit(solution)/shard_map/all_to_all | solution.py:401
  50.8 5.9 %all-to-all-start.1 = ((bf16[128,136,128]{2,1,0:T(8,128)(2,1)}), bf16[128,136,128]{2,1,0:T(8,128)(2,1)}, u32[]{:S(2)}, u32[]{:S(2)}) async-start(bf16[128,136,128]{2,1,0:T(8,128)(2,1)} %shard_map.110), calls=%async_computation.1 | async-start | bytes 8912896 | tf_op jit(solution)/shard_map/all_to_all | solution.py:401
  59.8 17.3 %shard_map.109 = (bf16[7168,1024]{1,0:T(8,128)(2,1)}, bf16[512,7168]{1,0:T(8,128)(2,1)}) custom-call(s32[4]{0:T(128)} %pad_add_fusion.order_ref, bf16[7168,512]{1,0:T(8,128)(2,1)} %bitcast.131, bf16[7168,512]{1,0:T(8,128)(2,1)} %bitcast.133, bf16[512,7168]{1,0:T(8,128)(2,1)} %bitcast.135), custom_call_target="tpu_custom_call" | custom-call | tf_op jit(solution)/shard_map/pallas_call | solution.py:75
  83.1 2.7 pad_maximum_fusion
  85.8 25.3 %all-to-all-done.1.incoming_ref = bf16[128,136,128]{2,1,0:T(8,128)(2,1)} async-done(((bf16[128,136,128]{2,1,0:T(8,128)(2,1)}), bf16[128,136,128]{2,1,0:T(8,128)(2,1)}, u32[]{:S(2)}, u32[]{:S(2)}) %all-to-all-start.1) | async-done | bytes 4456480 | tf_op jit(solution)/shard_map/all_to_all | solution.py:401
  112.4 4.9 %all-to-all-start.2 = ((bf16[32,8,10752]{2,1,0:T(8,128)(2,1)}), bf16[32,8,10752]{2,1,0:T(8,128)(2,1)}, u32[]{:S(2)}, u32[]{:S(2)}) async-start(bf16[32,8,10752]{2,1,0:T(8,128)(2,1)} %bitcast.138), calls=%async_computation.2 | async-start | bytes 11010048 | tf_op jit(solution)/shard_map/all_to_all | solution.py:401
  118.7 15.5 %shard_map.111 = (bf16[7168,1024]{1,0:T(8,128)(2,1)}, bf16[512,7168]{1,0:T(8,128)(2,1)}) custom-call(s32[6,128]{1,0:T(8,128)} %stack.41.where_ref, f32[128]{0:T(128)} %exponential_bitcast_fusion.scale_ref, bf16[128,136,128]{2,1,0:T(8,128)(2,1)} %all-to-all-done.1.incoming_ref, ...), custom_call_target="tpu_custom_call", output_to_operand_aliasing={{0}: (6, {}), {1}: (7, {})} | custom-call | tf_op jit(solution)/shard_map/pallas_call | solution.py:211
  134.2 6.0 %fusion.4 = f32[768,1024]{1,0:T(8,128)S(1)} fusion(bf16[768,1792]{1,0:T(8,128)(2,1)} %bitcast.8, bf16[7168,1024]{1,0:T(8,128)(2,1)} %get-tuple-element.49.gu_ref), kind=kOutput, calls=%fused_computation.10 | convolution fusion | flops 2818572288 | bytes 9568256 | tf_op jit(solution)/shard_map/dot_general | solution.py:238
  140.3 25.4 %collective-permute-done.3 = bf16[768,1792]{1,0:T(8,128)(2,1)} collective-permute-done((bf16[768,1792]{1,0:T(8,128)(2,1)}, bf16[768,1792]{1,0:T(8,128)(2,1)}, u32[]{:S(2)}, u32[]{:S(2)}) %collective-permute-start.3) | collective-permute-done | bytes 2752544 | tf_op jit(solution)/shard_map/ppermute | solution.py:398
  168.8 3.3 collective-permute-start.6
  172.1 4.8 %fusion.2 = f32[768,1024]{1,0:T(8,128)S(1)} fusion(bf16[768,1792]{1,0:T(8,128)(2,1)} %collective-permute-done.3, bf16[7168,1024]{1,0:T(8,128)(2,1)S(1)} %copy-done), kind=kOutput, calls=%fused_computation.8 | convolution fusion | flops 2818572288 | bytes 9568256 | tf_op jit(solution)/shard_map/dot_general | solution.py:238
  176.9 4.8 %add_add_fusion = f32[768,1024]{1,0:T(8,128)S(1)} fusion(f32[768,1024]{1,0:T(8,128)S(1)} %fusion.4, f32[768,1024]{1,0:T(8,128)S(1)} %fusion.2, bf16[768,1792]{1,0:T(8,128)(2,1)} %collective-permute-done.4, bf16[7168,1024]{1,0:T(8,128)(2,1)S(1)} %copy-done), kind=kOutput, calls=%fused_computation.17 | convolution fusion | flops 2820145152 | bytes 15859712 | tf_op jit(solution)/shard_map/dot_general | solution.py:238
  181.7 18.6 %collective-permute-done.5 = bf16[384,1792]{1,0:T(8,128)(2,1)S(1)} collective-permute-done((bf16[384,1792]{1,0:T(8,128)(2,1)S(1)}, bf16[384,1792]{1,0:T(8,128)(2,1)S(1)}, u32[]{:S(2)}, u32[]{:S(2)}) %collective-permute-start.5) | collective-permute-done | bytes 1376288 | tf_op jit(solution)/shard_map/ppermute | solution.py:398
  208.9 3.5 collective-permute-start.7
  212.4 13.4 %shard_map.112 = (bf16[256,512]{1,0:T(8,128)(2,1)}, bf16[256,512]{1,0:T(8,128)(2,1)}) custom-call(bf16[256,10752]{1,0:T(8,128)(2,1)} %bitcast.31.rows_ref.folded_ref, bf16[256,10752]{1,0:T(8,128)(2,1)} %bitcast.31.rows_ref.folded_ref, bf16[7168,1024]{1,0:T(8,128)(2,1)} %get-tuple-element.49.gu_ref), custom_call_target="tpu_custom_call" | custom-call | tf_op jit(solution)/shard_map/pallas_call | solution.py:291
  225.8 8.7 %shard_map.113 = bf16[256,10752]{1,0:T(8,128)(2,1)} custom-call(bf16[256,512]{1,0:T(8,128)(2,1)} %get-tuple-element.58.hidden_b_ref, bf16[256,512]{1,0:T(8,128)(2,1)} %get-tuple-element.59.hidden_c_ref, bf16[512,7168]{1,0:T(8,128)(2,1)} %get-tuple-element.53.dn_ref.dn_second_ref, bf16[512,7168]{1,0:T(8,128)(2,1)} %get-tuple-element.53.dn_ref.dn_second_ref), custom_call_target="tpu_custom_call" | custom-call | tf_op jit(solution)/shard_map/pallas_call | solution.py:326
  234.5 8.0 %all-to-all-start.3 = ((bf16[32,8,10752]{2,1,0:T(8,128)(2,1)}), bf16[32,8,10752]{2,1,0:T(8,128)(2,1)}, u32[]{:S(2)}, u32[]{:S(2)}) async-start(bf16[32,8,10752]{2,1,0:T(8,128)(2,1)} %bitcast.137), calls=%async_computation.3 | async-start | bytes 11010048 | tf_op jit(solution)/shard_map/all_to_all | solution.py:401
  242.6 3.9 %add_convert_fusion.1 = bf16[768,1792]{1,0:T(8,128)(2,1)S(1)} fusion(bf16[384,1792]{1,0:T(8,128)(2,1)} %collective-permute-done.9, bf16[512,7168]{1,0:T(8,128)(2,1)} %get-tuple-element.53.dn_ref.dn_second_ref, bf16[384,512]{1,0:T(8,128)(2,1)} %copy-done.5, bf16[384,512]{1,0:T(8,128)(2,1)} %copy-done.3), kind=kOutput, calls=%fused_computation.3 | convolution fusion | flops 1414987776 | bytes 6750208 | tf_op jit(solution)/shard_map/dot_general | solution.py:238
  246.6 3.0 add_convert_fusion.2
  249.6 3.3 collective-permute-start.8
  254.5 55.0 %collective-permute-done.10 = bf16[768,1792]{1,0:T(8,128)(2,1)S(1)} collective-permute-done((bf16[768,1792]{1,0:T(8,128)(2,1)S(1)}, bf16[768,1792]{1,0:T(8,128)(2,1)S(1)}, u32[]{:S(2)}, u32[]{:S(2)}) %collective-permute-start.10) | collective-permute-done | bytes 2752544 | tf_op jit(solution)/shard_map/ppermute | solution.py:398
  314.4 7.3 %all-to-all-start.4 = ((bf16[32,24,1792]{2,1,0:T(8,128)(2,1)}), bf16[32,24,1792]{2,1,0:T(8,128)(2,1)S(1)}, u32[]{:S(2)}, u32[]{:S(2)}) async-start(bf16[32,24,1792]{2,1,0:T(8,128)(2,1)} %bitcast.38), calls=%async_computation.4 | async-start | bytes 5505024 | tf_op jit(solution)/shard_map/all_to_all | solution.py:401
  321.7 8.5 %shard_map.114 = bf16[4,128,1792]{2,1,0:T(8,128)(2,1)} custom-call(bf16[256,256]{1,0:T(8,128)(2,1)} %pad_maximum_fusion.8.share_b_ref, bf16[512,256]{1,0:T(8,128)(2,1)} %pad_maximum_fusion.4.share_c_ref, bf16[256,10752]{1,0:T(8,128)(2,1)} %bitcast.33.rows_ref.folded_ref, bf16[256,10752]{1,0:T(8,128)(2,1)} %bitcast.33.rows_ref.folded_ref), custom_call_target="tpu_custom_call" | custom-call | tf_op jit(solution)/shard_map/pallas_call | solution.py:353
  332.6 2.7 collective-permute-start.13
  338.6 20.6 %all-to-all-done.4 = bf16[32,24,1792]{2,1,0:T(8,128)(2,1)S(1)} async-done(((bf16[32,24,1792]{2,1,0:T(8,128)(2,1)}), bf16[32,24,1792]{2,1,0:T(8,128)(2,1)S(1)}, u32[]{:S(2)}, u32[]{:S(2)}) %all-to-all-start.4) | async-done | bytes 2752544 | tf_op jit(solution)/shard_map/all_to_all | solution.py:401
  360.1 2.5 fusion.29
  (119 shorter events, 45.0 us)
Async XLA Ops:
  4.7 8.7 %copy-start.2 = (bf16[128,1792]{1,0:T(8,128)(2,1)S(1)}, bf16[128,1792]{1,0:T(8,128)(2,1)}, u32[]{:S(2)}) copy-start(bf16[128,1792]{1,0:T(8,128)(2,1)} %param.11) | copy-start | bytes 1376260
  4.7 14.0 %copy-start.8 = (s32[128,8]{0,1:T(8,128)S(1)}, s32[128,8]{0,1:T(8,128)}, u32[]{:S(2)}) copy-start(s32[128,8]{0,1:T(8,128)} %param.12) | copy-start | bytes 12292
  4.7 14.0 %copy-start.9 = (f32[128,8]{0,1:T(8,128)S(1)}, f32[128,8]{0,1:T(8,128)}, u32[]{:S(2)}) copy-start(f32[128,8]{0,1:T(8,128)} %param.13) | copy-start | bytes 12292
  4.7 14.8 %copy-start.1 = (bf16[64,16384]{1,0:T(8,128)(2,1)S(1)}, bf16[64,16384]{1,0:T(8,128)(2,1)}, u32[]{:S(2)}) copy-start(bf16[64,16384]{1,0:T(8,128)(2,1)} %param.17) | copy-start | bytes 6291460
  4.7 46.1 %all-to-all-start = ((bf16[32,24,1792]{2,1,0:T(8,128)(2,1)}), bf16[32,24,1792]{2,1,0:T(8,128)(2,1)}, u32[]{:S(2)}, u32[]{:S(2)}) async-start(bf16[32,24,1792]{2,1,0:T(8,128)(2,1)} %bitcast.7), calls=%async_computation | async-start | bytes 5505024 | tf_op jit(solution)/shard_map/all_to_all | solution.py:401
  13.3 8.7 %copy-start.12 = (s32[1,64]{1,0:T(1,128)S(1)}, s32[1,64]{1,0:T(1,128)}, u32[]{:S(2)}) copy-start(s32[1,64]{1,0:T(1,128)} %param.19) | copy-start | bytes 772
  13.4 8.8 %copy-start.10 = (s32[1,64]{1,0:T(1,128)S(1)}, s32[1,64]{1,0:T(1,128)}, u32[]{:S(2)}) copy-start(s32[1,64]{1,0:T(1,128)} %param.18) | copy-start | bytes 772
  13.4 8.8 %copy-start.11 = (s32[1,64]{1,0:T(1,128)S(1)}, s32[1,64]{1,0:T(1,128)}, u32[]{:S(2)}) copy-start(s32[1,64]{1,0:T(1,128)} %param.20) | copy-start | bytes 772
  13.4 15.1 %collective-permute-start.2 = (bf16[128,1792]{1,0:T(8,128)(2,1)S(1)}, bf16[128,1792]{1,0:T(8,128)(2,1)}, u32[]{:S(2)}, u32[]{:S(2)}) collective-permute-start(bf16[128,1792]{1,0:T(8,128)(2,1)S(1)} %copy-done.2), channel_id=1, source_target_pairs={{0,2},{1,3},{2,0},{3,1},{4,6},{5,7},{6,4},{7,5},{8,10},{9,11},{10,... | collective-permute-start | bytes 1376264 | tf_op jit(solution)/shard_map/ppermute | solution.py:398
  16.6 21.3 %collective-permute-start.1 = (bf16[128,1792]{1,0:T(8,128)(2,1)S(1)}, bf16[128,1792]{1,0:T(8,128)(2,1)}, u32[]{:S(2)}, u32[]{:S(2)}) collective-permute-start(bf16[128,1792]{1,0:T(8,128)(2,1)S(1)} %copy-done.2), channel_id=1, source_target_pairs={{0,3},{1,0},{2,1},{3,2},{4,7},{5,4},{6,5},{7,6},{8,11},{9,8},{10,9... | collective-permute-start | bytes 1376264 | tf_op jit(solution)/shard_map/ppermute | solution.py:398
  17.7 20.2 %collective-permute-start = (bf16[128,1792]{1,0:T(8,128)(2,1)S(1)}, bf16[128,1792]{1,0:T(8,128)(2,1)}, u32[]{:S(2)}, u32[]{:S(2)}) collective-permute-start(bf16[128,1792]{1,0:T(8,128)(2,1)S(1)} %copy-done.2), channel_id=1, source_target_pairs={{0,1},{1,2},{2,3},{3,0},{4,5},{5,6},{6,7},{7,4},{8,9},{9,10},{10,1... | collective-permute-start | bytes 1376264 | tf_op jit(solution)/shard_map/ppermute | solution.py:398
  50.8 60.4 %all-to-all-start.1 = ((bf16[128,136,128]{2,1,0:T(8,128)(2,1)}), bf16[128,136,128]{2,1,0:T(8,128)(2,1)}, u32[]{:S(2)}, u32[]{:S(2)}) async-start(bf16[128,136,128]{2,1,0:T(8,128)(2,1)} %shard_map.110), calls=%async_computation.1 | async-start | bytes 8912896 | tf_op jit(solution)/shard_map/all_to_all | solution.py:401
  79.8 85.9 %collective-permute-start.3 = (bf16[768,1792]{1,0:T(8,128)(2,1)}, bf16[768,1792]{1,0:T(8,128)(2,1)}, u32[]{:S(2)}, u32[]{:S(2)}) collective-permute-start(bf16[768,1792]{1,0:T(8,128)(2,1)} %bitcast.8), channel_id=1, source_target_pairs={{0,1},{1,2},{2,3},{3,0},{4,5},{5,6},{6,7},{7,4},{8,9},{9,10},{10,1... | collective-permute-start | bytes 8257544 | tf_op jit(solution)/shard_map/ppermute | solution.py:398
  80.7 86.7 %collective-permute-start.4 = (bf16[768,1792]{1,0:T(8,128)(2,1)}, bf16[768,1792]{1,0:T(8,128)(2,1)}, u32[]{:S(2)}, u32[]{:S(2)}) collective-permute-start(bf16[768,1792]{1,0:T(8,128)(2,1)} %bitcast.8), channel_id=1, source_target_pairs={{0,3},{1,0},{2,1},{3,2},{4,7},{5,4},{6,5},{7,6},{8,11},{9,8},{10,9... | collective-permute-start | bytes 8257544 | tf_op jit(solution)/shard_map/ppermute | solution.py:398
  112.4 96.4 %all-to-all-start.2 = ((bf16[32,8,10752]{2,1,0:T(8,128)(2,1)}), bf16[32,8,10752]{2,1,0:T(8,128)(2,1)}, u32[]{:S(2)}, u32[]{:S(2)}) async-start(bf16[32,8,10752]{2,1,0:T(8,128)(2,1)} %bitcast.138), calls=%async_computation.2 | async-start | bytes 11010048 | tf_op jit(solution)/shard_map/all_to_all | solution.py:401
  134.2 37.9 %copy-start = (bf16[7168,1024]{1,0:T(8,128)(2,1)S(1)}, bf16[7168,1024]{1,0:T(8,128)(2,1)}, u32[]{:S(2)}) copy-start(bf16[7168,1024]{1,0:T(8,128)(2,1)} %get-tuple-element.49.gu_ref) | copy-start | bytes 44040196
  167.1 33.2 %collective-permute-start.5 = (bf16[384,1792]{1,0:T(8,128)(2,1)S(1)}, bf16[384,1792]{1,0:T(8,128)(2,1)S(1)}, u32[]{:S(2)}, u32[]{:S(2)}) collective-permute-start(bf16[384,1792]{1,0:T(8,128)(2,1)S(1)} %slice.113), channel_id=1, source_target_pairs={{0,1},{1,2},{2,3},{3,0},{4,5},{5,6},{6,7},{7,4},{8,9},{9,10},{10,1... | collective-permute-start | bytes 4128776 | tf_op jit(solution)/shard_map/ppermute | solution.py:398
  168.8 32.2 %collective-permute-start.6 = (bf16[384,1792]{1,0:T(8,128)(2,1)S(1)}, bf16[384,1792]{1,0:T(8,128)(2,1)S(1)}, u32[]{:S(2)}, u32[]{:S(2)}) collective-permute-start(bf16[384,1792]{1,0:T(8,128)(2,1)S(1)} %slice.114), channel_id=1, source_target_pairs={{0,3},{1,0},{2,1},{3,2},{4,7},{5,4},{6,5},{7,6},{8,11},{9,8},{10,9... | collective-permute-start | bytes 4128776 | tf_op jit(solution)/shard_map/ppermute | solution.py:398
  201.1 3.7 %slice-start = ((s8[7340032]{0:T(1024)(128)(4,1)}), s8[4194304]{0:T(1024)(128)(4,1)S(1)}, s32[]{:S(2)}) async-start(s8[7340032]{0:T(1024)(128)(4,1)} %bitcast.127), calls=%async_computation.5 | async-start | bytes 8388608
  208.7 33.8 %collective-permute-start.9 = (bf16[384,1792]{1,0:T(8,128)(2,1)}, bf16[384,1792]{1,0:T(8,128)(2,1)}, u32[]{:S(2)}, u32[]{:S(2)}) collective-permute-start(bf16[384,1792]{1,0:T(8,128)(2,1)} %convolution_convert_fusion.3), channel_id=1, source_target_pairs={{0,1},{1,2},{2,3},{3,0},{4,5},{5,6},{6,7},{7,4},{8,9},{9,10},{10,1... | collective-permute-start | bytes 4128776 | tf_op jit(solution)/shard_map/ppermute | solution.py:398
  208.9 37.6 %collective-permute-start.7 = (bf16[384,1792]{1,0:T(8,128)(2,1)}, bf16[384,1792]{1,0:T(8,128)(2,1)}, u32[]{:S(2)}, u32[]{:S(2)}) collective-permute-start(bf16[384,1792]{1,0:T(8,128)(2,1)} %convolution_convert_fusion.4), channel_id=1, source_target_pairs={{0,3},{1,0},{2,1},{3,2},{4,7},{5,4},{6,5},{7,6},{8,11},{9,8},{10,9... | collective-permute-start | bytes 4128776 | tf_op jit(solution)/shard_map/ppermute | solution.py:398
  234.5 12.0 %slice-start.2 = ((s8[7340032]{0:T(1024)(128)(4,1)}), s8[3145728]{0:T(1024)(128)(4,1)S(1)}, s32[]{:S(2)}) async-start(s8[7340032]{0:T(1024)(128)(4,1)} %bitcast.129), calls=%async_computation.7 | async-start | bytes 6291456
  234.5 79.9 %all-to-all-start.3 = ((bf16[32,8,10752]{2,1,0:T(8,128)(2,1)}), bf16[32,8,10752]{2,1,0:T(8,128)(2,1)}, u32[]{:S(2)}, u32[]{:S(2)}) async-start(bf16[32,8,10752]{2,1,0:T(8,128)(2,1)} %bitcast.137), calls=%async_computation.3 | async-start | bytes 11010048 | tf_op jit(solution)/shard_map/all_to_all | solution.py:401
  242.5 4.0 %slice-start.3 = ((s8[7340032]{0:T(1024)(128)(4,1)}), s8[4194304]{0:T(1024)(128)(4,1)S(1)}, s32[]{:S(2)}) async-start(s8[7340032]{0:T(1024)(128)(4,1)} %bitcast.129), calls=%async_computation.8 | async-start | bytes 8388608
  242.5 4.0 %copy-start.4 = (bf16[384,512]{1,0:T(8,128)(2,1)S(1)}, bf16[384,512]{1,0:T(8,128)(2,1)}, u32[]{:S(2)}) copy-start(bf16[384,512]{1,0:T(8,128)(2,1)} %copy-done.3) | copy-start | bytes 1179652
  242.5 4.0 %copy-start.6 = (bf16[384,512]{1,0:T(8,128)(2,1)S(1)}, bf16[384,512]{1,0:T(8,128)(2,1)}, u32[]{:S(2)}) copy-start(bf16[384,512]{1,0:T(8,128)(2,1)} %copy-done.5) | copy-start | bytes 1179652
  246.4 63.1 %collective-permute-start.10 = (bf16[768,1792]{1,0:T(8,128)(2,1)S(1)}, bf16[768,1792]{1,0:T(8,128)(2,1)S(1)}, u32[]{:S(2)}, u32[]{:S(2)}) collective-permute-start(bf16[768,1792]{1,0:T(8,128)(2,1)S(1)} %add_convert_fusion.1), channel_id=1, source_target_pairs={{0,1},{1,2},{2,3},{3,0},{4,5},{5,6},{6,7},{7,4},{8,9},{9,10},{10,1... | collective-permute-start | bytes 8257544 | tf_op jit(solution)/shard_map/ppermute | solution.py:398
  249.6 62.3 %collective-permute-start.8 = (bf16[768,1792]{1,0:T(8,128)(2,1)S(1)}, bf16[768,1792]{1,0:T(8,128)(2,1)S(1)}, u32[]{:S(2)}, u32[]{:S(2)}) collective-permute-start(bf16[768,1792]{1,0:T(8,128)(2,1)S(1)} %add_convert_fusion.2), channel_id=1, source_target_pairs={{0,3},{1,0},{2,1},{3,2},{4,7},{5,4},{6,5},{7,6},{8,11},{9,8},{10,9... | collective-permute-start | bytes 8257544 | tf_op jit(solution)/shard_map/ppermute | solution.py:398
  314.4 44.7 %all-to-all-start.4 = ((bf16[32,24,1792]{2,1,0:T(8,128)(2,1)}), bf16[32,24,1792]{2,1,0:T(8,128)(2,1)S(1)}, u32[]{:S(2)}, u32[]{:S(2)}) async-start(bf16[32,24,1792]{2,1,0:T(8,128)(2,1)} %bitcast.38), calls=%async_computation.4 | async-start | bytes 5505024 | tf_op jit(solution)/shard_map/all_to_all | solution.py:401
  332.6 27.5 %collective-permute-start.13 = (bf16[128,1792]{1,0:T(8,128)(2,1)}, bf16[128,1792]{1,0:T(8,128)(2,1)}, u32[]{:S(2)}, u32[]{:S(2)}) collective-permute-start(bf16[128,1792]{1,0:T(8,128)(2,1)} %get-tuple-element.74), channel_id=1, source_target_pairs={{0,2},{1,3},{2,0},{3,1},{4,6},{5,7},{6,4},{7,5},{8,10},{9,11},{10,... | collective-permute-start | bytes 1376264 | tf_op jit(solution)/shard_map/ppermute | solution.py:398
  335.3 24.7 %collective-permute-start.12 = (bf16[128,1792]{1,0:T(8,128)(2,1)}, bf16[128,1792]{1,0:T(8,128)(2,1)}, u32[]{:S(2)}, u32[]{:S(2)}) collective-permute-start(bf16[128,1792]{1,0:T(8,128)(2,1)} %get-tuple-element.75), channel_id=1, source_target_pairs={{0,1},{1,2},{2,3},{3,0},{4,5},{5,6},{6,7},{7,4},{8,9},{9,10},{10,1... | collective-permute-start | bytes 1376264 | tf_op jit(solution)/shard_map/ppermute | solution.py:398
  337.1 22.9 %collective-permute-start.11 = (bf16[128,1792]{1,0:T(8,128)(2,1)}, bf16[128,1792]{1,0:T(8,128)(2,1)}, u32[]{:S(2)}, u32[]{:S(2)}) collective-permute-start(bf16[128,1792]{1,0:T(8,128)(2,1)} %get-tuple-element.73), channel_id=1, source_target_pairs={{0,3},{1,0},{2,1},{3,2},{4,7},{5,4},{6,5},{7,6},{8,11},{9,8},{10,9... | collective-permute-start | bytes 1376264 | tf_op jit(solution)/shard_map/ppermute | solution.py:398
  (4 other events, 7.3 us)

commit v4 on v3

--- a/solution.py
+++ b/solution.py
@@ -426,10 +426,6 @@
     pick_a = lax.optimization_barrier(pick(slot_a))
 
     send_a = dot(pick_a, tokens).astype(BF16)
-    send_a, tokens = lax.optimization_barrier((send_a, tokens))
-    tokens_all = jnp.concatenate(
-        [tokens, shift(tokens, 1), shift(tokens, -1), shift(tokens, 2)], axis=1
-    )
     recv_a = exchange(send_a.reshape(n_expert, slots_a, quarter), "expert")
     rows_a = recv_a.reshape(n_expert * slots_a, quarter)
 
@@ -441,8 +437,13 @@
     meta = jnp.pad(meta, ((0, 0), (0, META - 3))).astype(BF16)
     meta = jnp.broadcast_to(meta[:, :, None], (sources, META, BLOCK))
     blocks = delta_values.reshape(listed, BLOCK, BLOCK)
-    blocks, meta, tokens_all = lax.optimization_barrier((blocks, meta, tokens_all))
+    blocks, meta, _ = lax.optimization_barrier((blocks, meta, send_a))
     outgoing = spread_blocks(delta_owner[0], delta_count, blocks, meta)
+    tokens, outgoing = lax.optimization_barrier((tokens, outgoing))
+    tokens_all = jnp.concatenate(
+        [tokens, shift(tokens, 1), shift(tokens, -1), shift(tokens, 2)], axis=1
+    )
+    outgoing, _ = lax.optimization_barrier((outgoing, rows_a))
     incoming = exchange(outgoing, ("expert", "group"))
 
     gu, dn = arrange(order, gate, up, down)
@@ -458,8 +459,9 @@
     send_b = jnp.concatenate([send_b, send_c], axis=1)
 
     rows = n_expert * slots_a // 2
-    after, ahead = shift(rows_a, 1), shift(rows_a, -1)
-    far_top, far_bottom = shift(after[:rows], 1), shift(ahead[rows:], -1)
+    top, bottom = rows_a[:rows], rows_a[rows:]
+    after_top, ahead_bottom = shift(top, 1), shift(bottom, -1)
+    after_bottom, ahead_top = shift(bottom, 1), shift(top, -1)
 
     send_b, incoming = lax.optimization_barrier((send_b, incoming))
     recv_b = exchange(send_b.reshape(n_expert, slots_b, width + half), "expert")
@@ -497,13 +499,22 @@
     factors = (width**-0.5, (hid * n_group) ** -0.5)
     gu, dn = patch(factors, where, scale, incoming, gate, up, down, gu, dn)
 
+    gu, after_top, ahead_bottom = lax.optimization_barrier((gu, after_top, ahead_bottom))
+    far_top, far_bottom = shift(after_top, 1), shift(ahead_bottom, -1)
     acc = dot(rows_a, gu[:quarter])
-    acc = acc + dot(after, gu[quarter : 2 * quarter])
-    acc = acc + dot(ahead, gu[2 * quarter : 3 * quarter])
-    acc, far_top, far_bottom = lax.optimization_barrier((acc, far_top, far_bottom))
+
+    def near_products(acc, after, ahead):
+        acc = acc + dot(after, gu[quarter : 2 * quarter])
+        return acc + dot(ahead, gu[2 * quarter : 3 * quarter])
+
+    acc_top = near_products(acc[:rows], after_top, ahead_top)
+    acc_bottom = near_products(acc[rows:], after_bottom, ahead_bottom)
+    acc_top, acc_bottom, far_top, far_bottom = lax.optimization_barrier(
+        (acc_top, acc_bottom, far_top, far_bottom)
+    )
     last = gu[3 * quarter :]
-    hidden_top = silu_product(acc[:rows] + dot(far_top, last))
-    hidden_bottom = silu_product(acc[rows:] + dot(far_bottom, last))
+    hidden_top = silu_product(acc_top + dot(far_top, last))
+    hidden_bottom = silu_product(acc_bottom + dot(far_bottom, last))
 
     def part(hidden, index):
         return dot(hidden, dn[:, index * quarter : (index + 1) * quarter])
@@ -521,6 +532,7 @@
     none = jnp.zeros_like(top_3)
     part_1 = (part_1 + jnp.concatenate([top_3, none], axis=0).astype(F32)).astype(BF16)
     part_2 = (part_2 + jnp.concatenate([none, bottom_3], axis=0).astype(F32)).astype(BF16)
+    part_1, part_2 = lax.optimization_barrier((part_1, part_2))
     part_1, part_2 = shift(part_1, -1), shift(part_2, 1)
     out_a = part(hidden_a, 0) + part_1.astype(F32) + part_2.astype(F32)
     out_a, back_b = lax.optimization_barrier((out_a.astype(BF16), back_b))

time: 365 us -> 359 us (0.984)
  waiting for transfers between devices: 169 us -> 162 us
  starting transfers between devices: 59.9 us -> 56.2 us
    ppermute x14 -> x16, waiting for transfers between devices: 118 us -> 99.7 us  [shift(): return lax.ppermute(x, 'group', ring(n_group, by))]
    all_to_all x5, waiting for transfers between devices: 51.6 us -> 61.8 us  [exchange(): return lax.all_to_all(x, axes, split_axis=0, concat_axis=0, tiled=True)]
    ppermute x14 -> x16, starting transfers between devices: 25.1 us -> 21.7 us  [shift(): return lax.ppermute(x, 'group', ring(n_group, by))]
    dot_general x15 -> x17, matrix products: 37.6 us -> 39.2 us  [dot(): return jnp.dot(a, b, preferred_element_type=F32)]
  transfers between devices with their start and end apart: 19 -> 21, of which waited for: 10 -> 8; matrix products, arithmetic and copies ran while one was open for 15% -> 18% of each run, Pallas kernels for 19% -> 19%
where the time goes in v4:
time: 359 us; the launch traced here: 358 us
  waiting for transfers between devices  162 us (45%)
  Pallas kernels  68.2 us (19%)
  starting transfers between devices  56.2 us (16%)
  matrix products  39.2 us (11%)
  other arithmetic  19 us (5%)
  local copies, waits for them, and re-layouts  12.4 us (3%)
    ppermute x16, waiting for transfers between devices, shift(): return lax.ppermute(x, 'group', ring(n_group, by))  99.7 us
    all_to_all x5, waiting for transfers between devices, exchange(): return lax.all_to_all(x, axes, split_axis=0, concat_axis=0, tiled=True)  61.8 us
    dot_general x17, matrix products, dot(): return jnp.dot(a, b, preferred_element_type=F32)  39.2 us
    all_to_all x5, starting transfers between devices, exchange(): return lax.all_to_all(x, axes, split_axis=0, concat_axis=0, tiled=True)  34.5 us
    ppermute x16, starting transfers between devices, shift(): return lax.ppermute(x, 'group', ring(n_group, by))  21.7 us
    pallas_call x1, Pallas kernels, arrange(): pl.pallas_call(arrange_kernel, out_shape=(jax.ShapeDtypeStruct((width, 2...  17.2 us
    pallas_call x1, Pallas kernels, patch(): pl.pallas_call(functools.partial(patch_kernel, factors), out_shape=(jax.S...  15.5 us
    pallas_call x1, Pallas kernels, up_projection(): pl.pallas_call(functools.partial(up_kernel, slots), out_shape=(out, out),...  13.4 us
  transfers between devices with their start and end apart: 21, of which 8 were waited for; matrix products, arithmetic and copies ran while one was open for 18% of the time, Pallas kernels for 19%

profile of v4, /device:TPU:0, one launch (start us, length us, event | category | flops | bytes accessed | tf_op | source)
XLA Modules:
  0.0 357.7 jit_solution(17134669990564856913)
XLA Ops:
  1.2 3.4 convolution_convert_fusion.2
  4.6 8.4 %all-to-all-start = ((bf16[32,24,1792]{2,1,0:T(8,128)(2,1)}), bf16[32,24,1792]{2,1,0:T(8,128)(2,1)S(1)}, u32[]{:S(2)}, u32[]{:S(2)}) async-start(bf16[32,24,1792]{2,1,0:T(8,128)(2,1)} %bitcast.144), calls=%async_computation | async-start | bytes 5505024 | tf_op jit(solution)/shard_map/all_to_all | solution.py:401
  14.0 3.5 copy.50
  18.5 4.9 %shard_map.109 = bf16[128,136,128]{2,1,0:T(8,128)(2,1)} custom-call(s32[64]{0:T(128)} %bitcast.152, s32[1]{0:T(128)} %copy.53.count_ref, bf16[64,128,128]{2,1,0:T(8,128)(2,1)} %bitcast.146, bf16[128,8,128]{2,1,0:T(8,128)(2,1)} %broadcast_in_dim.147.meta_ref), custom_call_target="tpu_custom_call" | custom-call | tf_op jit(solution)/shard_map/pallas_call | solution.py:39
  36.0 14.5 %all-to-all-done = bf16[32,24,1792]{2,1,0:T(8,128)(2,1)S(1)} async-done(((bf16[32,24,1792]{2,1,0:T(8,128)(2,1)}), bf16[32,24,1792]{2,1,0:T(8,128)(2,1)S(1)}, u32[]{:S(2)}, u32[]{:S(2)}) %all-to-all-start) | async-done | bytes 2752544 | tf_op jit(solution)/shard_map/all_to_all | solution.py:401
  50.5 5.9 %all-to-all-start.1 = ((bf16[128,136,128]{2,1,0:T(8,128)(2,1)}), bf16[128,136,128]{2,1,0:T(8,128)(2,1)}, u32[]{:S(2)}, u32[]{:S(2)}) async-start(bf16[128,136,128]{2,1,0:T(8,128)(2,1)} %shard_map.109), calls=%async_computation.1 | async-start | bytes 8912896 | tf_op jit(solution)/shard_map/all_to_all | solution.py:401
  57.0 17.2 %shard_map.110 = (bf16[7168,1024]{1,0:T(8,128)(2,1)}, bf16[512,7168]{1,0:T(8,128)(2,1)}) custom-call(s32[4]{0:T(128)} %pad_add_fusion.order_ref, bf16[7168,512]{1,0:T(8,128)(2,1)} %bitcast.135, bf16[7168,512]{1,0:T(8,128)(2,1)} %bitcast.137, bf16[512,7168]{1,0:T(8,128)(2,1)} %bitcast.139), custom_call_target="tpu_custom_call" | custom-call | tf_op jit(solution)/shard_map/pallas_call | solution.py:75
  82.6 2.7 pad_maximum_fusion
  87.4 23.5 %all-to-all-done.1.incoming_ref = bf16[128,136,128]{2,1,0:T(8,128)(2,1)} async-done(((bf16[128,136,128]{2,1,0:T(8,128)(2,1)}), bf16[128,136,128]{2,1,0:T(8,128)(2,1)}, u32[]{:S(2)}, u32[]{:S(2)}) %all-to-all-start.1) | async-done | bytes 4456480 | tf_op jit(solution)/shard_map/all_to_all | solution.py:401
  112.1 4.9 %all-to-all-start.2 = ((bf16[32,8,10752]{2,1,0:T(8,128)(2,1)}), bf16[32,8,10752]{2,1,0:T(8,128)(2,1)}, u32[]{:S(2)}, u32[]{:S(2)}) async-start(bf16[32,8,10752]{2,1,0:T(8,128)(2,1)} %bitcast.142), calls=%async_computation.2 | async-start | bytes 11010048 | tf_op jit(solution)/shard_map/all_to_all | solution.py:401
  118.4 15.5 %shard_map.111 = (bf16[7168,1024]{1,0:T(8,128)(2,1)}, bf16[512,7168]{1,0:T(8,128)(2,1)}) custom-call(s32[6,128]{1,0:T(8,128)} %stack.41.where_ref, f32[128]{0:T(128)} %exponential_bitcast_fusion.scale_ref, bf16[128,136,128]{2,1,0:T(8,128)(2,1)} %all-to-all-done.1.incoming_ref, ...), custom_call_target="tpu_custom_call", output_to_operand_aliasing={{0}: (6, {}), {1}: (7, {})} | custom-call | tf_op jit(solution)/shard_map/pallas_call | solution.py:211
  133.9 2.5 collective-permute-done.3
  136.6 3.0 collective-permute-start.8
  139.6 4.2 %fusion.12 = f32[384,1024]{1,0:T(8,128)S(1)} fusion(bf16[384,1792]{1,0:T(8,128)(2,1)} %collective-permute-done.3, bf16[7168,1024]{1,0:T(8,128)(2,1)} %get-tuple-element.56.gu_ref), kind=kOutput, calls=%fused_computation.19 | convolution fusion | flops 1409286144 | bytes 6619136 | tf_op jit(solution)/shard_map/dot_general | solution.py:238
  143.8 20.8 %collective-permute-done.5 = bf16[384,1792]{1,0:T(8,128)(2,1)} collective-permute-done((bf16[384,1792]{1,0:T(8,128)(2,1)}, bf16[384,1792]{1,0:T(8,128)(2,1)}, u32[]{:S(2)}, u32[]{:S(2)}) %collective-permute-start.5) | collective-permute-done | bytes 1376288 | tf_op jit(solution)/shard_map/ppermute | solution.py:398
  164.6 4.0 %fusion.8 = f32[384,1024]{1,0:T(8,128)S(1)} fusion(bf16[384,1792]{1,0:T(8,128)(2,1)} %collective-permute-done.5, bf16[7168,1024]{1,0:T(8,128)(2,1)} %get-tuple-element.56.gu_ref), kind=kOutput, calls=%fused_computation.15 | convolution fusion | flops 1409286144 | bytes 6619136 | tf_op jit(solution)/shard_map/dot_general | solution.py:238
  168.7 3.0 fusion.10
  171.6 3.0 fusion
  174.7 3.3 fusion.29
  178.0 16.8 %collective-permute-done.7 = bf16[384,1792]{1,0:T(8,128)(2,1)S(1)} collective-permute-done((bf16[384,1792]{1,0:T(8,128)(2,1)}, bf16[384,1792]{1,0:T(8,128)(2,1)S(1)}, u32[]{:S(2)}, u32[]{:S(2)}) %collective-permute-start.7) | collective-permute-done | bytes 1376288 | tf_op jit(solution)/shard_map/ppermute | solution.py:398
  203.7 3.0 collective-permute-start.9
  206.8 13.4 %shard_map.112 = (bf16[256,512]{1,0:T(8,128)(2,1)}, bf16[256,512]{1,0:T(8,128)(2,1)}) custom-call(bf16[256,10752]{1,0:T(8,128)(2,1)} %bitcast.33.rows_ref.folded_ref, bf16[256,10752]{1,0:T(8,128)(2,1)} %bitcast.33.rows_ref.folded_ref, bf16[7168,1024]{1,0:T(8,128)(2,1)} %get-tuple-element.56.gu_ref), custom_call_target="tpu_custom_call" | custom-call | tf_op jit(solution)/shard_map/pallas_call | solution.py:291
  220.2 8.7 %shard_map.113 = bf16[256,10752]{1,0:T(8,128)(2,1)} custom-call(bf16[256,512]{1,0:T(8,128)(2,1)} %get-tuple-element.70.hidden_b_ref, bf16[256,512]{1,0:T(8,128)(2,1)} %get-tuple-element.71.hidden_c_ref, bf16[512,7168]{1,0:T(8,128)(2,1)} %get-tuple-element.63.dn_ref.dn_second_ref, bf16[512,7168]{1,0:T(8,128)(2,1)} %get-tuple-element.63.dn_ref.dn_second_ref), custom_call_target="tpu_custom_call" | custom-call | tf_op jit(solution)/shard_map/pallas_call | solution.py:326
  228.9 8.0 %all-to-all-start.3 = ((bf16[32,8,10752]{2,1,0:T(8,128)(2,1)}), bf16[32,8,10752]{2,1,0:T(8,128)(2,1)}, u32[]{:S(2)}, u32[]{:S(2)}) async-start(bf16[32,8,10752]{2,1,0:T(8,128)(2,1)} %bitcast.141), calls=%async_computation.3 | async-start | bytes 11010048 | tf_op jit(solution)/shard_map/all_to_all | solution.py:401
  236.9 3.8 %add_convert_fusion.1 = bf16[768,1792]{1,0:T(8,128)(2,1)S(1)} fusion(bf16[384,1792]{1,0:T(8,128)(2,1)} %collective-permute-done.10, bf16[512,7168]{1,0:T(8,128)(2,1)} %get-tuple-element.63.dn_ref.dn_second_ref, bf16[384,512]{1,0:T(8,128)(2,1)S(1)} %fusion.36, bf16[384,512]{1,0:T(8,128)(2,1)} %copy-done.3), kind=kOutput, calls=%fused_computation.3 | convolution fusion | flops 1414987776 | bytes 6750208 | tf_op jit(solution)/shard_map/dot_general | solution.py:238
  240.7 3.0 add_convert_fusion.2
  247.4 58.1 %collective-permute-done.11 = bf16[768,1792]{1,0:T(8,128)(2,1)S(1)} collective-permute-done((bf16[768,1792]{1,0:T(8,128)(2,1)S(1)}, bf16[768,1792]{1,0:T(8,128)(2,1)S(1)}, u32[]{:S(2)}, u32[]{:S(2)}) %collective-permute-start.11) | collective-permute-done | bytes 2752544 | tf_op jit(solution)/shard_map/ppermute | solution.py:398
  307.0 2.5 add_convert_fusion
  309.5 7.3 %all-to-all-start.4 = ((bf16[32,24,1792]{2,1,0:T(8,128)(2,1)}), bf16[32,24,1792]{2,1,0:T(8,128)(2,1)S(1)}, u32[]{:S(2)}, u32[]{:S(2)}) async-start(bf16[32,24,1792]{2,1,0:T(8,128)(2,1)} %bitcast.40), calls=%async_computation.4 | async-start | bytes 5505024 | tf_op jit(solution)/shard_map/all_to_all | solution.py:401
  316.8 8.5 %shard_map.114 = bf16[4,128,1792]{2,1,0:T(8,128)(2,1)} custom-call(bf16[256,256]{1,0:T(8,128)(2,1)} %pad_maximum_fusion.8.share_b_ref, bf16[512,256]{1,0:T(8,128)(2,1)} %pad_maximum_fusion.4.share_c_ref, bf16[256,10752]{1,0:T(8,128)(2,1)} %bitcast.35.rows_ref.folded_ref, bf16[256,10752]{1,0:T(8,128)(2,1)} %bitcast.35.rows_ref.folded_ref), custom_call_target="tpu_custom_call" | custom-call | tf_op jit(solution)/shard_map/pallas_call | solution.py:353
  330.4 23.9 %all-to-all-done.4 = bf16[32,24,1792]{2,1,0:T(8,128)(2,1)S(1)} async-done(((bf16[32,24,1792]{2,1,0:T(8,128)(2,1)}), bf16[32,24,1792]{2,1,0:T(8,128)(2,1)S(1)}, u32[]{:S(2)}, u32[]{:S(2)}) %all-to-all-start.4) | async-done | bytes 2752544 | tf_op jit(solution)/shard_map/all_to_all | solution.py:401
  355.2 2.5 fusion.33
  (120 shorter events, 48.8 us)
Async XLA Ops:
  4.6 9.1 %copy-start.9 = (s32[1,64]{1,0:T(1,128)S(1)}, s32[1,64]{1,0:T(1,128)}, u32[]{:S(2)}) copy-start(s32[1,64]{1,0:T(1,128)} %param.19) | copy-start | bytes 772
  4.6 9.1 %copy-start.7 = (s32[1,64]{1,0:T(1,128)S(1)}, s32[1,64]{1,0:T(1,128)}, u32[]{:S(2)}) copy-start(s32[1,64]{1,0:T(1,128)} %param.18) | copy-start | bytes 772
  4.6 9.1 %copy-start.8 = (s32[1,64]{1,0:T(1,128)S(1)}, s32[1,64]{1,0:T(1,128)}, u32[]{:S(2)}) copy-start(s32[1,64]{1,0:T(1,128)} %param.20) | copy-start | bytes 772
  4.6 45.9 %all-to-all-start = ((bf16[32,24,1792]{2,1,0:T(8,128)(2,1)}), bf16[32,24,1792]{2,1,0:T(8,128)(2,1)S(1)}, u32[]{:S(2)}, u32[]{:S(2)}) async-start(bf16[32,24,1792]{2,1,0:T(8,128)(2,1)} %bitcast.144), calls=%async_computation | async-start | bytes 5505024 | tf_op jit(solution)/shard_map/all_to_all | solution.py:401
  18.5 4.9 %copy-start.1 = (bf16[128,1792]{1,0:T(8,128)(2,1)S(1)}, bf16[128,1792]{1,0:T(8,128)(2,1)}, u32[]{:S(2)}) copy-start(bf16[128,1792]{1,0:T(8,128)(2,1)} %param.11) | copy-start | bytes 1376260
  18.5 10.2 %copy-start.5 = (s32[128,8]{0,1:T(8,128)S(1)}, s32[128,8]{0,1:T(8,128)}, u32[]{:S(2)}) copy-start(s32[128,8]{0,1:T(8,128)} %param.12) | copy-start | bytes 12292
  18.5 10.2 %copy-start.6 = (f32[128,8]{0,1:T(8,128)S(1)}, f32[128,8]{0,1:T(8,128)}, u32[]{:S(2)}) copy-start(f32[128,8]{0,1:T(8,128)} %param.13) | copy-start | bytes 12292
  23.4 50.9 %collective-permute-start = (bf16[128,1792]{1,0:T(8,128)(2,1)S(1)}, bf16[128,1792]{1,0:T(8,128)(2,1)}, u32[]{:S(2)}, u32[]{:S(2)}) collective-permute-start(bf16[128,1792]{1,0:T(8,128)(2,1)S(1)} %copy-done.1), channel_id=1, source_target_pairs={{0,1},{1,2},{2,3},{3,0},{4,5},{5,6},{6,7},{7,4},{8,9},{9,10},{10,1... | collective-permute-start | bytes 1376264 | tf_op jit(solution)/shard_map/ppermute | solution.py:398
  25.1 49.2 %collective-permute-start.1 = (bf16[128,1792]{1,0:T(8,128)(2,1)S(1)}, bf16[128,1792]{1,0:T(8,128)(2,1)}, u32[]{:S(2)}, u32[]{:S(2)}) collective-permute-start(bf16[128,1792]{1,0:T(8,128)(2,1)S(1)} %copy-done.1), channel_id=1, source_target_pairs={{0,3},{1,0},{2,1},{3,2},{4,7},{5,4},{6,5},{7,6},{8,11},{9,8},{10,9... | collective-permute-start | bytes 1376264 | tf_op jit(solution)/shard_map/ppermute | solution.py:398
  26.6 47.7 %collective-permute-start.2 = (bf16[128,1792]{1,0:T(8,128)(2,1)S(1)}, bf16[128,1792]{1,0:T(8,128)(2,1)}, u32[]{:S(2)}, u32[]{:S(2)}) collective-permute-start(bf16[128,1792]{1,0:T(8,128)(2,1)S(1)} %copy-done.1), channel_id=1, source_target_pairs={{0,2},{1,3},{2,0},{3,1},{4,6},{5,7},{6,4},{7,5},{8,10},{9,11},{10,... | collective-permute-start | bytes 1376264 | tf_op jit(solution)/shard_map/ppermute | solution.py:398
  50.5 60.4 %all-to-all-start.1 = ((bf16[128,136,128]{2,1,0:T(8,128)(2,1)}), bf16[128,136,128]{2,1,0:T(8,128)(2,1)}, u32[]{:S(2)}, u32[]{:S(2)}) async-start(bf16[128,136,128]{2,1,0:T(8,128)(2,1)} %shard_map.109), calls=%async_computation.1 | async-start | bytes 8912896 | tf_op jit(solution)/shard_map/all_to_all | solution.py:401
  79.4 57.0 %collective-permute-start.3 = (bf16[384,1792]{1,0:T(8,128)(2,1)}, bf16[384,1792]{1,0:T(8,128)(2,1)}, u32[]{:S(2)}, u32[]{:S(2)}) collective-permute-start(bf16[384,1792]{1,0:T(8,128)(2,1)} %bitcast.30), channel_id=1, source_target_pairs={{0,1},{1,2},{2,3},{3,0},{4,5},{5,6},{6,7},{7,4},{8,9},{9,10},{10,1... | collective-permute-start | bytes 4128776 | tf_op jit(solution)/shard_map/ppermute | solution.py:398
  80.3 56.1 %collective-permute-start.4 = (bf16[384,1792]{1,0:T(8,128)(2,1)}, bf16[384,1792]{1,0:T(8,128)(2,1)}, u32[]{:S(2)}, u32[]{:S(2)}) collective-permute-start(bf16[384,1792]{1,0:T(8,128)(2,1)} %bitcast.31), channel_id=1, source_target_pairs={{0,3},{1,0},{2,1},{3,2},{4,7},{5,4},{6,5},{7,6},{8,11},{9,8},{10,9... | collective-permute-start | bytes 4128776 | tf_op jit(solution)/shard_map/ppermute | solution.py:398
  85.3 79.3 %collective-permute-start.5 = (bf16[384,1792]{1,0:T(8,128)(2,1)}, bf16[384,1792]{1,0:T(8,128)(2,1)}, u32[]{:S(2)}, u32[]{:S(2)}) collective-permute-start(bf16[384,1792]{1,0:T(8,128)(2,1)} %bitcast.30), channel_id=1, source_target_pairs={{0,3},{1,0},{2,1},{3,2},{4,7},{5,4},{6,5},{7,6},{8,11},{9,8},{10,9... | collective-permute-start | bytes 4128776 | tf_op jit(solution)/shard_map/ppermute | solution.py:398
  86.3 82.4 %collective-permute-start.6 = (bf16[384,1792]{1,0:T(8,128)(2,1)}, bf16[384,1792]{1,0:T(8,128)(2,1)}, u32[]{:S(2)}, u32[]{:S(2)}) collective-permute-start(bf16[384,1792]{1,0:T(8,128)(2,1)} %bitcast.31), channel_id=1, source_target_pairs={{0,1},{1,2},{2,3},{3,0},{4,5},{5,6},{6,7},{7,4},{8,9},{9,10},{10,1... | collective-permute-start | bytes 4128776 | tf_op jit(solution)/shard_map/ppermute | solution.py:398
  112.1 91.5 %all-to-all-start.2 = ((bf16[32,8,10752]{2,1,0:T(8,128)(2,1)}), bf16[32,8,10752]{2,1,0:T(8,128)(2,1)}, u32[]{:S(2)}, u32[]{:S(2)}) async-start(bf16[32,8,10752]{2,1,0:T(8,128)(2,1)} %bitcast.142), calls=%async_computation.2 | async-start | bytes 11010048 | tf_op jit(solution)/shard_map/all_to_all | solution.py:401
  136.4 58.4 %collective-permute-start.7 = (bf16[384,1792]{1,0:T(8,128)(2,1)}, bf16[384,1792]{1,0:T(8,128)(2,1)S(1)}, u32[]{:S(2)}, u32[]{:S(2)}) collective-permute-start(bf16[384,1792]{1,0:T(8,128)(2,1)} %collective-permute-done.3), channel_id=1, source_target_pairs={{0,1},{1,2},{2,3},{3,0},{4,5},{5,6},{6,7},{7,4},{8,9},{9,10},{10,1... | collective-permute-start | bytes 4128776 | tf_op jit(solution)/shard_map/ppermute | solution.py:398
  136.6 58.2 %collective-permute-start.8 = (bf16[384,1792]{1,0:T(8,128)(2,1)}, bf16[384,1792]{1,0:T(8,128)(2,1)S(1)}, u32[]{:S(2)}, u32[]{:S(2)}) collective-permute-start(bf16[384,1792]{1,0:T(8,128)(2,1)} %collective-permute-done.4), channel_id=1, source_target_pairs={{0,3},{1,0},{2,1},{3,2},{4,7},{5,4},{6,5},{7,6},{8,11},{9,8},{10,9... | collective-permute-start | bytes 4128776 | tf_op jit(solution)/shard_map/ppermute | solution.py:398
  139.6 29.1 %copy-start = (bf16[7168,1024]{1,0:T(8,128)(2,1)S(1)}, bf16[7168,1024]{1,0:T(8,128)(2,1)}, u32[]{:S(2)}) copy-start(bf16[7168,1024]{1,0:T(8,128)(2,1)} %get-tuple-element.56.gu_ref) | copy-start | bytes 44040196
  203.5 33.3 %collective-permute-start.10 = (bf16[384,1792]{1,0:T(8,128)(2,1)}, bf16[384,1792]{1,0:T(8,128)(2,1)}, u32[]{:S(2)}, u32[]{:S(2)}) collective-permute-start(bf16[384,1792]{1,0:T(8,128)(2,1)} %convolution_convert_fusion.3), channel_id=1, source_target_pairs={{0,1},{1,2},{2,3},{3,0},{4,5},{5,6},{6,7},{7,4},{8,9},{9,10},{10,1... | collective-permute-start | bytes 4128776 | tf_op jit(solution)/shard_map/ppermute | solution.py:398
  203.7 36.9 %collective-permute-start.9 = (bf16[384,1792]{1,0:T(8,128)(2,1)}, bf16[384,1792]{1,0:T(8,128)(2,1)}, u32[]{:S(2)}, u32[]{:S(2)}) collective-permute-start(bf16[384,1792]{1,0:T(8,128)(2,1)} %convolution_convert_fusion.4), channel_id=1, source_target_pairs={{0,3},{1,0},{2,1},{3,2},{4,7},{5,4},{6,5},{7,6},{8,11},{9,8},{10,9... | collective-permute-start | bytes 4128776 | tf_op jit(solution)/shard_map/ppermute | solution.py:398
  228.8 11.8 %slice-start.2 = ((s8[7340032]{0:T(1024)(128)(4,1)}), s8[3145728]{0:T(1024)(128)(4,1)S(1)}, s32[]{:S(2)}) async-start(s8[7340032]{0:T(1024)(128)(4,1)} %bitcast.133), calls=%async_computation.7 | async-start | bytes 6291456
  228.9 80.7 %all-to-all-start.3 = ((bf16[32,8,10752]{2,1,0:T(8,128)(2,1)}), bf16[32,8,10752]{2,1,0:T(8,128)(2,1)}, u32[]{:S(2)}, u32[]{:S(2)}) async-start(bf16[32,8,10752]{2,1,0:T(8,128)(2,1)} %bitcast.141), calls=%async_computation.3 | async-start | bytes 11010048 | tf_op jit(solution)/shard_map/all_to_all | solution.py:401
  236.8 3.8 %slice-start.3 = ((s8[7340032]{0:T(1024)(128)(4,1)}), s8[4194304]{0:T(1024)(128)(4,1)S(1)}, s32[]{:S(2)}) async-start(s8[7340032]{0:T(1024)(128)(4,1)} %bitcast.133), calls=%async_computation.8 | async-start | bytes 8388608
  236.9 3.8 %copy-start.4 = (bf16[384,512]{1,0:T(8,128)(2,1)S(1)}, bf16[384,512]{1,0:T(8,128)(2,1)}, u32[]{:S(2)}) copy-start(bf16[384,512]{1,0:T(8,128)(2,1)} %copy-done.3) | copy-start | bytes 1179652
  243.7 61.8 %collective-permute-start.11 = (bf16[768,1792]{1,0:T(8,128)(2,1)S(1)}, bf16[768,1792]{1,0:T(8,128)(2,1)S(1)}, u32[]{:S(2)}, u32[]{:S(2)}) collective-permute-start(bf16[768,1792]{1,0:T(8,128)(2,1)S(1)} %add_convert_fusion.2), channel_id=1, source_target_pairs={{0,3},{1,0},{2,1},{3,2},{4,7},{5,4},{6,5},{7,6},{8,11},{9,8},{10,9... | collective-permute-start | bytes 8257544 | tf_op jit(solution)/shard_map/ppermute | solution.py:398
  244.3 62.7 %collective-permute-start.12 = (bf16[768,1792]{1,0:T(8,128)(2,1)S(1)}, bf16[768,1792]{1,0:T(8,128)(2,1)S(1)}, u32[]{:S(2)}, u32[]{:S(2)}) collective-permute-start(bf16[768,1792]{1,0:T(8,128)(2,1)S(1)} %add_convert_fusion.1), channel_id=1, source_target_pairs={{0,1},{1,2},{2,3},{3,0},{4,5},{5,6},{6,7},{7,4},{8,9},{9,10},{10,1... | collective-permute-start | bytes 8257544 | tf_op jit(solution)/shard_map/ppermute | solution.py:398
  309.5 44.7 %all-to-all-start.4 = ((bf16[32,24,1792]{2,1,0:T(8,128)(2,1)}), bf16[32,24,1792]{2,1,0:T(8,128)(2,1)S(1)}, u32[]{:S(2)}, u32[]{:S(2)}) async-start(bf16[32,24,1792]{2,1,0:T(8,128)(2,1)} %bitcast.40), calls=%async_computation.4 | async-start | bytes 5505024 | tf_op jit(solution)/shard_map/all_to_all | solution.py:401
  325.3 29.0 %copy-start.2 = (bf16[256,768]{0,1:T(8,128)(2,1)S(1)}, bf16[256,768]{0,1:T(8,128)(2,1)}, u32[]{:S(2)}) copy-start(bf16[256,768]{0,1:T(8,128)(2,1)} %pad_maximum_fusion.3) | copy-start | bytes 1179652
  327.7 27.4 %collective-permute-start.13 = (bf16[128,1792]{1,0:T(8,128)(2,1)}, bf16[128,1792]{1,0:T(8,128)(2,1)}, u32[]{:S(2)}, u32[]{:S(2)}) collective-permute-start(bf16[128,1792]{1,0:T(8,128)(2,1)} %get-tuple-element.87), channel_id=1, source_target_pairs={{0,3},{1,0},{2,1},{3,2},{4,7},{5,4},{6,5},{7,6},{8,11},{9,8},{10,9... | collective-permute-start | bytes 1376264 | tf_op jit(solution)/shard_map/ppermute | solution.py:398
  328.0 27.1 %collective-permute-start.14 = (bf16[128,1792]{1,0:T(8,128)(2,1)}, bf16[128,1792]{1,0:T(8,128)(2,1)}, u32[]{:S(2)}, u32[]{:S(2)}) collective-permute-start(bf16[128,1792]{1,0:T(8,128)(2,1)} %get-tuple-element.89), channel_id=1, source_target_pairs={{0,1},{1,2},{2,3},{3,0},{4,5},{5,6},{6,7},{7,4},{8,9},{9,10},{10,1... | collective-permute-start | bytes 1376264 | tf_op jit(solution)/shard_map/ppermute | solution.py:398
  329.8 25.4 %collective-permute-start.15 = (bf16[128,1792]{1,0:T(8,128)(2,1)}, bf16[128,1792]{1,0:T(8,128)(2,1)}, u32[]{:S(2)}, u32[]{:S(2)}) collective-permute-start(bf16[128,1792]{1,0:T(8,128)(2,1)} %get-tuple-element.88), channel_id=1, source_target_pairs={{0,2},{1,3},{2,0},{3,1},{4,6},{5,7},{6,4},{7,5},{8,10},{9,11},{10,... | collective-permute-start | bytes 1376264 | tf_op jit(solution)/shard_map/ppermute | solution.py:398
  (3 other events, 8.2 us)

commit v5 on v4

--- a/solution.py
+++ b/solution.py
@@ -310,12 +310,13 @@
 
 def down_kernel(slots, hidden_b_ref, hidden_c_ref, dn_ref, dn_second_ref, out_ref):
     step = dn_ref.shape[1]
-    hidden_c = hidden_c_ref[...]
-    row = lax.broadcasted_iota(jnp.int32, (hidden_c.shape[0], step), 0)
-    out_ref[:, :step] = dot(hidden_b_ref[...], dn_ref[...]).astype(BF16)
-    out_ref[:, step : 2 * step] = dot(hidden_b_ref[...], dn_second_ref[...]).astype(BF16)
-    first, second = dot(hidden_c, dn_ref[...]), dot(hidden_c, dn_second_ref[...])
-    folded = jnp.where(row % slots < slots // 2, first, second)
+    n = hidden_b_ref.shape[0]
+    hidden = jnp.concatenate([hidden_b_ref[...], hidden_c_ref[...]], axis=0)
+    first, second = dot(hidden, dn_ref[...]), dot(hidden, dn_second_ref[...])
+    out_ref[:, :step] = first[:n].astype(BF16)
+    out_ref[:, step : 2 * step] = second[:n].astype(BF16)
+    row = lax.broadcasted_iota(jnp.int32, (n, step), 0)
+    folded = jnp.where(row % slots < slots // 2, first[n:], second[n:])
     out_ref[:, 2 * step :] = folded.astype(BF16)
 
 

time: 359 us -> 359 us (level)
  no operation moved by 1% of the time
where the time goes in v5:
time: 359 us; the launch traced here: 358 us
  waiting for transfers between devices  162 us (45%)
  Pallas kernels  68.2 us (19%)
  starting transfers between devices  56.1 us (16%)
  matrix products  39.2 us (11%)
  other arithmetic  19 us (5%)
  local copies, waits for them, and re-layouts  12.4 us (3%)
    ppermute x16, waiting for transfers between devices, shift(): return lax.ppermute(x, 'group', ring(n_group, by))  99.7 us
    all_to_all x5, waiting for transfers between devices, exchange(): return lax.all_to_all(x, axes, split_axis=0, concat_axis=0, tiled=True)  61.9 us
    dot_general x17, matrix products, dot(): return jnp.dot(a, b, preferred_element_type=F32)  39.2 us
    all_to_all x5, starting transfers between devices, exchange(): return lax.all_to_all(x, axes, split_axis=0, concat_axis=0, tiled=True)  34.5 us
    ppermute x16, starting transfers between devices, shift(): return lax.ppermute(x, 'group', ring(n_group, by))  21.6 us
    pallas_call x1, Pallas kernels, arrange(): pl.pallas_call(arrange_kernel, out_shape=(jax.ShapeDtypeStruct((width, 2...  17.2 us
    pallas_call x1, Pallas kernels, patch(): pl.pallas_call(functools.partial(patch_kernel, factors), out_shape=(jax.S...  15.5 us
    pallas_call x1, Pallas kernels, up_projection(): pl.pallas_call(functools.partial(up_kernel, slots), out_shape=(out, out),...  13.4 us
  transfers between devices with their start and end apart: 21, of which 8 were waited for; matrix products, arithmetic and copies ran while one was open for 18% of the time, Pallas kernels for 19%

profile of v5, /device:TPU:0, one launch (start us, length us, event | category | flops | bytes accessed | tf_op | source)
XLA Modules:
  0.0 357.7 jit_solution(5861535280672848807)
XLA Ops:
  1.2 3.4 convolution_convert_fusion.2
  4.6 8.4 %all-to-all-start = ((bf16[32,24,1792]{2,1,0:T(8,128)(2,1)}), bf16[32,24,1792]{2,1,0:T(8,128)(2,1)S(1)}, u32[]{:S(2)}, u32[]{:S(2)}) async-start(bf16[32,24,1792]{2,1,0:T(8,128)(2,1)} %bitcast.144), calls=%async_computation | async-start | bytes 5505024 | tf_op jit(solution)/shard_map/all_to_all | solution.py:402
  14.0 3.5 copy.50
  18.5 4.9 %shard_map.109 = bf16[128,136,128]{2,1,0:T(8,128)(2,1)} custom-call(s32[64]{0:T(128)} %bitcast.152, s32[1]{0:T(128)} %copy.53.count_ref, bf16[64,128,128]{2,1,0:T(8,128)(2,1)} %bitcast.146, bf16[128,8,128]{2,1,0:T(8,128)(2,1)} %broadcast_in_dim.147.meta_ref), custom_call_target="tpu_custom_call" | custom-call | tf_op jit(solution)/shard_map/pallas_call | solution.py:39
  36.0 14.5 %all-to-all-done = bf16[32,24,1792]{2,1,0:T(8,128)(2,1)S(1)} async-done(((bf16[32,24,1792]{2,1,0:T(8,128)(2,1)}), bf16[32,24,1792]{2,1,0:T(8,128)(2,1)S(1)}, u32[]{:S(2)}, u32[]{:S(2)}) %all-to-all-start) | async-done | bytes 2752544 | tf_op jit(solution)/shard_map/all_to_all | solution.py:402
  50.5 5.9 %all-to-all-start.1 = ((bf16[128,136,128]{2,1,0:T(8,128)(2,1)}), bf16[128,136,128]{2,1,0:T(8,128)(2,1)}, u32[]{:S(2)}, u32[]{:S(2)}) async-start(bf16[128,136,128]{2,1,0:T(8,128)(2,1)} %shard_map.109), calls=%async_computation.1 | async-start | bytes 8912896 | tf_op jit(solution)/shard_map/all_to_all | solution.py:402
  57.0 17.2 %shard_map.110 = (bf16[7168,1024]{1,0:T(8,128)(2,1)}, bf16[512,7168]{1,0:T(8,128)(2,1)}) custom-call(s32[4]{0:T(128)} %pad_add_fusion.order_ref, bf16[7168,512]{1,0:T(8,128)(2,1)} %bitcast.135, bf16[7168,512]{1,0:T(8,128)(2,1)} %bitcast.137, bf16[512,7168]{1,0:T(8,128)(2,1)} %bitcast.139), custom_call_target="tpu_custom_call" | custom-call | tf_op jit(solution)/shard_map/pallas_call | solution.py:75
  82.6 2.7 pad_maximum_fusion
  87.4 23.5 %all-to-all-done.1.incoming_ref = bf16[128,136,128]{2,1,0:T(8,128)(2,1)} async-done(((bf16[128,136,128]{2,1,0:T(8,128)(2,1)}), bf16[128,136,128]{2,1,0:T(8,128)(2,1)}, u32[]{:S(2)}, u32[]{:S(2)}) %all-to-all-start.1) | async-done | bytes 4456480 | tf_op jit(solution)/shard_map/all_to_all | solution.py:402
  112.1 4.9 %all-to-all-start.2 = ((bf16[32,8,10752]{2,1,0:T(8,128)(2,1)}), bf16[32,8,10752]{2,1,0:T(8,128)(2,1)}, u32[]{:S(2)}, u32[]{:S(2)}) async-start(bf16[32,8,10752]{2,1,0:T(8,128)(2,1)} %bitcast.142), calls=%async_computation.2 | async-start | bytes 11010048 | tf_op jit(solution)/shard_map/all_to_all | solution.py:402
  118.4 15.5 %shard_map.111 = (bf16[7168,1024]{1,0:T(8,128)(2,1)}, bf16[512,7168]{1,0:T(8,128)(2,1)}) custom-call(s32[6,128]{1,0:T(8,128)} %stack.41.where_ref, f32[128]{0:T(128)} %exponential_bitcast_fusion.scale_ref, bf16[128,136,128]{2,1,0:T(8,128)(2,1)} %all-to-all-done.1.incoming_ref, ...), custom_call_target="tpu_custom_call", output_to_operand_aliasing={{0}: (6, {}), {1}: (7, {})} | custom-call | tf_op jit(solution)/shard_map/pallas_call | solution.py:211
  133.8 2.5 collective-permute-done.3
  136.6 3.0 collective-permute-start.8
  139.6 4.2 %fusion.12 = f32[384,1024]{1,0:T(8,128)S(1)} fusion(bf16[384,1792]{1,0:T(8,128)(2,1)} %collective-permute-done.3, bf16[7168,1024]{1,0:T(8,128)(2,1)} %get-tuple-element.56.gu_ref), kind=kOutput, calls=%fused_computation.19 | convolution fusion | flops 1409286144 | bytes 6619136 | tf_op jit(solution)/shard_map/dot_general | solution.py:238
  143.8 20.8 %collective-permute-done.5 = bf16[384,1792]{1,0:T(8,128)(2,1)} collective-permute-done((bf16[384,1792]{1,0:T(8,128)(2,1)}, bf16[384,1792]{1,0:T(8,128)(2,1)}, u32[]{:S(2)}, u32[]{:S(2)}) %collective-permute-start.5) | collective-permute-done | bytes 1376288 | tf_op jit(solution)/shard_map/ppermute | solution.py:399
  164.6 4.0 %fusion.8 = f32[384,1024]{1,0:T(8,128)S(1)} fusion(bf16[384,1792]{1,0:T(8,128)(2,1)} %collective-permute-done.5, bf16[7168,1024]{1,0:T(8,128)(2,1)} %get-tuple-element.56.gu_ref), kind=kOutput, calls=%fused_computation.15 | convolution fusion | flops 1409286144 | bytes 6619136 | tf_op jit(solution)/shard_map/dot_general | solution.py:238
  168.7 3.0 fusion.10
  171.6 3.0 fusion
  174.7 3.3 fusion.29
  178.0 16.8 %collective-permute-done.7 = bf16[384,1792]{1,0:T(8,128)(2,1)S(1)} collective-permute-done((bf16[384,1792]{1,0:T(8,128)(2,1)}, bf16[384,1792]{1,0:T(8,128)(2,1)S(1)}, u32[]{:S(2)}, u32[]{:S(2)}) %collective-permute-start.7) | collective-permute-done | bytes 1376288 | tf_op jit(solution)/shard_map/ppermute | solution.py:399
  203.7 3.0 collective-permute-start.9
  206.8 13.4 %shard_map.112 = (bf16[256,512]{1,0:T(8,128)(2,1)}, bf16[256,512]{1,0:T(8,128)(2,1)}) custom-call(bf16[256,10752]{1,0:T(8,128)(2,1)} %bitcast.33.rows_ref.folded_ref, bf16[256,10752]{1,0:T(8,128)(2,1)} %bitcast.33.rows_ref.folded_ref, bf16[7168,1024]{1,0:T(8,128)(2,1)} %get-tuple-element.56.gu_ref), custom_call_target="tpu_custom_call" | custom-call | tf_op jit(solution)/shard_map/pallas_call | solution.py:291
  220.2 8.7 %shard_map.113 = bf16[256,10752]{1,0:T(8,128)(2,1)} custom-call(bf16[256,512]{1,0:T(8,128)(2,1)} %get-tuple-element.70.hidden_b_ref, bf16[256,512]{1,0:T(8,128)(2,1)} %get-tuple-element.71.hidden_c_ref, bf16[512,7168]{1,0:T(8,128)(2,1)} %get-tuple-element.63.dn_ref.dn_second_ref, bf16[512,7168]{1,0:T(8,128)(2,1)} %get-tuple-element.63.dn_ref.dn_second_ref), custom_call_target="tpu_custom_call" | custom-call | tf_op jit(solution)/shard_map/pallas_call | solution.py:327
  228.8 8.0 %all-to-all-start.3 = ((bf16[32,8,10752]{2,1,0:T(8,128)(2,1)}), bf16[32,8,10752]{2,1,0:T(8,128)(2,1)}, u32[]{:S(2)}, u32[]{:S(2)}) async-start(bf16[32,8,10752]{2,1,0:T(8,128)(2,1)} %bitcast.141), calls=%async_computation.3 | async-start | bytes 11010048 | tf_op jit(solution)/shard_map/all_to_all | solution.py:402
  236.9 3.8 %add_convert_fusion.1 = bf16[768,1792]{1,0:T(8,128)(2,1)S(1)} fusion(bf16[384,1792]{1,0:T(8,128)(2,1)} %collective-permute-done.10, bf16[512,7168]{1,0:T(8,128)(2,1)} %get-tuple-element.63.dn_ref.dn_second_ref, bf16[384,512]{1,0:T(8,128)(2,1)S(1)} %fusion.36, bf16[384,512]{1,0:T(8,128)(2,1)} %copy-done.3), kind=kOutput, calls=%fused_computation.3 | convolution fusion | flops 1414987776 | bytes 6750208 | tf_op jit(solution)/shard_map/dot_general | solution.py:238
  240.7 3.0 add_convert_fusion.2
  247.4 58.1 %collective-permute-done.11 = bf16[768,1792]{1,0:T(8,128)(2,1)S(1)} collective-permute-done((bf16[768,1792]{1,0:T(8,128)(2,1)S(1)}, bf16[768,1792]{1,0:T(8,128)(2,1)S(1)}, u32[]{:S(2)}, u32[]{:S(2)}) %collective-permute-start.11) | collective-permute-done | bytes 2752544 | tf_op jit(solution)/shard_map/ppermute | solution.py:399
  307.0 2.5 add_convert_fusion
  309.5 7.3 %all-to-all-start.4 = ((bf16[32,24,1792]{2,1,0:T(8,128)(2,1)}), bf16[32,24,1792]{2,1,0:T(8,128)(2,1)S(1)}, u32[]{:S(2)}, u32[]{:S(2)}) async-start(bf16[32,24,1792]{2,1,0:T(8,128)(2,1)} %bitcast.40), calls=%async_computation.4 | async-start | bytes 5505024 | tf_op jit(solution)/shard_map/all_to_all | solution.py:402
  316.8 8.5 %shard_map.114 = bf16[4,128,1792]{2,1,0:T(8,128)(2,1)} custom-call(bf16[256,256]{1,0:T(8,128)(2,1)} %pad_maximum_fusion.8.share_b_ref, bf16[512,256]{1,0:T(8,128)(2,1)} %pad_maximum_fusion.4.share_c_ref, bf16[256,10752]{1,0:T(8,128)(2,1)} %bitcast.35.rows_ref.folded_ref, bf16[256,10752]{1,0:T(8,128)(2,1)} %bitcast.35.rows_ref.folded_ref), custom_call_target="tpu_custom_call" | custom-call | tf_op jit(solution)/shard_map/pallas_call | solution.py:354
  330.4 23.9 %all-to-all-done.4 = bf16[32,24,1792]{2,1,0:T(8,128)(2,1)S(1)} async-done(((bf16[32,24,1792]{2,1,0:T(8,128)(2,1)}), bf16[32,24,1792]{2,1,0:T(8,128)(2,1)S(1)}, u32[]{:S(2)}, u32[]{:S(2)}) %all-to-all-start.4) | async-done | bytes 2752544 | tf_op jit(solution)/shard_map/all_to_all | solution.py:402
  355.2 2.5 fusion.33
  (120 shorter events, 48.7 us)
Async XLA Ops:
  4.6 9.1 %copy-start.9 = (s32[1,64]{1,0:T(1,128)S(1)}, s32[1,64]{1,0:T(1,128)}, u32[]{:S(2)}) copy-start(s32[1,64]{1,0:T(1,128)} %param.19) | copy-start | bytes 772
  4.6 9.1 %copy-start.7 = (s32[1,64]{1,0:T(1,128)S(1)}, s32[1,64]{1,0:T(1,128)}, u32[]{:S(2)}) copy-start(s32[1,64]{1,0:T(1,128)} %param.18) | copy-start | bytes 772
  4.6 9.1 %copy-start.8 = (s32[1,64]{1,0:T(1,128)S(1)}, s32[1,64]{1,0:T(1,128)}, u32[]{:S(2)}) copy-start(s32[1,64]{1,0:T(1,128)} %param.20) | copy-start | bytes 772
  4.6 45.9 %all-to-all-start = ((bf16[32,24,1792]{2,1,0:T(8,128)(2,1)}), bf16[32,24,1792]{2,1,0:T(8,128)(2,1)S(1)}, u32[]{:S(2)}, u32[]{:S(2)}) async-start(bf16[32,24,1792]{2,1,0:T(8,128)(2,1)} %bitcast.144), calls=%async_computation | async-start | bytes 5505024 | tf_op jit(solution)/shard_map/all_to_all | solution.py:402
  18.5 4.9 %copy-start.1 = (bf16[128,1792]{1,0:T(8,128)(2,1)S(1)}, bf16[128,1792]{1,0:T(8,128)(2,1)}, u32[]{:S(2)}) copy-start(bf16[128,1792]{1,0:T(8,128)(2,1)} %param.11) | copy-start | bytes 1376260
  18.5 10.1 %copy-start.5 = (s32[128,8]{0,1:T(8,128)S(1)}, s32[128,8]{0,1:T(8,128)}, u32[]{:S(2)}) copy-start(s32[128,8]{0,1:T(8,128)} %param.12) | copy-start | bytes 12292
  18.5 10.1 %copy-start.6 = (f32[128,8]{0,1:T(8,128)S(1)}, f32[128,8]{0,1:T(8,128)}, u32[]{:S(2)}) copy-start(f32[128,8]{0,1:T(8,128)} %param.13) | copy-start | bytes 12292
  23.4 50.9 %collective-permute-start = (bf16[128,1792]{1,0:T(8,128)(2,1)S(1)}, bf16[128,1792]{1,0:T(8,128)(2,1)}, u32[]{:S(2)}, u32[]{:S(2)}) collective-permute-start(bf16[128,1792]{1,0:T(8,128)(2,1)S(1)} %copy-done.1), channel_id=1, source_target_pairs={{0,1},{1,2},{2,3},{3,0},{4,5},{5,6},{6,7},{7,4},{8,9},{9,10},{10,1... | collective-permute-start | bytes 1376264 | tf_op jit(solution)/shard_map/ppermute | solution.py:399
  25.0 49.3 %collective-permute-start.1 = (bf16[128,1792]{1,0:T(8,128)(2,1)S(1)}, bf16[128,1792]{1,0:T(8,128)(2,1)}, u32[]{:S(2)}, u32[]{:S(2)}) collective-permute-start(bf16[128,1792]{1,0:T(8,128)(2,1)S(1)} %copy-done.1), channel_id=1, source_target_pairs={{0,3},{1,0},{2,1},{3,2},{4,7},{5,4},{6,5},{7,6},{8,11},{9,8},{10,9... | collective-permute-start | bytes 1376264 | tf_op jit(solution)/shard_map/ppermute | solution.py:399
  26.6 47.6 %collective-permute-start.2 = (bf16[128,1792]{1,0:T(8,128)(2,1)S(1)}, bf16[128,1792]{1,0:T(8,128)(2,1)}, u32[]{:S(2)}, u32[]{:S(2)}) collective-permute-start(bf16[128,1792]{1,0:T(8,128)(2,1)S(1)} %copy-done.1), channel_id=1, source_target_pairs={{0,2},{1,3},{2,0},{3,1},{4,6},{5,7},{6,4},{7,5},{8,10},{9,11},{10,... | collective-permute-start | bytes 1376264 | tf_op jit(solution)/shard_map/ppermute | solution.py:399
  50.5 60.4 %all-to-all-start.1 = ((bf16[128,136,128]{2,1,0:T(8,128)(2,1)}), bf16[128,136,128]{2,1,0:T(8,128)(2,1)}, u32[]{:S(2)}, u32[]{:S(2)}) async-start(bf16[128,136,128]{2,1,0:T(8,128)(2,1)} %shard_map.109), calls=%async_computation.1 | async-start | bytes 8912896 | tf_op jit(solution)/shard_map/all_to_all | solution.py:402
  79.4 57.0 %collective-permute-start.3 = (bf16[384,1792]{1,0:T(8,128)(2,1)}, bf16[384,1792]{1,0:T(8,128)(2,1)}, u32[]{:S(2)}, u32[]{:S(2)}) collective-permute-start(bf16[384,1792]{1,0:T(8,128)(2,1)} %bitcast.30), channel_id=1, source_target_pairs={{0,1},{1,2},{2,3},{3,0},{4,5},{5,6},{6,7},{7,4},{8,9},{9,10},{10,1... | collective-permute-start | bytes 4128776 | tf_op jit(solution)/shard_map/ppermute | solution.py:399
  80.3 56.1 %collective-permute-start.4 = (bf16[384,1792]{1,0:T(8,128)(2,1)}, bf16[384,1792]{1,0:T(8,128)(2,1)}, u32[]{:S(2)}, u32[]{:S(2)}) collective-permute-start(bf16[384,1792]{1,0:T(8,128)(2,1)} %bitcast.31), channel_id=1, source_target_pairs={{0,3},{1,0},{2,1},{3,2},{4,7},{5,4},{6,5},{7,6},{8,11},{9,8},{10,9... | collective-permute-start | bytes 4128776 | tf_op jit(solution)/shard_map/ppermute | solution.py:399
  85.3 79.3 %collective-permute-start.5 = (bf16[384,1792]{1,0:T(8,128)(2,1)}, bf16[384,1792]{1,0:T(8,128)(2,1)}, u32[]{:S(2)}, u32[]{:S(2)}) collective-permute-start(bf16[384,1792]{1,0:T(8,128)(2,1)} %bitcast.30), channel_id=1, source_target_pairs={{0,3},{1,0},{2,1},{3,2},{4,7},{5,4},{6,5},{7,6},{8,11},{9,8},{10,9... | collective-permute-start | bytes 4128776 | tf_op jit(solution)/shard_map/ppermute | solution.py:399
  86.3 82.4 %collective-permute-start.6 = (bf16[384,1792]{1,0:T(8,128)(2,1)}, bf16[384,1792]{1,0:T(8,128)(2,1)}, u32[]{:S(2)}, u32[]{:S(2)}) collective-permute-start(bf16[384,1792]{1,0:T(8,128)(2,1)} %bitcast.31), channel_id=1, source_target_pairs={{0,1},{1,2},{2,3},{3,0},{4,5},{5,6},{6,7},{7,4},{8,9},{9,10},{10,1... | collective-permute-start | bytes 4128776 | tf_op jit(solution)/shard_map/ppermute | solution.py:399
  112.1 91.5 %all-to-all-start.2 = ((bf16[32,8,10752]{2,1,0:T(8,128)(2,1)}), bf16[32,8,10752]{2,1,0:T(8,128)(2,1)}, u32[]{:S(2)}, u32[]{:S(2)}) async-start(bf16[32,8,10752]{2,1,0:T(8,128)(2,1)} %bitcast.142), calls=%async_computation.2 | async-start | bytes 11010048 | tf_op jit(solution)/shard_map/all_to_all | solution.py:402
  136.4 58.4 %collective-permute-start.7 = (bf16[384,1792]{1,0:T(8,128)(2,1)}, bf16[384,1792]{1,0:T(8,128)(2,1)S(1)}, u32[]{:S(2)}, u32[]{:S(2)}) collective-permute-start(bf16[384,1792]{1,0:T(8,128)(2,1)} %collective-permute-done.3), channel_id=1, source_target_pairs={{0,1},{1,2},{2,3},{3,0},{4,5},{5,6},{6,7},{7,4},{8,9},{9,10},{10,1... | collective-permute-start | bytes 4128776 | tf_op jit(solution)/shard_map/ppermute | solution.py:399
  136.6 58.2 %collective-permute-start.8 = (bf16[384,1792]{1,0:T(8,128)(2,1)}, bf16[384,1792]{1,0:T(8,128)(2,1)S(1)}, u32[]{:S(2)}, u32[]{:S(2)}) collective-permute-start(bf16[384,1792]{1,0:T(8,128)(2,1)} %collective-permute-done.4), channel_id=1, source_target_pairs={{0,3},{1,0},{2,1},{3,2},{4,7},{5,4},{6,5},{7,6},{8,11},{9,8},{10,9... | collective-permute-start | bytes 4128776 | tf_op jit(solution)/shard_map/ppermute | solution.py:399
  139.6 29.1 %copy-start = (bf16[7168,1024]{1,0:T(8,128)(2,1)S(1)}, bf16[7168,1024]{1,0:T(8,128)(2,1)}, u32[]{:S(2)}) copy-start(bf16[7168,1024]{1,0:T(8,128)(2,1)} %get-tuple-element.56.gu_ref) | copy-start | bytes 44040196
  203.5 33.3 %collective-permute-start.10 = (bf16[384,1792]{1,0:T(8,128)(2,1)}, bf16[384,1792]{1,0:T(8,128)(2,1)}, u32[]{:S(2)}, u32[]{:S(2)}) collective-permute-start(bf16[384,1792]{1,0:T(8,128)(2,1)} %convolution_convert_fusion.3), channel_id=1, source_target_pairs={{0,1},{1,2},{2,3},{3,0},{4,5},{5,6},{6,7},{7,4},{8,9},{9,10},{10,1... | collective-permute-start | bytes 4128776 | tf_op jit(solution)/shard_map/ppermute | solution.py:399
  203.7 36.9 %collective-permute-start.9 = (bf16[384,1792]{1,0:T(8,128)(2,1)}, bf16[384,1792]{1,0:T(8,128)(2,1)}, u32[]{:S(2)}, u32[]{:S(2)}) collective-permute-start(bf16[384,1792]{1,0:T(8,128)(2,1)} %convolution_convert_fusion.4), channel_id=1, source_target_pairs={{0,3},{1,0},{2,1},{3,2},{4,7},{5,4},{6,5},{7,6},{8,11},{9,8},{10,9... | collective-permute-start | bytes 4128776 | tf_op jit(solution)/shard_map/ppermute | solution.py:399
  228.8 11.8 %slice-start.2 = ((s8[7340032]{0:T(1024)(128)(4,1)}), s8[3145728]{0:T(1024)(128)(4,1)S(1)}, s32[]{:S(2)}) async-start(s8[7340032]{0:T(1024)(128)(4,1)} %bitcast.133), calls=%async_computation.7 | async-start | bytes 6291456
  228.8 80.6 %all-to-all-start.3 = ((bf16[32,8,10752]{2,1,0:T(8,128)(2,1)}), bf16[32,8,10752]{2,1,0:T(8,128)(2,1)}, u32[]{:S(2)}, u32[]{:S(2)}) async-start(bf16[32,8,10752]{2,1,0:T(8,128)(2,1)} %bitcast.141), calls=%async_computation.3 | async-start | bytes 11010048 | tf_op jit(solution)/shard_map/all_to_all | solution.py:402
  236.8 3.8 %slice-start.3 = ((s8[7340032]{0:T(1024)(128)(4,1)}), s8[4194304]{0:T(1024)(128)(4,1)S(1)}, s32[]{:S(2)}) async-start(s8[7340032]{0:T(1024)(128)(4,1)} %bitcast.133), calls=%async_computation.8 | async-start | bytes 8388608
  236.8 3.8 %copy-start.4 = (bf16[384,512]{1,0:T(8,128)(2,1)S(1)}, bf16[384,512]{1,0:T(8,128)(2,1)}, u32[]{:S(2)}) copy-start(bf16[384,512]{1,0:T(8,128)(2,1)} %copy-done.3) | copy-start | bytes 1179652
  243.6 61.9 %collective-permute-start.11 = (bf16[768,1792]{1,0:T(8,128)(2,1)S(1)}, bf16[768,1792]{1,0:T(8,128)(2,1)S(1)}, u32[]{:S(2)}, u32[]{:S(2)}) collective-permute-start(bf16[768,1792]{1,0:T(8,128)(2,1)S(1)} %add_convert_fusion.2), channel_id=1, source_target_pairs={{0,3},{1,0},{2,1},{3,2},{4,7},{5,4},{6,5},{7,6},{8,11},{9,8},{10,9... | collective-permute-start | bytes 8257544 | tf_op jit(solution)/shard_map/ppermute | solution.py:399
  244.3 62.7 %collective-permute-start.12 = (bf16[768,1792]{1,0:T(8,128)(2,1)S(1)}, bf16[768,1792]{1,0:T(8,128)(2,1)S(1)}, u32[]{:S(2)}, u32[]{:S(2)}) collective-permute-start(bf16[768,1792]{1,0:T(8,128)(2,1)S(1)} %add_convert_fusion.1), channel_id=1, source_target_pairs={{0,1},{1,2},{2,3},{3,0},{4,5},{5,6},{6,7},{7,4},{8,9},{9,10},{10,1... | collective-permute-start | bytes 8257544 | tf_op jit(solution)/shard_map/ppermute | solution.py:399
  309.5 44.7 %all-to-all-start.4 = ((bf16[32,24,1792]{2,1,0:T(8,128)(2,1)}), bf16[32,24,1792]{2,1,0:T(8,128)(2,1)S(1)}, u32[]{:S(2)}, u32[]{:S(2)}) async-start(bf16[32,24,1792]{2,1,0:T(8,128)(2,1)} %bitcast.40), calls=%async_computation.4 | async-start | bytes 5505024 | tf_op jit(solution)/shard_map/all_to_all | solution.py:402
  325.3 29.0 %copy-start.2 = (bf16[256,768]{0,1:T(8,128)(2,1)S(1)}, bf16[256,768]{0,1:T(8,128)(2,1)}, u32[]{:S(2)}) copy-start(bf16[256,768]{0,1:T(8,128)(2,1)} %pad_maximum_fusion.3) | copy-start | bytes 1179652
  327.7 27.4 %collective-permute-start.13 = (bf16[128,1792]{1,0:T(8,128)(2,1)}, bf16[128,1792]{1,0:T(8,128)(2,1)}, u32[]{:S(2)}, u32[]{:S(2)}) collective-permute-start(bf16[128,1792]{1,0:T(8,128)(2,1)} %get-tuple-element.87), channel_id=1, source_target_pairs={{0,3},{1,0},{2,1},{3,2},{4,7},{5,4},{6,5},{7,6},{8,11},{9,8},{10,9... | collective-permute-start | bytes 1376264 | tf_op jit(solution)/shard_map/ppermute | solution.py:399
  328.0 27.1 %collective-permute-start.14 = (bf16[128,1792]{1,0:T(8,128)(2,1)}, bf16[128,1792]{1,0:T(8,128)(2,1)}, u32[]{:S(2)}, u32[]{:S(2)}) collective-permute-start(bf16[128,1792]{1,0:T(8,128)(2,1)} %get-tuple-element.89), channel_id=1, source_target_pairs={{0,1},{1,2},{2,3},{3,0},{4,5},{5,6},{6,7},{7,4},{8,9},{9,10},{10,1... | collective-permute-start | bytes 1376264 | tf_op jit(solution)/shard_map/ppermute | solution.py:399
  329.8 25.4 %collective-permute-start.15 = (bf16[128,1792]{1,0:T(8,128)(2,1)}, bf16[128,1792]{1,0:T(8,128)(2,1)}, u32[]{:S(2)}, u32[]{:S(2)}) collective-permute-start(bf16[128,1792]{1,0:T(8,128)(2,1)} %get-tuple-element.88), channel_id=1, source_target_pairs={{0,2},{1,3},{2,0},{3,1},{4,6},{5,7},{6,4},{7,5},{8,10},{9,11},{10,... | collective-permute-start | bytes 1376264 | tf_op jit(solution)/shard_map/ppermute | solution.py:399
  (3 other events, 8.2 us)
